TPU v7x, 128 devices: a whole 4x4x4 slice. The times are simulated.
128 devices in a mesh: seq: 32 (over z, x, core), head: 4 (over y).
Axes of the slice: x: 4, y: 4, z: 4, core: 2. Of those that a mesh axis runs over, the one named last changes fastest.
Arguments:
- keys_cache: bfloat16 [32, 16384, 1024], P(None, 'seq', 'head'), may hold values from -6 to 6
- values_cache: bfloat16 [32, 16384, 1024], P(None, 'seq', 'head'), may hold values from -6 to 6
- keep_blocks: int32 [32, 8, 128], P(None, 'head'), may hold values from 0 to 255, as said below
- keep_count: int32 [32, 8], P(None, 'head'), may hold values from 0 to 128, as said below
- queries: bfloat16 [3, 32, 8192], P(None, 'seq', 'head'), may hold values from -104 to 104
- new_keys: bfloat16 [3, 32, 1024], P(None, 'seq', 'head'), may hold values from -4.5 to 4.5
- new_values: bfloat16 [3, 32, 1024], P(None, 'seq', 'head'), may hold values from -6 to 6
- residual_in: bfloat16 [3, 32, 8192], P(None, None, 'seq'), may hold values from -40 to 40
- norm_gain: bfloat16 [8192], P('seq'), may hold values from 0.099609375 to 1.8984375
- w_out: bfloat16 [8192, 8192], P('head', 'seq'), may hold values from -0.375 to 0.375
- w_gate: bfloat16 [8192, 16384], P('seq', 'head'), may hold values from -0.0625 to 0.0625
- w_up: bfloat16 [8192, 16384], P('seq', 'head'), may hold values from -0.0625 to 0.0625
- w_down: bfloat16 [16384, 8192], P(('head', 'seq')), may hold values from -0.1875 to 0.1875
Outputs:
- attended: bfloat16 [3, 32, 8192], P(None, 'seq', 'head')
- layer_out: bfloat16 [3, 32, 8192], P(None, None, 'seq')
Inputs may be any that keep to these rules, and one draw needn't show every extreme that they name: `keep_blocks`: entries below keep_count are distinct block numbers in increasing order, the rest are 0. Of one prompt and key-value head, at most 4 kept blocks lie in each aligned run of 8 blocks, and some run holds exactly 4. `keep_count`: some prompt and head keep 128 blocks.
All inputs are finite; a program needn't handle non-finite values.
Results may differ from a plain program's by a relative error of at most 0.009.
Values may be sent and summed in bfloat16 or wider, within the bound.
No kernel may reach another device: no remote copies, remote signals or barrier semaphores. Data moves between devices by JAX's collectives and lax.ppermute only.
A program may use at most 128 MiB of HBM per device.

v0:
```python
import jax
import jax.numpy as jnp
from jax import lax
from jax.sharding import PartitionSpec as P

D = 8192
H = 64
KVH = 8
HD = 128
BLK = 64
CAP = 4


masked_score = -1e30
norm_eps = 1e-06


def on_device(
    keys_cache,
    values_cache,
    keep_blocks,
    keep_count,
    queries,
    new_keys,
    new_values,
    residual_in,
    norm_gain,
    w_out,
    w_gate,
    w_up,
    w_down,
):
    holders = lax.axis_size("seq")
    holder = lax.axis_index("seq")
    prompts = keys_cache.shape[0]
    per_dev = keys_cache.shape[1] // BLK
    kv_local = keep_blocks.shape[1]
    list_length = keep_blocks.shape[2]
    groups = H // KVH
    step_count = queries.shape[0]
    owned = queries.shape[1]
    score_scale = HD ** (-0.5)
    key_blocks = keys_cache.reshape(prompts, per_dev, BLK, kv_local, HD)
    value_blocks = values_cache.reshape(prompts, per_dev, BLK, kv_local, HD)
    local_ids = holder * per_dev + jnp.arange(per_dev)
    is_valid = jnp.arange(list_length)[None, None, :] < keep_count[:, :, None]
    matched = (keep_blocks[..., None] == local_ids) & is_valid[..., None]
    kept_flags = jnp.any(matched, axis=2)
    query_heads = queries.reshape(step_count, owned, kv_local, groups, HD)
    new_heads = new_keys.reshape(step_count, owned, kv_local, HD)
    new_vals = new_values.reshape(step_count, owned, kv_local, HD)
    new_scores = (
        jnp.einsum("tjhgd,ujhd->tjhgu", query_heads, new_heads, preferred_element_type=jnp.float32)
        * score_scale
    )
    causal = jnp.arange(step_count)[:, None] >= jnp.arange(step_count)[None, :]
    new_scores = jnp.where(causal[:, None, None, None, :], new_scores, masked_score)
    new_max = jnp.max(new_scores, axis=4)
    slot_rank = jnp.cumsum(kept_flags.astype(jnp.int32), axis=2) - 1
    select = (
        kept_flags[:, :, None, :]
        & (slot_rank[:, :, None, :] == jnp.arange(CAP)[None, None, :, None])
    ).astype(jnp.bfloat16)
    key_tiles = jnp.einsum(
        "bhkj,bjshd->bhksd", select, key_blocks, preferred_element_type=jnp.float32
    ).astype(jnp.bfloat16)
    value_tiles = jnp.einsum(
        "bhkj,bjshd->bhksd", select, value_blocks, preferred_element_type=jnp.float32
    ).astype(jnp.bfloat16)
    got_keys, got_values = (
        lax.all_to_all(key_tiles, "seq", split_axis=0, concat_axis=0, tiled=True),
        lax.all_to_all(value_tiles, "seq", split_axis=0, concat_axis=0, tiled=True),
    )
    got_keys = got_keys.reshape(holders, owned, kv_local, CAP, BLK, HD)
    got_values = got_values.reshape(holders, owned, kv_local, CAP, BLK, HD)
    own_lists = lax.dynamic_slice_in_dim(keep_blocks, holder * owned, owned, 0)
    own_counts = lax.dynamic_slice_in_dim(keep_count, holder * owned, owned, 0)
    own_valid = jnp.arange(list_length)[None, None, :] < own_counts[:, :, None]
    holder_of = own_lists // per_dev
    per_holder = jnp.sum(
        (own_valid[..., None] & (holder_of[..., None] == jnp.arange(holders))).astype(jnp.int32),
        axis=2,
    )
    slot_ok = jnp.arange(CAP)[None, None, None, :] < per_holder[..., None]
    scores = (
        jnp.einsum(
            "tjhgd,ijhksd->tjhgiks", query_heads, got_keys, preferred_element_type=jnp.float32
        )
        * score_scale
    )
    scores = jnp.where(slot_ok[None, :, :, None, :, :, None], scores, masked_score)
    row_max = jnp.maximum(jnp.max(scores, axis=(4, 5, 6)), new_max)
    weight = jnp.exp(scores - row_max[..., None, None, None]).astype(jnp.bfloat16)
    new_weight = jnp.exp(new_scores - row_max[..., None]).astype(jnp.bfloat16)
    weight_sum = jnp.sum(weight, axis=(4, 5, 6), dtype=jnp.float32) + jnp.sum(
        new_weight, axis=4, dtype=jnp.float32
    )
    summed = jnp.einsum(
        "tjhgiks,ijhksd->tjhgd", weight, got_values, preferred_element_type=jnp.float32
    )
    summed = summed + jnp.einsum(
        "tjhgu,ujhd->tjhgd", new_weight, new_vals, preferred_element_type=jnp.float32
    )
    attended = (
        (summed / weight_sum[..., None])
        .astype(jnp.bfloat16)
        .reshape(step_count, owned, kv_local * groups * HD)
    )
    partial_out = jnp.einsum(
        "tri,io->tro",
        lax.all_gather(attended, "seq", axis=1, tiled=True),
        w_out,
        preferred_element_type=jnp.float32,
    )
    projected = lax.psum(partial_out, "head")
    stream = residual_in.astype(jnp.float32) + projected
    square_sum = lax.psum(jnp.sum(stream * stream, axis=2), "seq")
    normed = (
        stream * lax.rsqrt(square_sum / D + norm_eps)[..., None] * norm_gain.astype(jnp.float32)
    ).astype(jnp.bfloat16)
    all_prompts = stream.shape[1]
    width_local = stream.shape[2]
    token_count = step_count * all_prompts
    flat_rows = normed.reshape(token_count, width_local)
    gate_part = lax.dot_general(
        w_gate, flat_rows, (((0,), (1,)), ((), ())), preferred_element_type=jnp.float32
    )
    up_part = lax.dot_general(
        w_up, flat_rows, (((0,), (1,)), ((), ())), preferred_element_type=jnp.float32
    )
    both_sums = lax.psum_scatter(
        jnp.concatenate([gate_part, up_part], axis=1), "seq", scatter_dimension=0, tiled=True
    )
    activated = (jax.nn.silu(both_sums[:, :token_count]) * both_sums[:, token_count:]).astype(
        jnp.bfloat16
    )
    down_part = lax.psum_scatter(
        lax.dot_general(
            w_down, activated, (((0,), (0,)), ((), ())), preferred_element_type=jnp.float32
        ),
        "seq",
        scatter_dimension=0,
        tiled=True,
    )
    lowered = lax.psum(down_part, "head")
    layer_out = (stream + lowered.T.reshape(step_count, all_prompts, width_local)).astype(
        jnp.bfloat16
    )
    return (attended, layer_out)


def solution(mesh):
    placed = (
        P(None, "seq", "head"),
        P(None, "seq", "head"),
        P(None, "head", None),
        P(None, "head"),
        P(None, "seq", "head"),
        P(None, "seq", "head"),
        P(None, "seq", "head"),
        P(None, None, "seq"),
        P("seq"),
        P("head", "seq"),
        P("seq", "head"),
        P("seq", "head"),
        P(("head", "seq"), None),
    )
    return jax.shard_map(
        on_device,
        mesh=mesh,
        in_specs=placed,
        out_specs=(P(None, "seq", "head"), P(None, None, "seq")),
        check_vma=False,
    )
```

profile of v0, /device:TPU:1, one launch (start us, length us, event | category | flops | bytes accessed | tf_op | source)
XLA Modules:
  0.0 514.1 jit_solution(9893526613668339064)
XLA Ops:
  7.2 0.9 copy.57
  8.2 2.0 and_reduce_fusion
  10.2 5.7 %reduce_window_sum.11 = s32[32,2,8]{2,1,0:T(2,128)S(1)} reduce-window(s32[32,2,8]{2,1,0:T(2,128)S(1)} %convert_element_type.55, s32[]{:T(128)} %constant.37.clone.1), window={size=1x1x8 pad=0_0x0_0x7_0}, to_apply=%region_1.2 | reduce-window | flops 3584 | bytes 4100 | tf_op jit(solution)/shard_map/jit(cumsum)/reduce_window_sum | solution.py:59
  15.9 12.5 %reshape.188 = bf16[32,8,64,2,128]{4,3,2,1,0:T(2,128)(2,1)} reshape(bf16[32,512,256]{2,1,0:T(8,128)(2,1)} %param.13) | data formatting | bytes 16777216 | tf_op jit(solution)/shard_map/reshape | solution.py:43
  28.5 13.4 %fusion.7 = bf16[32,2,4,64,128]{4,2,3,1,0:T(4,128)(2,1)S(1)} fusion(bf16[32,8,64,2,128]{4,3,2,1,0:T(2,128)(2,1)} %reshape.188, s32[32,2,8]{2,1,0:T(2,128)S(1)} %broadcast_add_fusion, pred[32,2,8]{2,1,0:T(4,128)(4,1)S(1)} %and_reduce_fusion), kind=kOutput, calls=%fused_computation.8 | convolution fusion | flops 35655680 | bytes 12585472 | tf_op jit(solution)/shard_map/bhkj,bjshd->bhksd/dot_general | solution.py:64
  41.8 3.2 copy.61
  45.0 9.5 %all-to-all-start.1 = ((bf16[32,2,4,64,128]{4,3,2,1,0:T(8,128)(2,1)}), bf16[32,2,4,64,128]{4,3,2,1,0:T(8,128)(2,1)}, u32[]{:S(2)}, u32[]{:S(2)}) async-start(bf16[32,2,4,64,128]{4,3,2,1,0:T(8,128)(2,1)} %copy.61), calls=%async_computation.1 | async-start | bytes 8388608 | tf_op jit(solution)/shard_map/all_to_all | solution.py:71
  54.5 12.5 %reshape.187 = bf16[32,8,64,2,128]{4,3,2,1,0:T(2,128)(2,1)} reshape(bf16[32,512,256]{2,1,0:T(8,128)(2,1)} %param.14) | data formatting | bytes 16777216 | tf_op jit(solution)/shard_map/reshape | solution.py:44
  67.1 13.4 %fusion.4 = bf16[32,2,4,64,128]{4,2,3,1,0:T(4,128)(2,1)S(1)} fusion(bf16[32,8,64,2,128]{4,3,2,1,0:T(2,128)(2,1)} %reshape.187, s32[32,2,8]{2,1,0:T(2,128)S(1)} %broadcast_add_fusion, pred[32,2,8]{2,1,0:T(4,128)(4,1)S(1)} %and_reduce_fusion), kind=kOutput, calls=%fused_computation.7 | convolution fusion | flops 35655680 | bytes 12585472 | tf_op jit(solution)/shard_map/bhkj,bjshd->bhksd/dot_general | solution.py:67
  80.4 3.2 copy.59
  83.6 21.1 %all-to-all-done.1 = bf16[32,2,4,64,128]{4,3,2,1,0:T(8,128)(2,1)} async-done(((bf16[32,2,4,64,128]{4,3,2,1,0:T(8,128)(2,1)}), bf16[32,2,4,64,128]{4,3,2,1,0:T(8,128)(2,1)}, u32[]{:S(2)}, u32[]{:S(2)}) %all-to-all-start.1) | async-done | bytes 4194336 | tf_op jit(solution)/shard_map/all_to_all | solution.py:71
  104.7 8.1 %all-to-all-start = ((bf16[32,2,4,64,128]{4,3,2,1,0:T(8,128)(2,1)}), bf16[32,2,4,64,128]{4,3,2,1,0:T(8,128)(2,1)}, u32[]{:S(2)}, u32[]{:S(2)}) async-start(bf16[32,2,4,64,128]{4,3,2,1,0:T(8,128)(2,1)} %copy.59), calls=%async_computation | async-start | bytes 8388608 | tf_op jit(solution)/shard_map/all_to_all | solution.py:72
  112.8 0.3 all-reduce.3.cloned.1.call-start
  113.2 0.7 fusion.38
  114.4 5.3 %bitcast_reduce_fusion = (f32[3,2,8]{2,0,1:T(4,128)S(1)}, f32[2,32,4,64,3,8]{3,5,4,2,1,0:T(8,128)S(1)}) fusion(pred[2,32,4]{2,1,0:T(8,128)(4,1)S(1)} %iota_compare_fusion.2, bf16[32,2,4,64,128]{4,3,2,1,0:T(8,128)(2,1)} %all-to-all-done.1, bf16[1,3,16,128]{3,1,2,0:T(4,128)(2,1)S(1)} %bitcast.127), kind=kOutput, calls=%fused_computation.15 | convolution fusion | flops 101842896 | bytes 5779904 | tf_op jit(solution)/shard_map/tjhgd,ijhksd->tjhgiks/dot_general | solution.py:86
  119.7 2.0 convert_reduce_fusion
  121.7 41.4 %all-to-all-done = bf16[32,2,4,64,128]{4,3,2,1,0:T(8,128)(2,1)} async-done(((bf16[32,2,4,64,128]{4,3,2,1,0:T(8,128)(2,1)}), bf16[32,2,4,64,128]{4,3,2,1,0:T(8,128)(2,1)}, u32[]{:S(2)}, u32[]{:S(2)}) %all-to-all-start) | async-done | bytes 4194336 | tf_op jit(solution)/shard_map/all_to_all | solution.py:72
  163.1 3.5 fusion.10
  166.9 25.1 %all_gather.3 = bf16[3,32,2048]{2,0,1:T(4,128)(2,1)S(1)} all-gather(bf16[3,1,2048]{2,0,1:T(4,128)(2,1)S(1)} %reshape.194), channel_id=1, replica_groups=mesh['seq'=32,'head'=4] {'seq'}, dimensions={1}, use_global_device_ids=true | all-gather | bytes 405504 | tf_op jit(solution)/shard_map/all_gather | solution.py:111
  192.0 1.1 fusion.23
  193.2 38.6 %all-reduce.3.cloned.1.call-done = f32[3,32,256]{2,1,0:T(8,128)} async-done(((f32[3,32,256]{2,1,0:T(8,128)}), f32[3,32,256]{2,1,0:T(8,128)}) %all-reduce.3.cloned.1.call-update) | async-done | bytes 98320 | tf_op jit(solution)/shard_map/psum | solution.py:115
  231.8 1.0 multiply_reduce_fusion
  232.8 64.9 %psum.22 = f32[3,32]{1,0:T(4,128)S(1)} all-reduce(f32[3,32]{1,0:T(4,128)S(1)} %multiply_reduce_fusion), channel_id=1, replica_groups=mesh['seq'=32,'head'=4] {'seq'}, use_global_device_ids=true, to_apply=%region_9.10 | all-reduce | flops 96 | bytes 768 | tf_op jit(solution)/shard_map/psum | solution.py:117
  297.7 1.1 multiply_convert_fusion
  298.8 2.1 convolution_bitcast_fusion.1
  300.9 0.5 convolution_bitcast_fusion.2
  301.3 2.0 pad_maximum_fusion
  303.4 77.0 %reduce-scatter.3.cloned.1.call-done = f32[128,192]{0,1:T(8,128)} async-done(((f32[4096,192]{0,1:T(8,128)}), f32[128,192]{0,1:T(8,128)}) %reduce-scatter.3.cloned.1.call-update) | async-done | bytes 98320 | tf_op jit(solution)/shard_map/reduce_scatter | solution.py:131
  380.4 3.1 convolution_bitcast_fusion
  383.6 80.3 %reduce-scatter.5.cloned.1.call-done = f32[256,96]{0,1:T(8,128)} async-done(((f32[8192,96]{0,1:T(8,128)}), f32[256,96]{0,1:T(8,128)}) %reduce-scatter.5.cloned.1.call-update) | async-done | bytes 98320 | tf_op jit(solution)/shard_map/reduce_scatter | solution.py:137
  463.9 42.1 %all-reduce.5.cloned.1.call-done = f32[3,32,256]{2,1,0:T(8,128)} async-done(((f32[3,32,256]{2,1,0:T(8,128)}), f32[3,32,256]{2,1,0:T(8,128)}) %all-reduce.5.cloned.1.call-update) | async-done | bytes 98320 | tf_op jit(solution)/shard_map/psum | solution.py:145
  506.0 1.5 add_convert_fusion
  (47 shorter events, 1.3 us)
Async XLA Ops:
  7.2 373.2 %copy-start = (bf16[128,8192]{1,0:T(8,128)(2,1)S(1)}, bf16[128,8192]{1,0:T(8,128)(2,1)}, u32[]{:S(2)}) copy-start(bf16[128,8192]{1,0:T(8,128)(2,1)} %param.25) | copy-start | bytes 6291460
  45.0 59.7 %all-to-all-start.1 = ((bf16[32,2,4,64,128]{4,3,2,1,0:T(8,128)(2,1)}), bf16[32,2,4,64,128]{4,3,2,1,0:T(8,128)(2,1)}, u32[]{:S(2)}, u32[]{:S(2)}) async-start(bf16[32,2,4,64,128]{4,3,2,1,0:T(8,128)(2,1)} %copy.61), calls=%async_computation.1 | async-start | bytes 8388608 | tf_op jit(solution)/shard_map/all_to_all | solution.py:71
  83.6 29.4 %copy-start.6 = (s32[32,2]{0,1:T(2,128)S(1)}, s32[32,2]{0,1:T(2,128)}, u32[]{:S(2)}) copy-start(s32[32,2]{0,1:T(2,128)} %param.16) | copy-start | bytes 772
  83.6 30.6 %copy-start.7 = (bf16[3,1,2048]{2,0,1:T(4,128)(2,1)S(1)}, bf16[3,1,2048]{2,0,1:T(4,128)(2,1)}, u32[]{:S(2)}) copy-start(bf16[3,1,2048]{2,0,1:T(4,128)(2,1)} %param.17) | copy-start | bytes 36868
  83.6 30.6 %copy-start.8 = (bf16[3,1,256]{2,0,1:T(4,128)(2,1)S(1)}, bf16[3,1,256]{2,0,1:T(4,128)(2,1)}, u32[]{:S(2)}) copy-start(bf16[3,1,256]{2,0,1:T(4,128)(2,1)} %param.18) | copy-start | bytes 4612
  104.7 58.5 %all-to-all-start = ((bf16[32,2,4,64,128]{4,3,2,1,0:T(8,128)(2,1)}), bf16[32,2,4,64,128]{4,3,2,1,0:T(8,128)(2,1)}, u32[]{:S(2)}, u32[]{:S(2)}) async-start(bf16[32,2,4,64,128]{4,3,2,1,0:T(8,128)(2,1)} %copy.59), calls=%async_computation | async-start | bytes 8388608 | tf_op jit(solution)/shard_map/all_to_all | solution.py:72
  112.8 119.0 %all-reduce.3.cloned.1.call-start = ((), (), s32[]{:S(2)}) async-start(), calls=%async_computation.4 | async-start | bytes 196608 | tf_op jit(solution)/shard_map/psum | solution.py:115
  121.7 44.9 %copy-start.9 = (bf16[3,1,256]{2,0,1:T(4,128)(2,1)S(1)}, bf16[3,1,256]{2,0,1:T(4,128)(2,1)}, u32[]{:S(2)}) copy-start(bf16[3,1,256]{2,0,1:T(4,128)(2,1)} %param.19) | copy-start | bytes 4612
  163.1 28.9 %copy-start.2 = (bf16[2048,256]{1,0:T(8,128)(2,1)S(1)}, bf16[2048,256]{1,0:T(8,128)(2,1)}, u32[]{:S(2)}) copy-start(bf16[2048,256]{1,0:T(8,128)(2,1)} %param.22) | copy-start | bytes 3145732
  163.1 30.1 %copy-start.10 = (bf16[256]{0:T(256)(128)(2,1)S(1)}, bf16[256]{0:T(256)(128)(2,1)}, u32[]{:S(2)}) copy-start(bf16[256]{0:T(256)(128)(2,1)} %param.21) | copy-start | bytes 1540
  163.1 68.7 %copy-start.4 = (bf16[3,32,256]{2,1,0:T(8,128)(2,1)S(1)}, bf16[3,32,256]{2,1,0:T(8,128)(2,1)}, u32[]{:S(2)}) copy-start(bf16[3,32,256]{2,1,0:T(8,128)(2,1)} %param.20) | copy-start | bytes 147460
  166.9 134.5 %copy-start.5 = (bf16[3,1,2048]{2,0,1:T(4,128)(2,1)}, bf16[3,1,2048]{2,0,1:T(4,128)(2,1)S(1)}, u32[]{:S(2)}) copy-start(bf16[3,1,2048]{2,0,1:T(4,128)(2,1)S(1)} %reshape.194) | copy-start | bytes 36868
  193.1 187.3 %reduce-scatter.3.cloned.1.call-start = ((), (), s32[]{:S(2)}) async-start(), calls=%async_computation.5 | async-start | bytes 3244032 | tf_op jit(solution)/shard_map/reduce_scatter | solution.py:131
  297.7 3.2 copy-start.1
  303.4 202.6 %copy-start.3 = (f32[3,32,256]{2,1,0:T(8,128)S(1)}, f32[3,32,256]{2,1,0:T(8,128)}, u32[]{:S(2)}) copy-start(f32[3,32,256]{2,1,0:T(8,128)} %all-reduce.3.cloned.1.call-done) | copy-start | bytes 294916
  303.4 160.5 %reduce-scatter.5.cloned.1.call-start = ((), (), s32[]{:S(2)}) async-start(), calls=%async_computation.6 | async-start | bytes 3244032 | tf_op jit(solution)/shard_map/reduce_scatter | solution.py:137
  383.5 122.5 %all-reduce.5.cloned.1.call-start = ((), (), s32[]{:S(2)}) async-start(), calls=%async_computation.7 | async-start | bytes 196608 | tf_op jit(solution)/shard_map/psum | solution.py:145
Sparse Core Ops, SparseCore 0:
  193.3 38.4 all-reduce.2
  303.5 76.8 reduce-scatter.2
  384.0 79.7 reduce-scatter.4
  466.1 39.8 all-reduce.4
where the time goes:
time: 516 us; the launch traced here: 514 us
  waiting for transfers between devices  301 us (58%)
  blocking collectives  90 us (17%)
  matrix products  42.5 us (8%)
  local copies, waits for them, and re-layouts  32.6 us (6%)
  starting transfers between devices  17.9 us (3%)
  other arithmetic  16.5 us (3%)
  between operations  14 us (3%)
    reduce_scatter x1, waiting for transfers between devices, on_device(): lax.psum_scatter(lax.dot_general(w_down, activated, (((0,), (0,)), ((), (...  80.3 us
    reduce_scatter x1, waiting for transfers between devices, on_device(): lax.psum_scatter(jnp.concatenate([gate_part, up_part], axis=1), 'seq', sc...  77 us
    psum x1, blocking collectives, on_device(): square_sum = lax.psum(jnp.sum(stream * stream, axis=2), 'seq')  64.9 us
    psum x1, waiting for transfers between devices, on_device(): lowered = lax.psum(down_part, 'head')  42.1 us
    all_to_all x1, waiting for transfers between devices, on_device(): lax.all_to_all(value_tiles, 'seq', split_axis=0, concat_axis=0, tiled=True)  41.4 us
    psum x1, waiting for transfers between devices, on_device(): projected = lax.psum(partial_out, 'head')  38.6 us
    all_gather x1, blocking collectives, on_device(): lax.all_gather(attended, 'seq', axis=1, tiled=True)  25.1 us
    all_to_all x1, waiting for transfers between devices, on_device(): lax.all_to_all(key_tiles, 'seq', split_axis=0, concat_axis=0, tiled=True)  21.1 us
  transfers between devices with their start and end apart: 6, of which 6 were waited for; matrix products, arithmetic and copies ran while one was open for 7% of the time, Pallas kernels for 0%

commit v1 on v0

v1 whole, which is shorter than its diff:
```python
import functools

import jax
import jax.numpy as jnp
from jax import lax
from jax.experimental import pallas as pl
from jax.experimental.pallas import tpu as pltpu
from jax.sharding import PartitionSpec as P

D = 8192
H = 64
KVH = 8
HD = 128
BLK = 64
GROUPS = H // KVH

masked_score = -1e30
norm_eps = 1e-06
score_scale = HD ** (-0.5)

f32 = jnp.float32
bf16 = jnp.bfloat16

STEPS = 3
KV = 2
HQ = KV * GROUPS
ROWS = STEPS * HQ
PACK = ROWS + 16


def dot(a, b, ca=1, cb=0):
    return lax.dot_general(a, b, (((ca,), (cb,)), ((), ())), preferred_element_type=f32)


def first_head_rows():
    rows = lax.broadcasted_iota(jnp.int32, (ROWS, 1), 0)
    return (rows // GROUPS) % KV == 0


def two_head_queries(q, first):
    zero = jnp.zeros_like(q)
    return jnp.concatenate([jnp.where(first, q, zero), jnp.where(first, zero, q)], axis=1)


def per_head(values, first):
    return jnp.where(first, values[:, :HD], values[:, HD:])


def attend_kernel(per_dev, where_ref, lists_ref, q_own_ref, q_sib_ref, k_ref, v_ref, out_ref):
    base = where_ref[0] * per_dev
    core = where_ref[1]
    prompts = k_ref.shape[0]
    positions = k_ref.shape[1]
    relative = lists_ref[...] - base
    block_of = lax.broadcasted_iota(jnp.int32, (2 * prompts, positions), 1) // BLK
    kept = jnp.zeros((2 * prompts, positions), f32)
    for j in range(per_dev):
        flag = jnp.max(jnp.where(relative == j, 1.0, 0.0), axis=1, keepdims=True)
        kept = jnp.where(block_of == j, flag, kept)
    first = first_head_rows()
    lane = lax.broadcasted_iota(jnp.int32, (ROWS, HD), 1)
    unit = (
        lax.broadcasted_iota(jnp.int32, (16, HD), 0) == lax.broadcasted_iota(jnp.int32, (16, HD), 1)
    ).astype(bf16)
    for p in range(prompts):
        q = jnp.where(core == p % 2, q_own_ref[p // 2], q_sib_ref[p // 2])
        score = dot(two_head_queries(q, first), k_ref[p], 1, 1) * score_scale
        pair = [
            jnp.broadcast_to(kept[2 * p + h : 2 * p + h + 1], (GROUPS, positions)) for h in range(KV)
        ]
        keep = jnp.concatenate(pair * STEPS, axis=0) > 0.5
        score = jnp.where(keep, score, masked_score)
        top = jnp.max(score, axis=1, keepdims=True).astype(bf16).astype(f32)
        weight = jnp.where(keep, jnp.exp(score - top), 0.0).astype(bf16)
        total = jnp.sum(weight.astype(f32), axis=1, keepdims=True)
        summed = per_head(dot(weight, v_ref[p]), first)
        total_hi = total.astype(bf16).astype(f32)
        notes = jnp.where(
            lane == 0, top, jnp.where(lane == 1, total_hi, jnp.where(lane == 2, total - total_hi, 0.0))
        ).astype(bf16)
        notes = jnp.concatenate([notes, jnp.zeros((HD - ROWS, HD), bf16)], axis=0)
        out_ref[p, :ROWS, :] = summed.astype(bf16)
        out_ref[p, ROWS:, :] = dot(unit, notes, 1, 1).astype(bf16)


def combine_kernel(got_ref, q_ref, nk_ref, nv_ref, out_ref):
    holders = got_ref.shape[0]
    notes = got_ref[:, ROWS:, :].reshape(holders * 16, HD)
    row = lax.broadcasted_iota(jnp.int32, (holders * 16, HD), 0)
    col = lax.broadcasted_iota(jnp.int32, (holders * 16, HD), 1)
    pick = ((col == (row % 16) * holders + row // 16) & (row % 16 < 3)).astype(bf16)
    columns = dot(notes, pick, 0, 0)[:ROWS]
    tops = columns[:, :holders]
    totals = columns[:, holders : 2 * holders] + columns[:, 2 * holders : 3 * holders]
    first = first_head_rows()
    new_score = dot(two_head_queries(q_ref[...], first), nk_ref[...], 1, 1) * score_scale
    step = lax.broadcasted_iota(jnp.int32, new_score.shape, 0) // HQ
    token = lax.broadcasted_iota(jnp.int32, new_score.shape, 1)
    causal = token <= step
    new_score = jnp.where(causal, new_score, masked_score)
    top = jnp.maximum(
        jnp.max(tops, axis=1, keepdims=True), jnp.max(new_score, axis=1, keepdims=True)
    )
    share = jnp.exp(tops - top)
    new_weight = jnp.where(causal, jnp.exp(new_score - top), 0.0).astype(bf16)
    total = jnp.sum(share * totals, axis=1, keepdims=True) + jnp.sum(
        new_weight.astype(f32), axis=1, keepdims=True
    )
    summed = per_head(dot(new_weight, nv_ref[...]), first)
    for i in range(holders):
        summed = summed + share[:, i : i + 1] * got_ref[i, :ROWS, :].astype(f32)
    out_ref[...] = (summed / total).astype(bf16)


def project_kernel(where_ref, got_ref, own_ref, sib_ref, out_ref, wide_ref):
    core = where_ref[1]
    chips = got_ref.shape[0]
    wide_ref[...] = got_ref[...].reshape(chips * ROWS, HD).astype(f32)
    own = jnp.zeros((STEPS * chips, own_ref.shape[1]), f32)
    sib = jnp.zeros((STEPS * chips, own_ref.shape[1]), f32)
    for pair in range(HQ // 2):
        parts = []
        for h in (2 * pair, 2 * pair + 1):
            parts.append(
                jnp.concatenate(
                    [wide_ref[pl.ds(t * HQ + h, chips, stride=ROWS), :] for t in range(STEPS)], axis=0
                )
            )
        rows = jnp.concatenate(parts, axis=1).astype(bf16)
        at = slice(pair * 2 * HD, (pair + 1) * 2 * HD)
        own = own + dot(rows, own_ref[at, :])
        sib = sib + dot(rows, sib_ref[at, :])
    half = own_ref.shape[1]
    out_ref[:, :half] = jnp.where(core == 0, own, sib)
    out_ref[:, half:] = jnp.where(core == 0, sib, own)


def gate_up_kernel(
    where_ref, p0, p1, p2, p3, res_ref, gain_ref, g_own, g_sib, u_own, u_sib,
    out_ref, stream_ref, mine_ref, other_ref, square_ref,
):
    core = where_ref[1]
    half = g_own.shape[0]

    @pl.when(pl.program_id(0) == 0)
    def _():
        stream = res_ref[...].astype(f32) + ((p0[...] + p1[...]) + (p2[...] + p3[...]))
        stream_ref[...] = stream
        scaled = stream * gain_ref[0:1, :].astype(f32)
        mine_ref[...] = jnp.where(core == 0, scaled[:, :half], scaled[:, half:]).astype(bf16)
        other_ref[...] = jnp.where(core == 0, scaled[:, half:], scaled[:, :half]).astype(bf16)
        square = jnp.sum(stream * stream, axis=1, keepdims=True)
        square_hi = square.astype(bf16).astype(f32)
        tokens = square.shape[0]
        lane = lax.broadcasted_iota(jnp.int32, (tokens, HD), 1)
        notes = jnp.where(
            lane == 0, square_hi, jnp.where(lane == 1, square - square_hi, 0.0)
        ).astype(bf16)
        notes = jnp.concatenate([notes, jnp.zeros((HD - tokens, HD), bf16)], axis=0)
        unit = (
            lax.broadcasted_iota(jnp.int32, (16, HD), 0)
            == lax.broadcasted_iota(jnp.int32, (16, HD), 1)
        ).astype(bf16)
        square_ref[...] = dot(unit, notes, 1, 1).astype(bf16)

    mine = mine_ref[...]
    other = other_ref[...]
    tokens = mine.shape[0]
    gate = (dot(mine, g_own[...]) + dot(other, g_sib[...])).astype(bf16)
    up = (dot(mine, u_own[...]) + dot(other, u_sib[...])).astype(bf16)
    for k in range(out_ref.shape[0]):
        for part in range(2):
            at = slice((2 * k + part) * HD, (2 * k + part + 1) * HD)
            out_ref[k, part * tokens : (part + 1) * tokens, :] = gate[:, at]
            out_ref[k, (2 + part) * tokens : (3 + part) * tokens, :] = up[:, at]
        out_ref[k, 4 * tokens :, :] = square_ref[...]


def down_kernel(where_ref, got_ref, own_ref, sib_ref, out_ref, mine_ref, other_ref):
    core = where_ref[1]
    chips = got_ref.shape[0]
    tokens = mine_ref.shape[0]

    @pl.when(pl.program_id(0) == 0)
    def _():
        total = got_ref[0].astype(f32)
        for i in range(1, chips):
            total = total + got_ref[i].astype(f32)
        square = total[4 * tokens : 4 * tokens + 1, :] + total[4 * tokens + 1 : 4 * tokens + 2, :]
        scale_row = lax.rsqrt(square / D + norm_eps)
        row = lax.broadcasted_iota(jnp.int32, (tokens, HD), 0)
        col = lax.broadcasted_iota(jnp.int32, (tokens, HD), 1)
        scale = jnp.sum(jnp.where(row == col, scale_row, 0.0), axis=1, keepdims=True)
        halves = []
        for part in range(2):
            gate = total[part * tokens : (part + 1) * tokens] * scale
            up = total[(2 + part) * tokens : (3 + part) * tokens] * scale
            halves.append(gate / (1.0 + jnp.exp(-gate)) * up)
        mine_ref[...] = jnp.where(core == 0, halves[0], halves[1]).astype(bf16)
        other_ref[...] = jnp.where(core == 0, halves[1], halves[0]).astype(bf16)

    down = (dot(mine_ref[...], own_ref[...]) + dot(other_ref[...], sib_ref[...])).astype(bf16)
    width = out_ref.shape[2]
    for k in range(out_ref.shape[0]):
        out_ref[k] = down[:, k * width : (k + 1) * width]


def on_device(
    keys_cache,
    values_cache,
    keep_blocks,
    keep_count,
    queries,
    new_keys,
    new_values,
    residual_in,
    norm_gain,
    w_out,
    w_gate,
    w_up,
    w_down,
):
    holders = lax.axis_size("seq")
    chips = holders // 2
    holder = lax.axis_index("seq").astype(jnp.int32)
    core = holder % 2
    prompts, positions = keys_cache.shape[:2]
    per_dev = positions // BLK
    list_length = keep_blocks.shape[2]
    tokens = STEPS * chips
    width = residual_in.shape[2]
    where = jnp.stack([holder, core])
    smem = pl.BlockSpec(memory_space=pltpu.SMEM)
    vmem = pl.BlockSpec(memory_space=pltpu.VMEM)
    params = pltpu.CompilerParams(vmem_limit_bytes=40 * 1024 * 1024)

    same_core = [[2 * i + c for i in range(chips)] for c in range(2)]
    swap = [(i, i ^ 1) for i in range(holders)]

    def over_chips(x):
        return lax.all_to_all(
            x, "seq", split_axis=0, concat_axis=0, tiled=True, axis_index_groups=same_core
        )

    def to_all_chips(x):
        return over_chips(jnp.broadcast_to(x[None], (chips,) + x.shape))

    def sibling(x):
        return lax.ppermute(x, "seq", swap)

    def heads(x):
        return [x] + [lax.ppermute(x, "head", [(i, i ^ s) for i in range(4)]) for s in (1, 2, 3)]

    def parity(x, which):
        x = x.reshape(STEPS, chips, 2, width)
        return lax.dynamic_slice_in_dim(x, which, 1, 2).reshape(tokens, width)

    def in_order(own, sib):
        low = jnp.where(core == 0, own, sib)
        high = jnp.where(core == 0, sib, own)
        return jnp.concatenate([low, high], axis=1)

    q_rows = queries.reshape(ROWS, HD)
    q_own = to_all_chips(q_rows)
    q_sib = sibling(q_own)

    lists = jnp.where(
        jnp.arange(list_length)[None, None, :] < keep_count[:, :, None], keep_blocks, -1
    ).reshape(prompts * KV, list_length)

    batch = 4
    partial = pl.pallas_call(
        functools.partial(attend_kernel, per_dev),
        grid=(prompts // batch,),
        in_specs=[
            smem,
            pl.BlockSpec((batch * KV, list_length), lambda i: (i, 0)),
            pl.BlockSpec((batch // 2, ROWS, HD), lambda i: (i, 0, 0)),
            pl.BlockSpec((batch // 2, ROWS, HD), lambda i: (i, 0, 0)),
            pl.BlockSpec((batch, positions, KV * HD), lambda i: (i, 0, 0)),
            pl.BlockSpec((batch, positions, KV * HD), lambda i: (i, 0, 0)),
        ],
        out_specs=pl.BlockSpec((batch, PACK, HD), lambda i: (i, 0, 0)),
        out_shape=jax.ShapeDtypeStruct((prompts, PACK, HD), bf16),
        compiler_params=params,
        name="attend",
    )(where, lists, q_own, q_sib, keys_cache, values_cache)

    (w_out_s, w_gate_s, w_up_s, w_down_s, res_s, gain_s), _ = lax.optimization_barrier(
        ((w_out, w_gate, w_up, w_down, parity(residual_in, 1 - core), norm_gain), q_own)
    )
    w_out_sib = sibling(w_out_s)
    w_gate_sib = sibling(w_gate_s)
    w_up_sib = sibling(w_up_s)
    w_down_sib = sibling(w_down_s)
    extra = sibling(jnp.concatenate([res_s, jnp.broadcast_to(gain_s[None], (16, width))], axis=0))
    res = in_order(parity(residual_in, core), extra[:tokens])
    gain = in_order(jnp.broadcast_to(norm_gain[None], (16, width)), extra[tokens:])

    got = lax.all_to_all(partial, "seq", split_axis=0, concat_axis=0, tiled=True)
    pad = ((0, 16 - STEPS), (0, 0))
    attended = pl.pallas_call(
        combine_kernel,
        in_specs=[vmem] * 4,
        out_specs=vmem,
        out_shape=jax.ShapeDtypeStruct((ROWS, HD), bf16),
        compiler_params=params,
        name="combine",
    )(
        got,
        q_rows,
        jnp.pad(new_keys.reshape(STEPS, KV * HD), pad),
        jnp.pad(new_values.reshape(STEPS, KV * HD), pad),
    )

    all_attended = to_all_chips(attended)
    projected = pl.pallas_call(
        project_kernel,
        in_specs=[smem, vmem, vmem, vmem],
        out_specs=vmem,
        out_shape=jax.ShapeDtypeStruct((tokens, 2 * width), f32),
        scratch_shapes=[pltpu.VMEM((chips * ROWS, HD), f32)],
        compiler_params=params,
        name="project",
    )(where, all_attended, w_out, w_out_sib)
    parts = heads(projected)

    fixed = lambda *shape: pl.BlockSpec(shape, lambda i: (0,) * len(shape))
    hidden = w_gate.shape[1]
    per_step = 2
    gate_block = pl.BlockSpec((width, hidden // chips * per_step), lambda i: (0, i))
    shares, stream = pl.pallas_call(
        gate_up_kernel,
        grid=(chips // per_step,),
        in_specs=[smem]
        + [fixed(tokens, 2 * width)] * 5
        + [fixed(16, 2 * width)]
        + [gate_block] * 4,
        out_specs=[
            pl.BlockSpec((per_step, 4 * tokens + 16, HD), lambda i: (i, 0, 0)),
            fixed(tokens, 2 * width),
        ],
        out_shape=[
            jax.ShapeDtypeStruct((chips, 4 * tokens + 16, HD), bf16),
            jax.ShapeDtypeStruct((tokens, 2 * width), f32),
        ],
        scratch_shapes=[
            pltpu.VMEM((tokens, width), bf16),
            pltpu.VMEM((tokens, width), bf16),
            pltpu.VMEM((16, HD), bf16),
        ],
        compiler_params=params,
        name="gate_up",
    )(where, *parts, res, gain, w_gate, w_gate_sib, w_up, w_up_sib)

    got_shares = over_chips(shares)
    rows = w_down.shape[0]
    down_step = 4
    down_block = pl.BlockSpec((rows, 2 * width * down_step), lambda i: (0, i))
    down = pl.pallas_call(
        down_kernel,
        grid=(chips // down_step,),
        in_specs=[smem, fixed(chips, 4 * tokens + 16, HD), down_block, down_block],
        out_specs=pl.BlockSpec((down_step, tokens, 2 * width), lambda i: (i, 0, 0)),
        out_shape=jax.ShapeDtypeStruct((chips, tokens, 2 * width), bf16),
        scratch_shapes=[pltpu.VMEM((tokens, rows), bf16), pltpu.VMEM((tokens, rows), bf16)],
        compiler_params=params,
        name="down",
    )(where, got_shares, w_down, w_down_sib)

    lowered = jnp.sum(over_chips(down).astype(f32), axis=0)
    l0, l1, l2, l3 = heads(lowered)
    final = (stream + ((l0 + l1) + (l2 + l3))).astype(bf16)
    low, high = final[:, :width], final[:, width:]
    keep = jnp.where(core == 0, low, high)
    come = sibling(jnp.where(core == 0, high, low))
    even = jnp.where(core == 0, keep, come).reshape(STEPS, chips, 1, width)
    odd = jnp.where(core == 0, come, keep).reshape(STEPS, chips, 1, width)
    layer_out = jnp.concatenate([even, odd], axis=2).reshape(STEPS, holders, width)
    return (attended.reshape(STEPS, 1, HQ * HD), layer_out)


def solution(mesh):
    placed = (
        P(None, "seq", "head"),
        P(None, "seq", "head"),
        P(None, "head", None),
        P(None, "head"),
        P(None, "seq", "head"),
        P(None, "seq", "head"),
        P(None, "seq", "head"),
        P(None, None, "seq"),
        P("seq"),
        P("head", "seq"),
        P("seq", "head"),
        P("seq", "head"),
        P(("head", "seq"), None),
    )
    return jax.shard_map(
        on_device,
        mesh=mesh,
        in_specs=placed,
        out_specs=(P(None, "seq", "head"), P(None, None, "seq")),
        check_vma=False,
    )
```

time: 516 us -> 143 us (0.28)
  waiting for transfers between devices: 301 us -> 46.6 us
  blocking collectives: 90 us -> 14.4 us
  matrix products: 42.5 us -> 0 us
  Pallas kernels: 0 us -> 27.9 us
  starting transfers between devices: 17.9 us -> 37.6 us
  local copies, waits for them, and re-layouts: 32.6 us -> 13 us
  other arithmetic: 16.5 us -> 1.14 us
  between operations: 14 us -> 0.86 us
    reduce_scatter x2 -> x0, waiting for transfers between devices: 157 us -> none  [the longest x1 80.3 us: on_device(): lax.psum_scatter(lax.dot_general(w_down, activated, (((0,), (0,)), ((), (...]
    psum x2 -> x0, waiting for transfers between devices: 80.7 us -> none  [the longest x1 42.1 us: on_device(): lowered = lax.psum(down_part, 'head')]
    psum x1 -> x0, blocking collectives: 64.9 us -> none  [on_device(): square_sum = lax.psum(jnp.sum(stream * stream, axis=2), 'seq')]
    dot_general x10 -> x0, matrix products: 42.5 us -> none  [the longest x1 13.4 us: on_device(): jnp.einsum('bhkj,bjshd->bhksd', select, key_blocks, preferred_element_typ...]
    pallas_call x0 -> x5, Pallas kernels: none -> 27.9 us  [the longest x1 15 us: on_device(): pl.pallas_call(functools.partial(attend_kernel, per_dev), grid=(prompts /...]
    all_to_all x2 -> x4, waiting for transfers between devices: 62.5 us -> 36.6 us  [the longest x3 26.3 us: over_chips(): lax.all_to_all(x, 'seq', split_axis=0, concat_axis=0, tiled=True, axis_in...]
    all_gather x1 -> x0, blocking collectives: 25.1 us -> none  [on_device(): lax.all_gather(attended, 'seq', axis=1, tiled=True)]
    reshape x3, local copies, waits for them, and re-layouts: 25.1 us -> 2.09 us  [the longest x1 0.82 us: parity(): x = x.reshape(STEPS, chips, 2, width)]
  transfers between devices with their start and end apart: 6 -> 17, of which waited for: 6 -> 11; matrix products, arithmetic and copies ran while one was open for 7% -> 3% of each run, Pallas kernels for 0% -> 17%
where the time goes in v1:
time: 143 us; the launch traced here: 142 us
  waiting for transfers between devices  46.6 us (33%)
  starting transfers between devices  37.6 us (26%)
  Pallas kernels  27.9 us (20%)
  blocking collectives  14.4 us (10%)
  local copies, waits for them, and re-layouts  13 us (9%)
    all_to_all x3, waiting for transfers between devices, over_chips(): lax.all_to_all(x, 'seq', split_axis=0, concat_axis=0, tiled=True, axis_in...  26.3 us
    all_to_all x3, starting transfers between devices, over_chips(): lax.all_to_all(x, 'seq', split_axis=0, concat_axis=0, tiled=True, axis_in...  15.6 us
    pallas_call x1, Pallas kernels, on_device(): pl.pallas_call(functools.partial(attend_kernel, per_dev), grid=(prompts /...  15 us
    all_to_all x1, blocking collectives, over_chips(): lax.all_to_all(x, 'seq', split_axis=0, concat_axis=0, tiled=True, axis_in...  14.4 us
    all_to_all x1, waiting for transfers between devices, on_device(): lax.all_to_all(partial, 'seq', split_axis=0, concat_axis=0, tiled=True)  10.3 us
    ppermute x7, starting transfers between devices, sibling(): return lax.ppermute(x, 'seq', swap)  9.16 us
    ppermute x6, starting transfers between devices, heads(): lax.ppermute(x, 'head', [(i, i ^ s) for i in range(4)])  9 us
    unnamed x19, local copies, waits for them, and re-layouts  8.58 us
  transfers between devices with their start and end apart: 17, of which 11 were waited for; matrix products, arithmetic and copies ran while one was open for 3% of the time, Pallas kernels for 17%

profile of v1, /device:TPU:1, one launch (start us, length us, event | category | flops | bytes accessed | tf_op | source)
XLA Modules:
  0.0 141.5 jit_solution(10823052329805881413)
XLA Ops:
  2.1 8.4 %all-to-all-start = ((bf16[16,48,128]{2,1,0:T(8,128)(2,1)}), bf16[16,48,128]{2,1,0:T(8,128)(2,1)S(1)}, u32[]{:S(2)}, u32[]{:S(2)}) async-start(bf16[16,48,128]{2,1,0:T(8,128)(2,1)} %broadcast_in_dim.16), calls=%async_computation | async-start | bytes 393216 | tf_op jit(solution)/shard_map/all_to_all | solution.py:241
  10.5 0.8 reshape.45
  11.5 6.2 %all-to-all-done.q_own_ref = bf16[16,48,128]{2,1,0:T(8,128)(2,1)S(1)} async-done(((bf16[16,48,128]{2,1,0:T(8,128)(2,1)}), bf16[16,48,128]{2,1,0:T(8,128)(2,1)S(1)}, u32[]{:S(2)}, u32[]{:S(2)}) %all-to-all-start) | async-done | bytes 196640 | tf_op jit(solution)/shard_map/all_to_all | solution.py:241
  17.7 2.1 %collective-permute-start.6 = (bf16[256,4096]{1,0:T(8,128)(2,1)}, bf16[256,4096]{1,0:T(8,128)(2,1)}, u32[]{:S(2)}, u32[]{:S(2)}) collective-permute-start(bf16[256,4096]{1,0:T(8,128)(2,1)} %g_own.1), channel_id=1, source_target_pairs={{0,4},{4,0},{8,12},{12,8},{16,20},{20,16},{24,28},{28,24},{32,36},... | collective-permute-start | bytes 6291464 | tf_op jit(solution)/shard_map/ppermute | solution.py:249
  21.7 0.9 compare_select_fusion
  22.5 1.6 %collective-permute-done.q_sib_ref = bf16[16,48,128]{2,1,0:T(8,128)(2,1)S(1)} collective-permute-done((bf16[16,48,128]{2,1,0:T(8,128)(2,1)S(1)}, bf16[16,48,128]{2,1,0:T(8,128)(2,1)S(1)}, u32[]{:S(2)}, u32[]{:S(2)}) %collective-permute-start) | collective-permute-done | bytes 196640 | tf_op jit(solution)/shard_map/ppermute | solution.py:249
  24.2 3.4 %copy-done = bf16[32,512,256]{2,1,0:T(8,128)(2,1)S(1)} copy-done((bf16[32,512,256]{2,1,0:T(8,128)(2,1)S(1)}, bf16[32,512,256]{2,1,0:T(8,128)(2,1)}, u32[]{:S(2)}) %copy-start) | copy-done | bytes 8388632
  27.5 15.0 %attend.1 = bf16[32,64,128]{2,1,0:T(8,128)(2,1)} custom-call(s32[2]{0:T(128)S(1)} %pad_add_fusion.where_ref, s32[64,128]{1,0:T(8,128)S(1)} %bitcast.13, bf16[16,48,128]{2,1,0:T(8,128)(2,1)S(1)} %all-to-all-done.q_own_ref, bf16[16,48,128]{2,1,0:T(8,128)(2,1)S(1)} %collective-permute-done.q_sib_ref, bf16[32,512,256]{2,1,0:T(8,128)(2,1)S(1)} %copy-done, ...), custom_call_target="tpu_custom_call" | custom-call | tf_op jit(solution)/shard_map/attend/pallas_call | solution.py:272
  42.5 3.9 %all-to-all-start.1 = ((bf16[32,64,128]{2,1,0:T(8,128)(2,1)}), bf16[32,64,128]{2,1,0:T(8,128)(2,1)S(1)}, u32[]{:S(2)}, u32[]{:S(2)}) async-start(bf16[32,64,128]{2,1,0:T(8,128)(2,1)} %attend.1), calls=%async_computation.1 | async-start | bytes 1048576 | tf_op jit(solution)/shard_map/all_to_all | solution.py:300
  47.0 0.8 collective-permute-done.5
  47.8 10.3 %all-to-all-done.1.got_ref = bf16[32,64,128]{2,1,0:T(8,128)(2,1)S(1)} async-done(((bf16[32,64,128]{2,1,0:T(8,128)(2,1)}), bf16[32,64,128]{2,1,0:T(8,128)(2,1)S(1)}, u32[]{:S(2)}, u32[]{:S(2)}) %all-to-all-start.1) | async-done | bytes 524320 | tf_op jit(solution)/shard_map/all_to_all | solution.py:300
  59.6 3.5 %all-to-all-start.2 = ((bf16[16,48,128]{2,1,0:T(8,128)(2,1)}), bf16[16,48,128]{2,1,0:T(8,128)(2,1)S(1)}, u32[]{:S(2)}, u32[]{:S(2)}) async-start(bf16[16,48,128]{2,1,0:T(8,128)(2,1)} %broadcast_in_dim.17), calls=%async_computation.2 | async-start | bytes 393216 | tf_op jit(solution)/shard_map/all_to_all | solution.py:241
  63.2 7.6 %all-to-all-done.2.got_ref = bf16[16,48,128]{2,1,0:T(8,128)(2,1)S(1)} async-done(((bf16[16,48,128]{2,1,0:T(8,128)(2,1)}), bf16[16,48,128]{2,1,0:T(8,128)(2,1)S(1)}, u32[]{:S(2)}, u32[]{:S(2)}) %all-to-all-start.2) | async-done | bytes 196640 | tf_op jit(solution)/shard_map/all_to_all | solution.py:241
  70.8 1.2 copy-done.4
  72.0 1.7 %project.1.p0 = f32[48,512]{1,0:T(8,128)S(1)} custom-call(s32[2]{0:T(128)S(1)} %pad_add_fusion.where_ref, bf16[16,48,128]{2,1,0:T(8,128)(2,1)S(1)} %all-to-all-done.2.got_ref, bf16[2048,256]{1,0:T(8,128)(2,1)S(1)} %copy-done.4, bf16[2048,256]{1,0:T(8,128)(2,1)} %collective-permute-done.1.sib_ref), custom_call_target="tpu_custom_call" | custom-call | tf_op jit(solution)/shard_map/project/pallas_call | solution.py:317
  73.7 1.4 collective-permute-start.2
  75.1 2.6 %collective-permute-start.3 = (f32[48,512]{1,0:T(8,128)S(1)}, f32[48,512]{1,0:T(8,128)S(1)}, u32[]{:S(2)}, u32[]{:S(2)}) collective-permute-start(f32[48,512]{1,0:T(8,128)S(1)} %project.1.p0), channel_id=1, source_target_pairs={{0,2},{1,3},{2,0},{3,1},{4,6},{5,7},{6,4},{7,5},{8,10},{9,11},{10,... | collective-permute-start | bytes 294920 | tf_op jit(solution)/shard_map/ppermute | solution.py:252
  77.7 2.3 %collective-permute-start.4 = (f32[48,512]{1,0:T(8,128)S(1)}, f32[48,512]{1,0:T(8,128)S(1)}, u32[]{:S(2)}, u32[]{:S(2)}) collective-permute-start(f32[48,512]{1,0:T(8,128)S(1)} %project.1.p0), channel_id=1, source_target_pairs={{0,3},{1,2},{2,1},{3,0},{4,7},{5,6},{6,5},{7,4},{8,11},{9,10},{10,... | collective-permute-start | bytes 294920 | tf_op jit(solution)/shard_map/ppermute | solution.py:252
  80.0 1.1 collective-permute-done.3.p2
  81.0 2.4 %collective-permute-done.4.p3 = f32[48,512]{1,0:T(8,128)S(1)} collective-permute-done((f32[48,512]{1,0:T(8,128)S(1)}, f32[48,512]{1,0:T(8,128)S(1)}, u32[]{:S(2)}, u32[]{:S(2)}) %collective-permute-start.4) | collective-permute-done | bytes 98336 | tf_op jit(solution)/shard_map/ppermute | solution.py:252
  83.4 1.6 %copy-done.2 = bf16[256,4096]{1,0:T(8,128)(2,1)S(1)} copy-done((bf16[256,4096]{1,0:T(8,128)(2,1)S(1)}, bf16[256,4096]{1,0:T(8,128)(2,1)}, u32[]{:S(2)}) %copy-start.2) | copy-done | bytes 2097176
  85.0 7.1 %gate_up.1 = (bf16[16,208,128]{2,1,0:T(8,128)(2,1)}, f32[48,512]{1,0:T(8,128)S(1)}) custom-call(s32[2]{0:T(128)S(1)} %pad_add_fusion.where_ref, f32[48,512]{1,0:T(8,128)S(1)} %project.1.p0, f32[48,512]{1,0:T(8,128)S(1)} %collective-permute-done.2.p1, f32[48,512]{1,0:T(8,128)S(1)} %collective-permute-done.3.p2, f32[48,512]{1,0:T(8,128)S(1)} %collective-permute-done.4.p3, ...), custom_call_target="tpu_custom_call" | custom-call | tf_op jit(solution)/shard_map/gate_up/pallas_call | solution.py:332
  92.1 3.6 %all-to-all-start.3 = ((bf16[16,208,128]{2,1,0:T(8,128)(2,1)}), bf16[16,208,128]{2,1,0:T(8,128)(2,1)S(1)}, u32[]{:S(2)}, u32[]{:S(2)}) async-start(bf16[16,208,128]{2,1,0:T(8,128)(2,1)} %get-tuple-element.16), calls=%async_computation.3 | async-start | bytes 1703936 | tf_op jit(solution)/shard_map/all_to_all | solution.py:241
  95.8 12.5 %all-to-all-done.3.got_ref = bf16[16,208,128]{2,1,0:T(8,128)(2,1)S(1)} async-done(((bf16[16,208,128]{2,1,0:T(8,128)(2,1)}), bf16[16,208,128]{2,1,0:T(8,128)(2,1)S(1)}, u32[]{:S(2)}, u32[]{:S(2)}) %all-to-all-start.3) | async-done | bytes 852000 | tf_op jit(solution)/shard_map/all_to_all | solution.py:241
  108.3 1.6 %copy-done.3 = bf16[128,8192]{1,0:T(8,128)(2,1)S(1)} copy-done((bf16[128,8192]{1,0:T(8,128)(2,1)S(1)}, bf16[128,8192]{1,0:T(8,128)(2,1)}, u32[]{:S(2)}) %copy-start.3) | copy-done | bytes 2097176
  109.9 3.3 %down.1 = bf16[16,48,512]{2,1,0:T(8,128)(2,1)S(1)} custom-call(s32[2]{0:T(128)S(1)} %pad_add_fusion.where_ref, bf16[16,208,128]{2,1,0:T(8,128)(2,1)S(1)} %all-to-all-done.3.got_ref, bf16[128,8192]{1,0:T(8,128)(2,1)S(1)} %copy-done.3, bf16[128,8192]{1,0:T(8,128)(2,1)} %collective-permute-done.8.sib_ref), custom_call_target="tpu_custom_call" | custom-call | tf_op jit(solution)/shard_map/down/pallas_call | solution.py:360
  113.1 14.4 %all_to_all.25 = bf16[16,48,512]{2,1,0:T(8,128)(2,1)S(1)} all-to-all(bf16[16,48,512]{2,1,0:T(8,128)(2,1)S(1)} %down.1), channel_id=1, replica_groups={{0,8,16,24,32,40,48,56,64,72,80,88,96,104,112,120},{4,12,20,28,36,44,52..., dimensions={0} | all-to-all | bytes 1572864 | tf_op jit(solution)/shard_map/all_to_all | solution.py:241
  127.7 1.9 %collective-permute-start.10 = (f32[48,512]{1,0:T(8,128)S(1)}, f32[48,512]{1,0:T(8,128)S(1)}, u32[]{:S(2)}, u32[]{:S(2)}) collective-permute-start(f32[48,512]{1,0:T(8,128)S(1)} %convert_reduce_fusion), channel_id=1, source_target_pairs={{0,2},{1,3},{2,0},{3,1},{4,6},{5,7},{6,4},{7,5},{8,10},{9,11},{10,... | collective-permute-start | bytes 294920 | tf_op jit(solution)/shard_map/ppermute | solution.py:252
  129.6 0.8 collective-permute-start.9
  130.4 2.3 %collective-permute-done.10 = f32[48,512]{1,0:T(8,128)S(1)} collective-permute-done((f32[48,512]{1,0:T(8,128)S(1)}, f32[48,512]{1,0:T(8,128)S(1)}, u32[]{:S(2)}, u32[]{:S(2)}) %collective-permute-start.10) | collective-permute-done | bytes 98336 | tf_op jit(solution)/shard_map/ppermute | solution.py:252
  132.7 1.5 %collective-permute-done.11 = f32[48,512]{1,0:T(8,128)S(1)} collective-permute-done((f32[48,512]{1,0:T(8,128)S(1)}, f32[48,512]{1,0:T(8,128)S(1)}, u32[]{:S(2)}, u32[]{:S(2)}) %collective-permute-start.11) | collective-permute-done | bytes 98336 | tf_op jit(solution)/shard_map/ppermute | solution.py:252
  134.3 5.6 %collective-permute-start.12 = (bf16[48,256]{1,0:T(8,128)(2,1)S(1)}, bf16[48,256]{1,0:T(8,128)(2,1)S(1)}, u32[]{:S(2)}, u32[]{:S(2)}) collective-permute-start(bf16[48,256]{1,0:T(8,128)(2,1)S(1)} %broadcast_select_fusion.2), channel_id=1, source_target_pairs={{0,4},{4,0},{8,12},{12,8},{16,20},{20,16},{24,28},{28,24},{32,36},... | collective-permute-start | bytes 73736 | tf_op jit(solution)/shard_map/ppermute | solution.py:249
  (50 shorter events, 7.2 us)
Async XLA Ops:
  2.1 15.6 %all-to-all-start = ((bf16[16,48,128]{2,1,0:T(8,128)(2,1)}), bf16[16,48,128]{2,1,0:T(8,128)(2,1)S(1)}, u32[]{:S(2)}, u32[]{:S(2)}) async-start(bf16[16,48,128]{2,1,0:T(8,128)(2,1)} %broadcast_in_dim.16), calls=%async_computation | async-start | bytes 393216 | tf_op jit(solution)/shard_map/all_to_all | solution.py:241
  17.7 65.7 %collective-permute-start.6 = (bf16[256,4096]{1,0:T(8,128)(2,1)}, bf16[256,4096]{1,0:T(8,128)(2,1)}, u32[]{:S(2)}, u32[]{:S(2)}) collective-permute-start(bf16[256,4096]{1,0:T(8,128)(2,1)} %g_own.1), channel_id=1, source_target_pairs={{0,4},{4,0},{8,12},{12,8},{16,20},{20,16},{24,28},{28,24},{32,36},... | collective-permute-start | bytes 6291464 | tf_op jit(solution)/shard_map/ppermute | solution.py:249
  19.8 63.6 %collective-permute-start.7 = (bf16[256,4096]{1,0:T(8,128)(2,1)}, bf16[256,4096]{1,0:T(8,128)(2,1)}, u32[]{:S(2)}, u32[]{:S(2)}) collective-permute-start(bf16[256,4096]{1,0:T(8,128)(2,1)} %u_own.1), channel_id=1, source_target_pairs={{0,4},{4,0},{8,12},{12,8},{16,20},{20,16},{24,28},{28,24},{32,36},... | collective-permute-start | bytes 6291464 | tf_op jit(solution)/shard_map/ppermute | solution.py:249
  19.8 76.0 %collective-permute-start.8 = (bf16[128,8192]{1,0:T(8,128)(2,1)}, bf16[128,8192]{1,0:T(8,128)(2,1)}, u32[]{:S(2)}, u32[]{:S(2)}) collective-permute-start(bf16[128,8192]{1,0:T(8,128)(2,1)} %own_ref.3), channel_id=1, source_target_pairs={{0,4},{4,0},{8,12},{12,8},{16,20},{20,16},{24,28},{28,24},{32,36},... | collective-permute-start | bytes 6291464 | tf_op jit(solution)/shard_map/ppermute | solution.py:249
  21.1 49.7 %collective-permute-start.1 = (bf16[2048,256]{1,0:T(8,128)(2,1)}, bf16[2048,256]{1,0:T(8,128)(2,1)}, u32[]{:S(2)}, u32[]{:S(2)}) collective-permute-start(bf16[2048,256]{1,0:T(8,128)(2,1)} %own_ref.2), channel_id=1, source_target_pairs={{0,4},{4,0},{8,12},{12,8},{16,20},{20,16},{24,28},{28,24},{32,36},... | collective-permute-start | bytes 3145736 | tf_op jit(solution)/shard_map/ppermute | solution.py:249
  21.2 3.0 %collective-permute-start = (bf16[16,48,128]{2,1,0:T(8,128)(2,1)S(1)}, bf16[16,48,128]{2,1,0:T(8,128)(2,1)S(1)}, u32[]{:S(2)}, u32[]{:S(2)}) collective-permute-start(bf16[16,48,128]{2,1,0:T(8,128)(2,1)S(1)} %all-to-all-done.q_own_ref), channel_id=1, source_target_pairs={{0,4},{4,0},{8,12},{12,8},{16,20},{20,16},{24,28},{28,24},{32,36},... | collective-permute-start | bytes 589832 | tf_op jit(solution)/shard_map/ppermute | solution.py:249
  24.2 3.4 %copy-start = (bf16[32,512,256]{2,1,0:T(8,128)(2,1)S(1)}, bf16[32,512,256]{2,1,0:T(8,128)(2,1)}, u32[]{:S(2)}) copy-start(bf16[32,512,256]{2,1,0:T(8,128)(2,1)} %k_ref.1) | copy-start | bytes 25165828
  27.5 18.9 %copy-start.5 = (bf16[256]{0:T(256)(128)(2,1)S(1)}, bf16[256]{0:T(256)(128)(2,1)}, u32[]{:S(2)}) copy-start(bf16[256]{0:T(256)(128)(2,1)} %param.21) | copy-start | bytes 1540
  27.5 19.4 %copy-start.6 = (bf16[3,1,256]{2,0,1:T(4,128)(2,1)S(1)}, bf16[3,1,256]{2,0,1:T(4,128)(2,1)}, u32[]{:S(2)}) copy-start(bf16[3,1,256]{2,0,1:T(4,128)(2,1)} %param.18) | copy-start | bytes 4612
  27.5 19.4 %copy-start.7 = (bf16[3,1,256]{2,0,1:T(4,128)(2,1)S(1)}, bf16[3,1,256]{2,0,1:T(4,128)(2,1)}, u32[]{:S(2)}) copy-start(bf16[3,1,256]{2,0,1:T(4,128)(2,1)} %param.19) | copy-start | bytes 4612
  42.5 15.6 %all-to-all-start.1 = ((bf16[32,64,128]{2,1,0:T(8,128)(2,1)}), bf16[32,64,128]{2,1,0:T(8,128)(2,1)S(1)}, u32[]{:S(2)}, u32[]{:S(2)}) async-start(bf16[32,64,128]{2,1,0:T(8,128)(2,1)} %attend.1), calls=%async_computation.1 | async-start | bytes 1048576 | tf_op jit(solution)/shard_map/all_to_all | solution.py:300
  46.5 37.0 %copy-start.1 = (bf16[256,4096]{1,0:T(8,128)(2,1)S(1)}, bf16[256,4096]{1,0:T(8,128)(2,1)}, u32[]{:S(2)}) copy-start(bf16[256,4096]{1,0:T(8,128)(2,1)} %g_own.1) | copy-start | bytes 6291460
  46.5 1.3 collective-permute-start.5
  59.6 11.1 %all-to-all-start.2 = ((bf16[16,48,128]{2,1,0:T(8,128)(2,1)}), bf16[16,48,128]{2,1,0:T(8,128)(2,1)S(1)}, u32[]{:S(2)}, u32[]{:S(2)}) async-start(bf16[16,48,128]{2,1,0:T(8,128)(2,1)} %broadcast_in_dim.17), calls=%async_computation.2 | async-start | bytes 393216 | tf_op jit(solution)/shard_map/all_to_all | solution.py:241
  70.8 1.2 copy-start.4
  73.7 4.0 %collective-permute-start.2 = (f32[48,512]{1,0:T(8,128)S(1)}, f32[48,512]{1,0:T(8,128)S(1)}, u32[]{:S(2)}, u32[]{:S(2)}) collective-permute-start(f32[48,512]{1,0:T(8,128)S(1)} %project.1.p0), channel_id=1, source_target_pairs={{0,1},{1,0},{2,3},{3,2},{4,5},{5,4},{6,7},{7,6},{8,9},{9,8},{10,11... | collective-permute-start | bytes 294920 | tf_op jit(solution)/shard_map/ppermute | solution.py:252
  75.1 6.0 %collective-permute-start.3 = (f32[48,512]{1,0:T(8,128)S(1)}, f32[48,512]{1,0:T(8,128)S(1)}, u32[]{:S(2)}, u32[]{:S(2)}) collective-permute-start(f32[48,512]{1,0:T(8,128)S(1)} %project.1.p0), channel_id=1, source_target_pairs={{0,2},{1,3},{2,0},{3,1},{4,6},{5,7},{6,4},{7,5},{8,10},{9,11},{10,... | collective-permute-start | bytes 294920 | tf_op jit(solution)/shard_map/ppermute | solution.py:252
  77.7 5.7 %collective-permute-start.4 = (f32[48,512]{1,0:T(8,128)S(1)}, f32[48,512]{1,0:T(8,128)S(1)}, u32[]{:S(2)}, u32[]{:S(2)}) collective-permute-start(f32[48,512]{1,0:T(8,128)S(1)} %project.1.p0), channel_id=1, source_target_pairs={{0,3},{1,2},{2,1},{3,0},{4,7},{5,6},{6,5},{7,4},{8,11},{9,10},{10,... | collective-permute-start | bytes 294920 | tf_op jit(solution)/shard_map/ppermute | solution.py:252
  83.4 1.6 %copy-start.2 = (bf16[256,4096]{1,0:T(8,128)(2,1)S(1)}, bf16[256,4096]{1,0:T(8,128)(2,1)}, u32[]{:S(2)}) copy-start(bf16[256,4096]{1,0:T(8,128)(2,1)} %u_own.1) | copy-start | bytes 6291460
  92.1 16.1 %all-to-all-start.3 = ((bf16[16,208,128]{2,1,0:T(8,128)(2,1)}), bf16[16,208,128]{2,1,0:T(8,128)(2,1)S(1)}, u32[]{:S(2)}, u32[]{:S(2)}) async-start(bf16[16,208,128]{2,1,0:T(8,128)(2,1)} %get-tuple-element.16), calls=%async_computation.3 | async-start | bytes 1703936 | tf_op jit(solution)/shard_map/all_to_all | solution.py:241
  108.3 1.6 %copy-start.3 = (bf16[128,8192]{1,0:T(8,128)(2,1)S(1)}, bf16[128,8192]{1,0:T(8,128)(2,1)}, u32[]{:S(2)}) copy-start(bf16[128,8192]{1,0:T(8,128)(2,1)} %own_ref.3) | copy-start | bytes 6291460
  127.7 5.1 %collective-permute-start.10 = (f32[48,512]{1,0:T(8,128)S(1)}, f32[48,512]{1,0:T(8,128)S(1)}, u32[]{:S(2)}, u32[]{:S(2)}) collective-permute-start(f32[48,512]{1,0:T(8,128)S(1)} %convert_reduce_fusion), channel_id=1, source_target_pairs={{0,2},{1,3},{2,0},{3,1},{4,6},{5,7},{6,4},{7,5},{8,10},{9,11},{10,... | collective-permute-start | bytes 294920 | tf_op jit(solution)/shard_map/ppermute | solution.py:252
  129.6 4.7 %collective-permute-start.11 = (f32[48,512]{1,0:T(8,128)S(1)}, f32[48,512]{1,0:T(8,128)S(1)}, u32[]{:S(2)}, u32[]{:S(2)}) collective-permute-start(f32[48,512]{1,0:T(8,128)S(1)} %convert_reduce_fusion), channel_id=1, source_target_pairs={{0,3},{1,2},{2,1},{3,0},{4,7},{5,6},{6,5},{7,4},{8,11},{9,10},{10,... | collective-permute-start | bytes 294920 | tf_op jit(solution)/shard_map/ppermute | solution.py:252
  129.6 4.7 %collective-permute-start.9 = (f32[48,512]{1,0:T(8,128)S(1)}, f32[48,512]{1,0:T(8,128)S(1)}, u32[]{:S(2)}, u32[]{:S(2)}) collective-permute-start(f32[48,512]{1,0:T(8,128)S(1)} %convert_reduce_fusion), channel_id=1, source_target_pairs={{0,1},{1,0},{2,3},{3,2},{4,5},{5,4},{6,7},{7,6},{8,9},{9,8},{10,11... | collective-permute-start | bytes 294920 | tf_op jit(solution)/shard_map/ppermute | solution.py:252
  134.3 6.5 %collective-permute-start.12 = (bf16[48,256]{1,0:T(8,128)(2,1)S(1)}, bf16[48,256]{1,0:T(8,128)(2,1)S(1)}, u32[]{:S(2)}, u32[]{:S(2)}) collective-permute-start(bf16[48,256]{1,0:T(8,128)(2,1)S(1)} %broadcast_select_fusion.2), channel_id=1, source_target_pairs={{0,4},{4,0},{8,12},{12,8},{16,20},{20,16},{24,28},{28,24},{32,36},... | collective-permute-start | bytes 73736 | tf_op jit(solution)/shard_map/ppermute | solution.py:249

commit v2 on v1

v2 whole, which is shorter than its diff:
```python
import functools

import jax
import jax.numpy as jnp
from jax import lax
from jax.experimental import pallas as pl
from jax.experimental.pallas import tpu as pltpu
from jax.sharding import PartitionSpec as P

D = 8192
H = 64
KVH = 8
HD = 128
BLK = 64
CAP = 4
GROUPS = H // KVH

masked_score = -1e30
norm_eps = 1e-06
score_scale = HD ** (-0.5)

f32 = jnp.float32
bf16 = jnp.bfloat16
MIB = 1 << 20

STEPS = 3
KV = 2
HQ = KV * GROUPS
ROWS = STEPS * HQ
PACK = ROWS + 16


def dot(a, b, ca=1, cb=0):
    return lax.dot_general(a, b, (((ca,), (cb,)), ((), ())), preferred_element_type=f32)


def first_head_rows():
    rows = lax.broadcasted_iota(jnp.int32, (ROWS, 1), 0)
    return (rows // GROUPS) % KV == 0


def two_head_queries(q, first):
    zero = jnp.zeros_like(q)
    return jnp.concatenate([jnp.where(first, q, zero), jnp.where(first, zero, q)], axis=1)


def per_head(values, first):
    return jnp.where(first, values[:, :HD], values[:, HD:])


def pack_prompt(prompt, codes, k_ref, v_ref, packed_ref, sem):
    half = CAP * BLK
    for h in range(KV):
        lanes = pl.ds(h * HD, HD)
        for s in range(CAP):
            at = pl.multiple_of(((codes[h] >> (3 * s)) & 7) * BLK, BLK)
            for part, cache_ref in enumerate((k_ref, v_ref)):
                pltpu.make_async_copy(
                    cache_ref.at[prompt, pl.ds(at, BLK), lanes],
                    packed_ref.at[pl.ds(part * half + s * BLK, BLK), lanes],
                    sem,
                ).start()


def gather_kernel(
    where_ref, count_ref, lists_ref, k_ref, v_ref, out_ref, codes_ref,
    wide_ref, scalar_ref, packed_ref, list_sem, in_sems, out_sems,
):
    core = where_ref[1]
    per_dev = k_ref.shape[1] // BLK
    base = where_ref[0] * per_dev
    sib_base = (where_ref[0] + 1 - 2 * core) * per_dev
    lists = lists_ref[...]
    lane = lax.broadcasted_iota(jnp.int32, lists.shape, 2)
    valid = (lists > 0) | (lane == 0)
    before = jnp.sum(jnp.where(valid & (lists < base), 1.0, 0.0), axis=2, keepdims=True)
    local = lists - base
    mine = valid & (local >= 0) & (local < per_dev)
    theirs = valid & (lists >= sib_base) & (lists < sib_base + per_dev)
    rank = jnp.clip(lane - before.astype(jnp.int32), 0, CAP - 1)
    share = jnp.where(mine, jnp.left_shift(local, 3 * rank) + (1 << 12), 0)
    share = share + jnp.where(theirs, 1 << 15, 0)
    code = jnp.sum(share.astype(f32), axis=2, keepdims=True).astype(jnp.int32)
    spot = lax.broadcasted_iota(jnp.int32, lists.shape, 0) * KV + lax.broadcasted_iota(
        jnp.int32, lists.shape, 1
    )
    wide_ref[...] = jnp.sum(jnp.sum(jnp.where(lane == spot, code, 0), axis=0), axis=0, keepdims=True)
    listed = pltpu.make_async_copy(wide_ref, scalar_ref, list_sem)
    listed.start()
    listed.wait()

    def code_of(prompt, h):
        return jnp.where(count_ref[h, prompt] > 0, scalar_ref[0, prompt * KV + h], 0)

    chips = packed_ref.shape[0]
    groups = in_sems.shape[0]
    size = chips // groups
    for g in range(groups):

        def one(i, carry):
            chip = g * size + i
            prompt = chip * 2 + 1 - core
            codes = [code_of(prompt, h) for h in range(KV)]
            pack_prompt(prompt, codes, k_ref, v_ref, packed_ref.at[chip], in_sems.at[g])
            for h in range(KV):
                codes_ref[chip * KV + h] = code_of(chip * 2 + core, h)
            return carry

        lax.fori_loop(0, size, one, 0)
    leaving = []
    for g in range(groups):
        at = pl.ds(g * size, size)
        pltpu.make_async_copy(packed_ref.at[at], packed_ref.at[at], in_sems.at[g]).wait()
        leaving.append(pltpu.make_async_copy(packed_ref.at[at], out_ref.at[at], out_sems.at[g]))
        leaving[-1].start()
    for copy in leaving:
        copy.wait()


def attend_kernel(
    where_ref, codes_ref, q_ref, k_ref, v_ref, sib_hbm, out_ref, own_ref, sib_ref, own_sems, sib_sems
):
    core = where_ref[1]
    half = CAP * BLK
    chips = q_ref.shape[0]
    groups = own_sems.shape[0]
    size = chips // groups
    first = first_head_rows()
    lane = lax.broadcasted_iota(jnp.int32, (ROWS, HD), 1)
    slot_lane = lax.broadcasted_iota(jnp.int32, (ROWS, half), 1)
    unit = (
        lax.broadcasted_iota(jnp.int32, (16, HD), 0) == lax.broadcasted_iota(jnp.int32, (16, HD), 1)
    ).astype(bf16)

    def from_sib(g):
        at = pl.ds(g * size, size)
        return pltpu.make_async_copy(sib_hbm.at[at], sib_ref.at[at], sib_sems.at[g])

    def fetch(g):
        from_sib(g).start()

        def one(i, carry):
            chip = g * size + i
            codes = [codes_ref[chip * KV + h] for h in range(KV)]
            pack_prompt(chip * 2 + core, codes, k_ref, v_ref, own_ref.at[chip], own_sems.at[g])
            return carry

        lax.fori_loop(0, size, one, 0)

    def score_of(chip):
        queries = two_head_queries(q_ref[chip], first)
        scores, keeps = [], []
        for shift, blocks_ref in ((12, own_ref), (15, sib_ref)):
            ends = [((codes_ref[chip * KV + h] >> shift) & 7) * BLK for h in range(KV)]
            keeps.append(slot_lane < jnp.where(first, ends[0], ends[1]))
            scores.append(dot(queries, blocks_ref[chip, :half, :], 1, 1))
        return jnp.concatenate(keeps, axis=1), jnp.concatenate(scores, axis=1)

    def weigh(keep, score):
        score = jnp.where(keep, score * score_scale, masked_score)
        top = jnp.max(score, axis=1, keepdims=True).astype(bf16).astype(f32)
        weight = jnp.where(keep, jnp.exp(score - top), 0.0).astype(bf16)
        return top, weight, jnp.sum(weight.astype(f32), axis=1, keepdims=True)

    def store(chip, top, weight, total):
        summed = per_head(
            dot(weight[:, :half], own_ref[chip, half:, :])
            + dot(weight[:, half:], sib_ref[chip, half:, :]),
            first,
        )
        total_hi = total.astype(bf16).astype(f32)
        notes = jnp.where(
            lane == 0, top, jnp.where(lane == 1, total_hi, jnp.where(lane == 2, total - total_hi, 0.0))
        ).astype(bf16)
        notes = jnp.concatenate([notes, jnp.zeros((HD - ROWS, HD), bf16)], axis=0)
        out_ref[chip, :ROWS, :] = summed.astype(bf16)
        out_ref[chip, ROWS:, :] = dot(unit, notes, 1, 1).astype(bf16)

    fetch(0)
    for g in range(groups):
        if g + 1 < groups:
            fetch(g + 1)
        at = pl.ds(g * size, size)
        pltpu.make_async_copy(own_ref.at[at], own_ref.at[at], own_sems.at[g]).wait()
        from_sib(g).wait()
        chips_now = range(g * size, (g + 1) * size)
        scored = [score_of(chip) for chip in chips_now]
        weighed = [weigh(*each) for each in scored]
        for chip, each in zip(chips_now, weighed):
            store(chip, *each)


def combine_kernel(got_ref, q_ref, nk_ref, nv_ref, out_ref):
    holders = got_ref.shape[0]
    notes = got_ref[:, ROWS:, :].reshape(holders * 16, HD)
    row = lax.broadcasted_iota(jnp.int32, (holders * 16, HD), 0)
    col = lax.broadcasted_iota(jnp.int32, (holders * 16, HD), 1)
    pick = ((col == (row % 16) * holders + row // 16) & (row % 16 < 3)).astype(bf16)
    columns = dot(notes, pick, 0, 0)[:ROWS]
    tops = columns[:, :holders]
    totals = columns[:, holders : 2 * holders] + columns[:, 2 * holders : 3 * holders]
    first = first_head_rows()
    new_score = dot(two_head_queries(q_ref[...], first), nk_ref[...], 1, 1) * score_scale
    step = lax.broadcasted_iota(jnp.int32, new_score.shape, 0) // HQ
    token = lax.broadcasted_iota(jnp.int32, new_score.shape, 1)
    causal = token <= step
    new_score = jnp.where(causal, new_score, masked_score)
    top = jnp.maximum(
        jnp.max(tops, axis=1, keepdims=True), jnp.max(new_score, axis=1, keepdims=True)
    )
    share = jnp.exp(tops - top)
    new_weight = jnp.where(causal, jnp.exp(new_score - top), 0.0).astype(bf16)
    total = jnp.sum(share * totals, axis=1, keepdims=True) + jnp.sum(
        new_weight.astype(f32), axis=1, keepdims=True
    )
    summed = per_head(dot(new_weight, nv_ref[...]), first)
    for i in range(holders):
        summed = summed + share[:, i : i + 1] * got_ref[i, :ROWS, :].astype(f32)
    out_ref[...] = (summed / total).astype(bf16)


def project_kernel(where_ref, got_ref, own_ref, sib_ref, out_ref, wide_ref):
    core = where_ref[1]
    chips = got_ref.shape[0]
    wide_ref[...] = got_ref[...].reshape(chips * ROWS, HD).astype(f32)
    own = jnp.zeros((STEPS * chips, own_ref.shape[1]), f32)
    sib = jnp.zeros((STEPS * chips, own_ref.shape[1]), f32)
    for pair in range(HQ // 2):
        parts = []
        for h in (2 * pair, 2 * pair + 1):
            parts.append(
                jnp.concatenate(
                    [wide_ref[pl.ds(t * HQ + h, chips, stride=ROWS), :] for t in range(STEPS)], axis=0
                )
            )
        rows = jnp.concatenate(parts, axis=1).astype(bf16)
        at = slice(pair * 2 * HD, (pair + 1) * 2 * HD)
        own = own + dot(rows, own_ref[at, :])
        sib = sib + dot(rows, sib_ref[at, :])
    half = own_ref.shape[1]
    out_ref[:, :half] = jnp.where(core == 0, own, sib)
    out_ref[:, half:] = jnp.where(core == 0, sib, own)


def gate_up_kernel(
    where_ref, p0, p1, p2, p3, res_ref, gain_ref, g_own, g_sib, u_own, u_sib, out_ref, stream_ref
):
    core = where_ref[1]
    half = g_own.shape[0]
    chips = out_ref.shape[0]
    stream = res_ref[...].astype(f32) + ((p0[...] + p1[...]) + (p2[...] + p3[...]))
    stream_ref[...] = stream
    scaled = stream * gain_ref[0:1, :].astype(f32)
    mine = jnp.where(core == 0, scaled[:, :half], scaled[:, half:]).astype(bf16)
    other = jnp.where(core == 0, scaled[:, half:], scaled[:, :half]).astype(bf16)
    square = jnp.sum(stream * stream, axis=1, keepdims=True)
    square_hi = square.astype(bf16).astype(f32)
    tokens = square.shape[0]
    lane = lax.broadcasted_iota(jnp.int32, (tokens, HD), 1)
    notes = jnp.where(
        lane == 0, square_hi, jnp.where(lane == 1, square - square_hi, 0.0)
    ).astype(bf16)
    notes = jnp.concatenate([notes, jnp.zeros((HD - tokens, HD), bf16)], axis=0)
    unit = (
        lax.broadcasted_iota(jnp.int32, (16, HD), 0) == lax.broadcasted_iota(jnp.int32, (16, HD), 1)
    ).astype(bf16)
    squares = dot(unit, notes, 1, 1).astype(bf16)
    wide = g_own.shape[1] // chips

    def store(k, gate, up):
        for part in range(2):
            at = slice(part * HD, (part + 1) * HD)
            out_ref[k, part * tokens : (part + 1) * tokens, :] = gate[:, at]
            out_ref[k, (2 + part) * tokens : (3 + part) * tokens, :] = up[:, at]
        out_ref[k, 4 * tokens :, :] = squares

    ready = None
    for k in range(chips):
        at = slice(k * wide, (k + 1) * wide)
        gate = dot(mine, g_own[:, at]) + dot(other, g_sib[:, at])
        up = dot(mine, u_own[:, at]) + dot(other, u_sib[:, at])
        if ready:
            store(*ready)
        ready = k, gate.astype(bf16), up.astype(bf16)
    store(*ready)


def down_kernel(where_ref, got_ref, own_ref, sib_ref, out_ref):
    core = where_ref[1]
    chips, tokens, width = out_ref.shape
    total = got_ref[0].astype(f32)
    for i in range(1, chips):
        total = total + got_ref[i].astype(f32)
    square = total[4 * tokens : 4 * tokens + 1, :] + total[4 * tokens + 1 : 4 * tokens + 2, :]
    scale_row = lax.rsqrt(square / D + norm_eps)
    row = lax.broadcasted_iota(jnp.int32, (tokens, HD), 0)
    col = lax.broadcasted_iota(jnp.int32, (tokens, HD), 1)
    scale = jnp.sum(jnp.where(row == col, scale_row, 0.0), axis=1, keepdims=True)
    halves = []
    for part in range(2):
        gate = total[part * tokens : (part + 1) * tokens] * scale
        up = total[(2 + part) * tokens : (3 + part) * tokens] * scale
        halves.append(gate / (1.0 + jnp.exp(-gate)) * up)
    mine = jnp.where(core == 0, halves[0], halves[1]).astype(bf16)
    other = jnp.where(core == 0, halves[1], halves[0]).astype(bf16)
    rows = jnp.concatenate([mine, other], axis=1)
    for k in range(chips):
        at = slice(k * width, (k + 1) * width)
        out_ref[k] = dot(rows, jnp.concatenate([own_ref[:, at], sib_ref[:, at]], axis=0)).astype(bf16)


def on_device(
    keys_cache,
    values_cache,
    keep_blocks,
    keep_count,
    queries,
    new_keys,
    new_values,
    residual_in,
    norm_gain,
    w_out,
    w_gate,
    w_up,
    w_down,
):
    holders = lax.axis_size("seq")
    chips = holders // 2
    holder = lax.axis_index("seq").astype(jnp.int32)
    core = holder % 2
    prompts, positions = keys_cache.shape[:2]
    per_dev = positions // BLK
    list_length = keep_blocks.shape[2]
    tokens = STEPS * chips
    width = residual_in.shape[2]
    where = jnp.stack([holder, core])
    smem = pl.BlockSpec(memory_space=pltpu.SMEM)
    vmem = pl.BlockSpec(memory_space=pltpu.VMEM)
    hbm = pl.BlockSpec(memory_space=pltpu.HBM)
    params = pltpu.CompilerParams(vmem_limit_bytes=24 * MIB)

    same_core = [[2 * i + c for i in range(chips)] for c in range(2)]
    swap = [(i, i ^ 1) for i in range(holders)]

    def over_chips(x):
        return lax.all_to_all(
            x, "seq", split_axis=0, concat_axis=0, tiled=True, axis_index_groups=same_core
        )

    def to_all_chips(x):
        return over_chips(jnp.broadcast_to(x[None], (chips,) + x.shape))

    def sibling(x):
        return lax.ppermute(x, "seq", swap)

    def heads(x):
        return [x] + [lax.ppermute(x, "head", [(i, i ^ s) for i in range(4)]) for s in (1, 2, 3)]

    def parity(x, which):
        x = x.reshape(STEPS, chips, 2, width)
        return lax.dynamic_slice_in_dim(x, which, 1, 2).reshape(tokens, width)

    def in_order(own, sib):
        low = jnp.where(core == 0, own, sib)
        high = jnp.where(core == 0, sib, own)
        return jnp.concatenate([low, high], axis=1)

    q_rows = queries.reshape(ROWS, HD)
    q_own = to_all_chips(q_rows)

    half = CAP * BLK
    tile = (chips, 2 * half, KV * HD)
    groups = 4
    dma = pltpu.SemaphoreType.DMA
    to_sib, codes = pl.pallas_call(
        gather_kernel,
        in_specs=[smem, smem, vmem, hbm, hbm],
        out_specs=[hbm, smem],
        out_shape=[jax.ShapeDtypeStruct(tile, bf16), jax.ShapeDtypeStruct((chips * KV,), jnp.int32)],
        scratch_shapes=[
            pltpu.VMEM((1, list_length), jnp.int32),
            pltpu.SMEM((1, list_length), jnp.int32),
            pltpu.VMEM(tile, bf16),
            dma,
            dma((groups,)),
            dma((groups,)),
        ],
        compiler_params=pltpu.CompilerParams(vmem_limit_bytes=50 * MIB),
        name="gather",
    )(where, keep_count.T, keep_blocks, keys_cache, values_cache)
    sib_packed = sibling(to_sib)
    partial = pl.pallas_call(
        attend_kernel,
        in_specs=[smem, smem, vmem, hbm, hbm, pl.BlockSpec(memory_space=pl.ANY)],
        out_specs=vmem,
        out_shape=jax.ShapeDtypeStruct((chips, PACK, HD), bf16),
        scratch_shapes=[pltpu.VMEM(tile, bf16)] * 2 + [dma((groups,))] * 2,
        compiler_params=pltpu.CompilerParams(vmem_limit_bytes=50 * MIB),
        name="attend",
    )(where, codes, q_own, keys_cache, values_cache, sib_packed)

    (w_out_s, w_gate_s, w_up_s, w_down_s, res_s, gain_s), _ = lax.optimization_barrier(
        ((w_out, w_gate, w_up, w_down, parity(residual_in, 1 - core), norm_gain), q_own)
    )
    w_out_sib = sibling(w_out_s)
    w_gate_sib = sibling(w_gate_s)
    w_up_sib = sibling(w_up_s)
    w_down_sib = sibling(w_down_s)
    extra = sibling(jnp.concatenate([res_s, jnp.broadcast_to(gain_s[None], (16, width))], axis=0))
    res = in_order(parity(residual_in, core), extra[:tokens])
    gain = in_order(jnp.broadcast_to(norm_gain[None], (16, width)), extra[tokens:])

    got = over_chips(partial)
    pad = ((0, 16 - STEPS), (0, 0))
    attended = pl.pallas_call(
        combine_kernel,
        in_specs=[vmem] * 4,
        out_specs=vmem,
        out_shape=jax.ShapeDtypeStruct((ROWS, HD), bf16),
        compiler_params=params,
        name="combine",
    )(
        got,
        q_rows,
        jnp.pad(new_keys.reshape(STEPS, KV * HD), pad),
        jnp.pad(new_values.reshape(STEPS, KV * HD), pad),
    )

    all_attended = to_all_chips(attended)
    projected = pl.pallas_call(
        project_kernel,
        in_specs=[smem, vmem, vmem, vmem],
        out_specs=vmem,
        out_shape=jax.ShapeDtypeStruct((tokens, 2 * width), f32),
        scratch_shapes=[pltpu.VMEM((chips * ROWS, HD), f32)],
        compiler_params=params,
        name="project",
    )(where, all_attended, w_out, w_out_sib)
    parts = heads(projected)

    shares, stream = pl.pallas_call(
        gate_up_kernel,
        in_specs=[smem] + [vmem] * 10,
        out_specs=[vmem, vmem],
        out_shape=[
            jax.ShapeDtypeStruct((chips, 4 * tokens + 16, HD), bf16),
            jax.ShapeDtypeStruct((tokens, 2 * width), f32),
        ],
        compiler_params=params,
        name="gate_up",
    )(where, *parts, res, gain, w_gate, w_gate_sib, w_up, w_up_sib)

    got_shares = over_chips(shares)
    down = pl.pallas_call(
        down_kernel,
        in_specs=[smem, vmem, vmem, vmem],
        out_specs=vmem,
        out_shape=jax.ShapeDtypeStruct((chips, tokens, 2 * width), bf16),
        compiler_params=params,
        name="down",
    )(where, got_shares, w_down, w_down_sib)

    lowered = jnp.sum(over_chips(down).astype(f32), axis=0)
    l0, l1, l2, l3 = heads(lowered)
    final = (stream + ((l0 + l1) + (l2 + l3))).astype(bf16)
    low, high = final[:, :width], final[:, width:]
    keep = jnp.where(core == 0, low, high)
    come = sibling(jnp.where(core == 0, high, low))
    even = jnp.where(core == 0, keep, come).reshape(STEPS, chips, 1, width)
    odd = jnp.where(core == 0, come, keep).reshape(STEPS, chips, 1, width)
    layer_out = jnp.concatenate([even, odd], axis=2).reshape(STEPS, holders, width)
    return (attended.reshape(STEPS, 1, HQ * HD), layer_out)


def solution(mesh):
    placed = (
        P(None, "seq", "head"),
        P(None, "seq", "head"),
        P(None, "head", None),
        P(None, "head"),
        P(None, "seq", "head"),
        P(None, "seq", "head"),
        P(None, "seq", "head"),
        P(None, None, "seq"),
        P("seq"),
        P("head", "seq"),
        P("seq", "head"),
        P("seq", "head"),
        P(("head", "seq"), None),
    )
    return jax.shard_map(
        on_device,
        mesh=mesh,
        in_specs=placed,
        out_specs=(P(None, "seq", "head"), P(None, None, "seq")),
        check_vma=False,
    )
```

time: 143 us -> 123 us (0.86)
  local copies, waits for them, and re-layouts: 13 us -> 5.98 us
  Pallas kernels: 27.9 us -> 21.8 us
  starting transfers between devices: 37.6 us -> 34.9 us
  waiting for transfers between devices: 46.6 us -> 43.9 us
    all_to_all x1 -> x0, waiting for transfers between devices: 10.3 us -> none  [on_device(): lax.all_to_all(partial, 'seq', split_axis=0, concat_axis=0, tiled=True)]
    all_to_all x3 -> x4, waiting for transfers between devices: 26.3 us -> 35.5 us  [over_chips(): lax.all_to_all(x, 'seq', split_axis=0, concat_axis=0, tiled=True, axis_in...]
    pallas_call x3 -> x4, Pallas kernels: 25.4 us -> 19.4 us  [the longest x1 6.74 us: on_device(): pl.pallas_call(attend_kernel, in_specs=[smem, smem, vmem, hbm, hbm, pl.Bl...]
    unnamed x19 -> x24, local copies, waits for them, and re-layouts: 8.58 us -> 3.08 us
    all_to_all x1 -> x0, starting transfers between devices: 3.91 us -> none  [on_device(): lax.all_to_all(partial, 'seq', split_axis=0, concat_axis=0, tiled=True)]
    all_to_all x3 -> x4, starting transfers between devices: 15.6 us -> 18.7 us  [over_chips(): lax.all_to_all(x, 'seq', split_axis=0, concat_axis=0, tiled=True, axis_in...]
    ppermute x7, waiting for transfers between devices: 2.68 us -> 0.25 us  [sibling(): return lax.ppermute(x, 'seq', swap)]
    ppermute x6, starting transfers between devices: 9 us -> 6.67 us  [heads(): lax.ppermute(x, 'head', [(i, i ^ s) for i in range(4)])]
  transfers between devices with their start and end apart: 17 -> 17, of which waited for: 11 -> 9; matrix products, arithmetic and copies ran while one was open for 3% -> 2% of each run, Pallas kernels for 17% -> 11%
where the time goes in v2:
time: 123 us; the launch traced here: 122 us
  waiting for transfers between devices  43.9 us (36%)
  starting transfers between devices  34.9 us (28%)
  Pallas kernels  21.8 us (18%)
  blocking collectives  13.9 us (11%)
  local copies, waits for them, and re-layouts  5.98 us (5%)
    all_to_all x4, waiting for transfers between devices, over_chips(): lax.all_to_all(x, 'seq', split_axis=0, concat_axis=0, tiled=True, axis_in...  35.5 us
    all_to_all x4, starting transfers between devices, over_chips(): lax.all_to_all(x, 'seq', split_axis=0, concat_axis=0, tiled=True, axis_in...  18.7 us
    all_to_all x1, blocking collectives, over_chips(): lax.all_to_all(x, 'seq', split_axis=0, concat_axis=0, tiled=True, axis_in...  13.9 us
    ppermute x7, starting transfers between devices, sibling(): return lax.ppermute(x, 'seq', swap)  9.55 us
    ppermute x6, waiting for transfers between devices, heads(): lax.ppermute(x, 'head', [(i, i ^ s) for i in range(4)])  8.18 us
    pallas_call x1, Pallas kernels, on_device(): pl.pallas_call(attend_kernel, in_specs=[smem, smem, vmem, hbm, hbm, pl.Bl...  6.74 us
    ppermute x6, starting transfers between devices, heads(): lax.ppermute(x, 'head', [(i, i ^ s) for i in range(4)])  6.67 us
    pallas_call x1, Pallas kernels, on_device(): pl.pallas_call(gather_kernel, in_specs=[smem, smem, vmem, hbm, hbm], out_...  5.6 us
  transfers between devices with their start and end apart: 17, of which 9 were waited for; matrix products, arithmetic and copies ran while one was open for 2% of the time, Pallas kernels for 11%

profile of v2, /device:TPU:1, one launch (start us, length us, event | category | flops | bytes accessed | tf_op | source)
XLA Modules:
  0.0 121.8 jit_solution(16805619991644810786)
XLA Ops:
  0.7 0.8 copy-done.4
  1.5 0.7 copy-done.5
  2.2 5.6 %gather.1 = (bf16[16,512,256]{2,1,0:T(8,128)(2,1)}, s32[32]{0:T(128)S(1)}) custom-call(s32[2]{0:T(128)S(1)} %pad_add_fusion.where_ref, s32[2,32]{1,0:T(2,128)S(1)} %bitcast.13, s32[32,2,128]{2,1,0:T(2,128)S(1)} %copy-done.4, bf16[32,512,256]{2,1,0:T(8,128)(2,1)} %k_ref.3, bf16[32,512,256]{2,1,0:T(8,128)(2,1)} %v_ref.3), custom_call_target="tpu_custom_call" | custom-call | tf_op jit(solution)/shard_map/gather/pallas_call | solution.py:375
  7.8 1.5 %collective-permute-start = (bf16[16,512,256]{2,1,0:T(8,128)(2,1)}, bf16[16,512,256]{2,1,0:T(8,128)(2,1)}, u32[]{:S(2)}, u32[]{:S(2)}) collective-permute-start(bf16[16,512,256]{2,1,0:T(8,128)(2,1)} %get-tuple-element.13), channel_id=1, source_target_pairs={{0,4},{4,0},{8,12},{12,8},{16,20},{20,16},{24,28},{28,24},{32,36},... | collective-permute-start | bytes 12582920 | tf_op jit(solution)/shard_map/ppermute | solution.py:354
  9.3 0.7 broadcast_in_dim.11
  10.0 7.7 %all-to-all-start = ((bf16[16,48,128]{2,1,0:T(8,128)(2,1)}), bf16[16,48,128]{2,1,0:T(8,128)(2,1)S(1)}, u32[]{:S(2)}, u32[]{:S(2)}) async-start(bf16[16,48,128]{2,1,0:T(8,128)(2,1)} %broadcast_in_dim.11), calls=%async_computation | async-start | bytes 393216 | tf_op jit(solution)/shard_map/all_to_all | solution.py:346
  17.9 7.6 %all-to-all-done.q_ref = bf16[16,48,128]{2,1,0:T(8,128)(2,1)S(1)} async-done(((bf16[16,48,128]{2,1,0:T(8,128)(2,1)}), bf16[16,48,128]{2,1,0:T(8,128)(2,1)S(1)}, u32[]{:S(2)}, u32[]{:S(2)}) %all-to-all-start) | async-done | bytes 196640 | tf_op jit(solution)/shard_map/all_to_all | solution.py:346
  25.5 1.2 collective-permute-start.6
  27.8 6.7 %attend.1 = bf16[16,64,128]{2,1,0:T(8,128)(2,1)} custom-call(s32[2]{0:T(128)S(1)} %pad_add_fusion.where_ref, s32[32]{0:T(128)S(1)} %get-tuple-element.12.codes_ref, bf16[16,48,128]{2,1,0:T(8,128)(2,1)S(1)} %all-to-all-done.q_ref, bf16[32,512,256]{2,1,0:T(8,128)(2,1)} %k_ref.3, bf16[32,512,256]{2,1,0:T(8,128)(2,1)} %v_ref.3, ...), custom_call_target="tpu_custom_call" | custom-call | tf_op jit(solution)/shard_map/attend/pallas_call | solution.py:392
  34.6 3.5 %all-to-all-start.1 = ((bf16[16,64,128]{2,1,0:T(8,128)(2,1)}), bf16[16,64,128]{2,1,0:T(8,128)(2,1)S(1)}, u32[]{:S(2)}, u32[]{:S(2)}) async-start(bf16[16,64,128]{2,1,0:T(8,128)(2,1)} %attend.1), calls=%async_computation.1 | async-start | bytes 524288 | tf_op jit(solution)/shard_map/all_to_all | solution.py:346
  38.2 8.6 %all-to-all-done.1.got_ref = bf16[16,64,128]{2,1,0:T(8,128)(2,1)S(1)} async-done(((bf16[16,64,128]{2,1,0:T(8,128)(2,1)}), bf16[16,64,128]{2,1,0:T(8,128)(2,1)S(1)}, u32[]{:S(2)}, u32[]{:S(2)}) %all-to-all-start.1) | async-done | bytes 262176 | tf_op jit(solution)/shard_map/all_to_all | solution.py:346
  46.8 0.6 combine.1
  47.4 0.7 broadcast_in_dim.12
  48.1 3.5 %all-to-all-start.2 = ((bf16[16,48,128]{2,1,0:T(8,128)(2,1)}), bf16[16,48,128]{2,1,0:T(8,128)(2,1)S(1)}, u32[]{:S(2)}, u32[]{:S(2)}) async-start(bf16[16,48,128]{2,1,0:T(8,128)(2,1)} %broadcast_in_dim.12), calls=%async_computation.2 | async-start | bytes 393216 | tf_op jit(solution)/shard_map/all_to_all | solution.py:346
  51.7 7.1 %all-to-all-done.2.got_ref = bf16[16,48,128]{2,1,0:T(8,128)(2,1)S(1)} async-done(((bf16[16,48,128]{2,1,0:T(8,128)(2,1)}), bf16[16,48,128]{2,1,0:T(8,128)(2,1)S(1)}, u32[]{:S(2)}, u32[]{:S(2)}) %all-to-all-start.2) | async-done | bytes 196640 | tf_op jit(solution)/shard_map/all_to_all | solution.py:346
  58.8 1.8 %project.1.p0 = f32[48,512]{1,0:T(8,128)S(1)} custom-call(s32[2]{0:T(128)S(1)} %pad_add_fusion.where_ref, bf16[16,48,128]{2,1,0:T(8,128)(2,1)S(1)} %all-to-all-done.2.got_ref, bf16[2048,256]{1,0:T(8,128)(2,1)S(1)} %copy-done.3, bf16[2048,256]{1,0:T(8,128)(2,1)} %collective-permute-done.1.sib_ref), custom_call_target="tpu_custom_call" | custom-call | tf_op jit(solution)/shard_map/project/pallas_call | solution.py:430
  60.6 1.0 collective-permute-start.2
  61.6 2.7 %collective-permute-start.3 = (f32[48,512]{1,0:T(8,128)S(1)}, f32[48,512]{1,0:T(8,128)S(1)}, u32[]{:S(2)}, u32[]{:S(2)}) collective-permute-start(f32[48,512]{1,0:T(8,128)S(1)} %project.1.p0), channel_id=1, source_target_pairs={{0,2},{1,3},{2,0},{3,1},{4,6},{5,7},{6,4},{7,5},{8,10},{9,11},{10,... | collective-permute-start | bytes 294920 | tf_op jit(solution)/shard_map/ppermute | solution.py:357
  64.6 2.9 %collective-permute-done.3.p2 = f32[48,512]{1,0:T(8,128)S(1)} collective-permute-done((f32[48,512]{1,0:T(8,128)S(1)}, f32[48,512]{1,0:T(8,128)S(1)}, u32[]{:S(2)}, u32[]{:S(2)}) %collective-permute-start.3) | collective-permute-done | bytes 98336 | tf_op jit(solution)/shard_map/ppermute | solution.py:357
  67.4 1.9 %collective-permute-done.4.p3 = f32[48,512]{1,0:T(8,128)S(1)} collective-permute-done((f32[48,512]{1,0:T(8,128)S(1)}, f32[48,512]{1,0:T(8,128)S(1)}, u32[]{:S(2)}, u32[]{:S(2)}) %collective-permute-start.4) | collective-permute-done | bytes 98336 | tf_op jit(solution)/shard_map/ppermute | solution.py:357
  69.4 4.5 %gate_up.1 = (bf16[16,208,128]{2,1,0:T(8,128)(2,1)}, f32[48,512]{1,0:T(8,128)S(1)}) custom-call(s32[2]{0:T(128)S(1)} %pad_add_fusion.where_ref, f32[48,512]{1,0:T(8,128)S(1)} %project.1.p0, f32[48,512]{1,0:T(8,128)S(1)} %collective-permute-done.2.p1, f32[48,512]{1,0:T(8,128)S(1)} %collective-permute-done.3.p2, f32[48,512]{1,0:T(8,128)S(1)} %collective-permute-done.4.p3, ...), custom_call_target="tpu_custom_call" | custom-call | tf_op jit(solution)/shard_map/gate_up/pallas_call | solution.py:441
  73.9 4.0 %all-to-all-start.3 = ((bf16[16,208,128]{2,1,0:T(8,128)(2,1)}), bf16[16,208,128]{2,1,0:T(8,128)(2,1)S(1)}, u32[]{:S(2)}, u32[]{:S(2)}) async-start(bf16[16,208,128]{2,1,0:T(8,128)(2,1)} %get-tuple-element.20), calls=%async_computation.3 | async-start | bytes 1703936 | tf_op jit(solution)/shard_map/all_to_all | solution.py:346
  77.9 12.2 %all-to-all-done.3.got_ref = bf16[16,208,128]{2,1,0:T(8,128)(2,1)S(1)} async-done(((bf16[16,208,128]{2,1,0:T(8,128)(2,1)}), bf16[16,208,128]{2,1,0:T(8,128)(2,1)S(1)}, u32[]{:S(2)}, u32[]{:S(2)}) %all-to-all-start.3) | async-done | bytes 852000 | tf_op jit(solution)/shard_map/all_to_all | solution.py:346
  90.1 1.6 %copy-done.2 = bf16[128,8192]{1,0:T(8,128)(2,1)S(1)} copy-done((bf16[128,8192]{1,0:T(8,128)(2,1)S(1)}, bf16[128,8192]{1,0:T(8,128)(2,1)}, u32[]{:S(2)}) %copy-start.2) | copy-done | bytes 2097176
  91.7 2.5 %down.1 = bf16[16,48,512]{2,1,0:T(8,128)(2,1)S(1)} custom-call(s32[2]{0:T(128)S(1)} %pad_add_fusion.where_ref, bf16[16,208,128]{2,1,0:T(8,128)(2,1)S(1)} %all-to-all-done.3.got_ref, bf16[128,8192]{1,0:T(8,128)(2,1)S(1)} %copy-done.2, bf16[128,8192]{1,0:T(8,128)(2,1)} %collective-permute-done.8.sib_ref), custom_call_target="tpu_custom_call" | custom-call | tf_op jit(solution)/shard_map/down/pallas_call | solution.py:454
  94.2 13.9 %all_to_all.25 = bf16[16,48,512]{2,1,0:T(8,128)(2,1)S(1)} all-to-all(bf16[16,48,512]{2,1,0:T(8,128)(2,1)S(1)} %down.1), channel_id=1, replica_groups={{0,8,16,24,32,40,48,56,64,72,80,88,96,104,112,120},{4,12,20,28,36,44,52..., dimensions={0} | all-to-all | bytes 1572864 | tf_op jit(solution)/shard_map/all_to_all | solution.py:346
  108.3 1.3 %collective-permute-start.10 = (f32[48,512]{1,0:T(8,128)S(1)}, f32[48,512]{1,0:T(8,128)S(1)}, u32[]{:S(2)}, u32[]{:S(2)}) collective-permute-start(f32[48,512]{1,0:T(8,128)S(1)} %convert_reduce_fusion), channel_id=1, source_target_pairs={{0,2},{1,3},{2,0},{3,1},{4,6},{5,7},{6,4},{7,5},{8,10},{9,11},{10,... | collective-permute-start | bytes 294920 | tf_op jit(solution)/shard_map/ppermute | solution.py:357
  109.6 1.4 %collective-permute-start.9 = (f32[48,512]{1,0:T(8,128)S(1)}, f32[48,512]{1,0:T(8,128)S(1)}, u32[]{:S(2)}, u32[]{:S(2)}) collective-permute-start(f32[48,512]{1,0:T(8,128)S(1)} %convert_reduce_fusion), channel_id=1, source_target_pairs={{0,1},{1,0},{2,3},{3,2},{4,5},{5,4},{6,7},{7,6},{8,9},{9,8},{10,11... | collective-permute-start | bytes 294920 | tf_op jit(solution)/shard_map/ppermute | solution.py:357
  111.0 2.3 %collective-permute-done.10 = f32[48,512]{1,0:T(8,128)S(1)} collective-permute-done((f32[48,512]{1,0:T(8,128)S(1)}, f32[48,512]{1,0:T(8,128)S(1)}, u32[]{:S(2)}, u32[]{:S(2)}) %collective-permute-start.10) | collective-permute-done | bytes 98336 | tf_op jit(solution)/shard_map/ppermute | solution.py:357
  113.3 1.0 collective-permute-done.11
  114.4 5.8 %collective-permute-start.12 = (bf16[48,256]{1,0:T(8,128)(2,1)S(1)}, bf16[48,256]{1,0:T(8,128)(2,1)S(1)}, u32[]{:S(2)}, u32[]{:S(2)}) collective-permute-start(bf16[48,256]{1,0:T(8,128)(2,1)S(1)} %broadcast_select_fusion.2), channel_id=1, source_target_pairs={{0,4},{4,0},{8,12},{12,8},{16,20},{20,16},{24,28},{28,24},{32,36},... | collective-permute-start | bytes 73736 | tf_op jit(solution)/shard_map/ppermute | solution.py:354
  121.2 0.6 reshape.45
  (55 shorter events, 2.7 us)
Async XLA Ops:
  0.7 0.8 copy-start.4
  1.5 0.7 copy-start.5
  2.2 7.2 %copy-start.7 = (bf16[3,1,2048]{2,0,1:T(4,128)(2,1)S(1)}, bf16[3,1,2048]{2,0,1:T(4,128)(2,1)}, u32[]{:S(2)}) copy-start(bf16[3,1,2048]{2,0,1:T(4,128)(2,1)} %param.17) | copy-start | bytes 36868
  2.2 15.6 %copy-start.6 = (bf16[3,32,256]{2,1,0:T(8,128)(2,1)S(1)}, bf16[3,32,256]{2,1,0:T(8,128)(2,1)}, u32[]{:S(2)}) copy-start(bf16[3,32,256]{2,1,0:T(8,128)(2,1)} %param.20) | copy-start | bytes 147460
  2.2 23.4 %copy-start = (bf16[256,4096]{1,0:T(8,128)(2,1)S(1)}, bf16[256,4096]{1,0:T(8,128)(2,1)}, u32[]{:S(2)}) copy-start(bf16[256,4096]{1,0:T(8,128)(2,1)} %g_own.1) | copy-start | bytes 6291460
  2.2 25.0 %copy-start.3 = (bf16[2048,256]{1,0:T(8,128)(2,1)S(1)}, bf16[2048,256]{1,0:T(8,128)(2,1)}, u32[]{:S(2)}) copy-start(bf16[2048,256]{1,0:T(8,128)(2,1)} %own_ref.2) | copy-start | bytes 3145732
  2.2 25.0 %copy-start.8 = (bf16[256]{0:T(256)(128)(2,1)S(1)}, bf16[256]{0:T(256)(128)(2,1)}, u32[]{:S(2)}) copy-start(bf16[256]{0:T(256)(128)(2,1)} %param.21) | copy-start | bytes 1540
  2.2 25.6 %copy-start.9 = (bf16[3,1,256]{2,0,1:T(4,128)(2,1)S(1)}, bf16[3,1,256]{2,0,1:T(4,128)(2,1)}, u32[]{:S(2)}) copy-start(bf16[3,1,256]{2,0,1:T(4,128)(2,1)} %param.18) | copy-start | bytes 4612
  2.2 25.6 %copy-start.10 = (bf16[3,1,256]{2,0,1:T(4,128)(2,1)S(1)}, bf16[3,1,256]{2,0,1:T(4,128)(2,1)}, u32[]{:S(2)}) copy-start(bf16[3,1,256]{2,0,1:T(4,128)(2,1)} %param.19) | copy-start | bytes 4612
  7.8 19.4 %collective-permute-start = (bf16[16,512,256]{2,1,0:T(8,128)(2,1)}, bf16[16,512,256]{2,1,0:T(8,128)(2,1)}, u32[]{:S(2)}, u32[]{:S(2)}) collective-permute-start(bf16[16,512,256]{2,1,0:T(8,128)(2,1)} %get-tuple-element.13), channel_id=1, source_target_pairs={{0,4},{4,0},{8,12},{12,8},{16,20},{20,16},{24,28},{28,24},{32,36},... | collective-permute-start | bytes 12582920 | tf_op jit(solution)/shard_map/ppermute | solution.py:354
  10.0 15.5 %all-to-all-start = ((bf16[16,48,128]{2,1,0:T(8,128)(2,1)}), bf16[16,48,128]{2,1,0:T(8,128)(2,1)S(1)}, u32[]{:S(2)}, u32[]{:S(2)}) async-start(bf16[16,48,128]{2,1,0:T(8,128)(2,1)} %broadcast_in_dim.11), calls=%async_computation | async-start | bytes 393216 | tf_op jit(solution)/shard_map/all_to_all | solution.py:346
  25.5 38.9 %collective-permute-start.6 = (bf16[256,4096]{1,0:T(8,128)(2,1)S(1)}, bf16[256,4096]{1,0:T(8,128)(2,1)}, u32[]{:S(2)}, u32[]{:S(2)}) collective-permute-start(bf16[256,4096]{1,0:T(8,128)(2,1)S(1)} %copy-done), channel_id=1, source_target_pairs={{0,4},{4,0},{8,12},{12,8},{16,20},{20,16},{24,28},{28,24},{32,36},... | collective-permute-start | bytes 6291464 | tf_op jit(solution)/shard_map/ppermute | solution.py:354
  26.7 37.9 %collective-permute-start.7 = (bf16[256,4096]{1,0:T(8,128)(2,1)}, bf16[256,4096]{1,0:T(8,128)(2,1)}, u32[]{:S(2)}, u32[]{:S(2)}) collective-permute-start(bf16[256,4096]{1,0:T(8,128)(2,1)} %u_own.1), channel_id=1, source_target_pairs={{0,4},{4,0},{8,12},{12,8},{16,20},{20,16},{24,28},{28,24},{32,36},... | collective-permute-start | bytes 6291464 | tf_op jit(solution)/shard_map/ppermute | solution.py:354
  26.7 51.2 %collective-permute-start.8 = (bf16[128,8192]{1,0:T(8,128)(2,1)}, bf16[128,8192]{1,0:T(8,128)(2,1)}, u32[]{:S(2)}, u32[]{:S(2)}) collective-permute-start(bf16[128,8192]{1,0:T(8,128)(2,1)} %own_ref.3), channel_id=1, source_target_pairs={{0,4},{4,0},{8,12},{12,8},{16,20},{20,16},{24,28},{28,24},{32,36},... | collective-permute-start | bytes 6291464 | tf_op jit(solution)/shard_map/ppermute | solution.py:354
  27.2 24.5 %collective-permute-start.1 = (bf16[2048,256]{1,0:T(8,128)(2,1)S(1)}, bf16[2048,256]{1,0:T(8,128)(2,1)}, u32[]{:S(2)}, u32[]{:S(2)}) collective-permute-start(bf16[2048,256]{1,0:T(8,128)(2,1)S(1)} %copy-done.3), channel_id=1, source_target_pairs={{0,4},{4,0},{8,12},{12,8},{16,20},{20,16},{24,28},{28,24},{32,36},... | collective-permute-start | bytes 3145736 | tf_op jit(solution)/shard_map/ppermute | solution.py:354
  27.2 10.9 %collective-permute-start.5 = (bf16[64,256]{1,0:T(8,128)(2,1)S(1)}, bf16[64,256]{1,0:T(8,128)(2,1)S(1)}, u32[]{:S(2)}, u32[]{:S(2)}) collective-permute-start(bf16[64,256]{1,0:T(8,128)(2,1)S(1)} %pad_maximum_fusion.2), channel_id=1, source_target_pairs={{0,4},{4,0},{8,12},{12,8},{16,20},{20,16},{24,28},{28,24},{32,36},... | collective-permute-start | bytes 98312 | tf_op jit(solution)/shard_map/ppermute | solution.py:354
  34.6 12.2 %all-to-all-start.1 = ((bf16[16,64,128]{2,1,0:T(8,128)(2,1)}), bf16[16,64,128]{2,1,0:T(8,128)(2,1)S(1)}, u32[]{:S(2)}, u32[]{:S(2)}) async-start(bf16[16,64,128]{2,1,0:T(8,128)(2,1)} %attend.1), calls=%async_computation.1 | async-start | bytes 524288 | tf_op jit(solution)/shard_map/all_to_all | solution.py:346
  48.1 10.7 %all-to-all-start.2 = ((bf16[16,48,128]{2,1,0:T(8,128)(2,1)}), bf16[16,48,128]{2,1,0:T(8,128)(2,1)S(1)}, u32[]{:S(2)}, u32[]{:S(2)}) async-start(bf16[16,48,128]{2,1,0:T(8,128)(2,1)} %broadcast_in_dim.12), calls=%async_computation.2 | async-start | bytes 393216 | tf_op jit(solution)/shard_map/all_to_all | solution.py:346
  58.8 10.6 %copy-start.1 = (bf16[256,4096]{1,0:T(8,128)(2,1)S(1)}, bf16[256,4096]{1,0:T(8,128)(2,1)}, u32[]{:S(2)}) copy-start(bf16[256,4096]{1,0:T(8,128)(2,1)} %u_own.1) | copy-start | bytes 6291460
  60.6 4.0 %collective-permute-start.2 = (f32[48,512]{1,0:T(8,128)S(1)}, f32[48,512]{1,0:T(8,128)S(1)}, u32[]{:S(2)}, u32[]{:S(2)}) collective-permute-start(f32[48,512]{1,0:T(8,128)S(1)} %project.1.p0), channel_id=1, source_target_pairs={{0,1},{1,0},{2,3},{3,2},{4,5},{5,4},{6,7},{7,6},{8,9},{9,8},{10,11... | collective-permute-start | bytes 294920 | tf_op jit(solution)/shard_map/ppermute | solution.py:357
  61.6 5.8 %collective-permute-start.3 = (f32[48,512]{1,0:T(8,128)S(1)}, f32[48,512]{1,0:T(8,128)S(1)}, u32[]{:S(2)}, u32[]{:S(2)}) collective-permute-start(f32[48,512]{1,0:T(8,128)S(1)} %project.1.p0), channel_id=1, source_target_pairs={{0,2},{1,3},{2,0},{3,1},{4,6},{5,7},{6,4},{7,5},{8,10},{9,11},{10,... | collective-permute-start | bytes 294920 | tf_op jit(solution)/shard_map/ppermute | solution.py:357
  64.4 5.0 %collective-permute-start.4 = (f32[48,512]{1,0:T(8,128)S(1)}, f32[48,512]{1,0:T(8,128)S(1)}, u32[]{:S(2)}, u32[]{:S(2)}) collective-permute-start(f32[48,512]{1,0:T(8,128)S(1)} %project.1.p0), channel_id=1, source_target_pairs={{0,3},{1,2},{2,1},{3,0},{4,7},{5,6},{6,5},{7,4},{8,11},{9,10},{10,... | collective-permute-start | bytes 294920 | tf_op jit(solution)/shard_map/ppermute | solution.py:357
  73.9 16.2 %all-to-all-start.3 = ((bf16[16,208,128]{2,1,0:T(8,128)(2,1)}), bf16[16,208,128]{2,1,0:T(8,128)(2,1)S(1)}, u32[]{:S(2)}, u32[]{:S(2)}) async-start(bf16[16,208,128]{2,1,0:T(8,128)(2,1)} %get-tuple-element.20), calls=%async_computation.3 | async-start | bytes 1703936 | tf_op jit(solution)/shard_map/all_to_all | solution.py:346
  90.1 1.6 %copy-start.2 = (bf16[128,8192]{1,0:T(8,128)(2,1)S(1)}, bf16[128,8192]{1,0:T(8,128)(2,1)}, u32[]{:S(2)}) copy-start(bf16[128,8192]{1,0:T(8,128)(2,1)} %own_ref.3) | copy-start | bytes 6291460
  108.3 5.1 %collective-permute-start.10 = (f32[48,512]{1,0:T(8,128)S(1)}, f32[48,512]{1,0:T(8,128)S(1)}, u32[]{:S(2)}, u32[]{:S(2)}) collective-permute-start(f32[48,512]{1,0:T(8,128)S(1)} %convert_reduce_fusion), channel_id=1, source_target_pairs={{0,2},{1,3},{2,0},{3,1},{4,6},{5,7},{6,4},{7,5},{8,10},{9,11},{10,... | collective-permute-start | bytes 294920 | tf_op jit(solution)/shard_map/ppermute | solution.py:357
  109.5 4.8 %collective-permute-start.11 = (f32[48,512]{1,0:T(8,128)S(1)}, f32[48,512]{1,0:T(8,128)S(1)}, u32[]{:S(2)}, u32[]{:S(2)}) collective-permute-start(f32[48,512]{1,0:T(8,128)S(1)} %convert_reduce_fusion), channel_id=1, source_target_pairs={{0,3},{1,2},{2,1},{3,0},{4,7},{5,6},{6,5},{7,4},{8,11},{9,10},{10,... | collective-permute-start | bytes 294920 | tf_op jit(solution)/shard_map/ppermute | solution.py:357
  109.6 4.8 %collective-permute-start.9 = (f32[48,512]{1,0:T(8,128)S(1)}, f32[48,512]{1,0:T(8,128)S(1)}, u32[]{:S(2)}, u32[]{:S(2)}) collective-permute-start(f32[48,512]{1,0:T(8,128)S(1)} %convert_reduce_fusion), channel_id=1, source_target_pairs={{0,1},{1,0},{2,3},{3,2},{4,5},{5,4},{6,7},{7,6},{8,9},{9,8},{10,11... | collective-permute-start | bytes 294920 | tf_op jit(solution)/shard_map/ppermute | solution.py:357
  114.4 6.7 %collective-permute-start.12 = (bf16[48,256]{1,0:T(8,128)(2,1)S(1)}, bf16[48,256]{1,0:T(8,128)(2,1)S(1)}, u32[]{:S(2)}, u32[]{:S(2)}) collective-permute-start(bf16[48,256]{1,0:T(8,128)(2,1)S(1)} %broadcast_select_fusion.2), channel_id=1, source_target_pairs={{0,4},{4,0},{8,12},{12,8},{16,20},{20,16},{24,28},{28,24},{32,36},... | collective-permute-start | bytes 73736 | tf_op jit(solution)/shard_map/ppermute | solution.py:354

commit v3 on v2

--- a/solution.py
+++ b/solution.py
@@ -63,9 +63,14 @@
 
 
 def gather_kernel(
-    where_ref, count_ref, lists_ref, k_ref, v_ref, out_ref, codes_ref,
-    wide_ref, scalar_ref, packed_ref, list_sem, in_sems, out_sems,
+    where_ref, count_ref, lists_ref, q_ref, k_ref, v_ref, out_ref, q_out, codes_ref,
+    wide_ref, scalar_ref, packed_ref, list_sem, q_sems, in_sems, out_sems,
 ):
+    spread = [
+        pltpu.make_async_copy(q_ref, q_out.at[i], q_sems.at[i]) for i in range(q_out.shape[0])
+    ]
+    for copy in spread:
+        copy.start()
     core = where_ref[1]
     per_dev = k_ref.shape[1] // BLK
     base = where_ref[0] * per_dev
@@ -113,7 +118,7 @@
         pltpu.make_async_copy(packed_ref.at[at], packed_ref.at[at], in_sems.at[g]).wait()
         leaving.append(pltpu.make_async_copy(packed_ref.at[at], out_ref.at[at], out_sems.at[g]))
         leaving[-1].start()
-    for copy in leaving:
+    for copy in leaving + spread:
         copy.wait()
 
 
@@ -243,9 +248,37 @@
 
 
 def gate_up_kernel(
-    where_ref, p0, p1, p2, p3, res_ref, gain_ref, g_own, g_sib, u_own, u_sib, out_ref, stream_ref
+    where_ref, p0, p1, p2, p3, res_ref, gain_ref, g_own_hbm, u_own_hbm, g_sib_hbm, u_sib_hbm,
+    d_own_hbm, d_sib_hbm, out_ref, stream_ref, d_own_ref, d_sib_ref, g_own, u_own, g_sib, u_sib,
+    part_sems, whole_sems,
 ):
     core = where_ref[1]
+    parts = part_sems.shape[1]
+    columns = g_own.shape[1] // parts
+    brought = []
+    for part in range(parts):
+        at = (slice(None), pl.ds(part * columns, columns))
+        brought.append(
+            [
+                pltpu.make_async_copy(source.at[at], target.at[at], part_sems.at[n, part])
+                for n, (source, target) in enumerate(
+                    (
+                        (g_own_hbm, g_own),
+                        (g_sib_hbm, g_sib),
+                        (u_own_hbm, u_own),
+                        (u_sib_hbm, u_sib),
+                    )
+                )
+            ]
+        )
+        for copy in brought[-1]:
+            copy.start()
+    later = [
+        pltpu.make_async_copy(source, target, whole_sems.at[n])
+        for n, (source, target) in enumerate(((d_own_hbm, d_own_ref), (d_sib_hbm, d_sib_ref)))
+    ]
+    for copy in later:
+        copy.start()
     half = g_own.shape[0]
     chips = out_ref.shape[0]
     stream = res_ref[...].astype(f32) + ((p0[...] + p1[...]) + (p2[...] + p3[...]))
@@ -276,6 +309,9 @@
 
     ready = None
     for k in range(chips):
+        if k % (chips // parts) == 0:
+            for copy in brought[k // (chips // parts)]:
+                copy.wait()
         at = slice(k * wide, (k + 1) * wide)
         gate = dot(mine, g_own[:, at]) + dot(other, g_sib[:, at])
         up = dot(mine, u_own[:, at]) + dot(other, u_sib[:, at])
@@ -283,6 +319,8 @@
             store(*ready)
         ready = k, gate.astype(bf16), up.astype(bf16)
     store(*ready)
+    for copy in later:
+        copy.wait()
 
 
 def down_kernel(where_ref, got_ref, own_ref, sib_ref, out_ref):
@@ -347,9 +385,6 @@
             x, "seq", split_axis=0, concat_axis=0, tiled=True, axis_index_groups=same_core
         )
 
-    def to_all_chips(x):
-        return over_chips(jnp.broadcast_to(x[None], (chips,) + x.shape))
-
     def sibling(x):
         return lax.ppermute(x, "seq", swap)
 
@@ -366,28 +401,33 @@
         return jnp.concatenate([low, high], axis=1)
 
     q_rows = queries.reshape(ROWS, HD)
-    q_own = to_all_chips(q_rows)
 
     half = CAP * BLK
     tile = (chips, 2 * half, KV * HD)
     groups = 4
     dma = pltpu.SemaphoreType.DMA
-    to_sib, codes = pl.pallas_call(
+    to_sib, q_copies, codes = pl.pallas_call(
         gather_kernel,
-        in_specs=[smem, smem, vmem, hbm, hbm],
-        out_specs=[hbm, smem],
-        out_shape=[jax.ShapeDtypeStruct(tile, bf16), jax.ShapeDtypeStruct((chips * KV,), jnp.int32)],
+        in_specs=[smem, smem, vmem, vmem, hbm, hbm],
+        out_specs=[hbm, hbm, smem],
+        out_shape=[
+            jax.ShapeDtypeStruct(tile, bf16),
+            jax.ShapeDtypeStruct((chips, ROWS, HD), bf16),
+            jax.ShapeDtypeStruct((chips * KV,), jnp.int32),
+        ],
         scratch_shapes=[
             pltpu.VMEM((1, list_length), jnp.int32),
             pltpu.SMEM((1, list_length), jnp.int32),
             pltpu.VMEM(tile, bf16),
             dma,
+            dma((chips,)),
             dma((groups,)),
             dma((groups,)),
         ],
         compiler_params=pltpu.CompilerParams(vmem_limit_bytes=50 * MIB),
         name="gather",
-    )(where, keep_count.T, keep_blocks, keys_cache, values_cache)
+    )(where, keep_count.T, keep_blocks, q_rows, keys_cache, values_cache)
+    q_own = over_chips(q_copies)
     sib_packed = sibling(to_sib)
     partial = pl.pallas_call(
         attend_kernel,
@@ -399,9 +439,8 @@
         name="attend",
     )(where, codes, q_own, keys_cache, values_cache, sib_packed)
 
-    (w_out_s, w_gate_s, w_up_s, w_down_s, res_s, gain_s), _ = lax.optimization_barrier(
-        ((w_out, w_gate, w_up, w_down, parity(residual_in, 1 - core), norm_gain), q_own)
-    )
+    w_out_s, w_gate_s, w_up_s, w_down_s = w_out, w_gate, w_up, w_down
+    res_s, gain_s = parity(residual_in, 1 - core), norm_gain
     w_out_sib = sibling(w_out_s)
     w_gate_sib = sibling(w_gate_s)
     w_up_sib = sibling(w_up_s)
@@ -426,7 +465,7 @@
         jnp.pad(new_values.reshape(STEPS, KV * HD), pad),
     )
 
-    all_attended = to_all_chips(attended)
+    all_attended = over_chips(jnp.broadcast_to(attended[None], (chips, ROWS, HD)))
     projected = pl.pallas_call(
         project_kernel,
         in_specs=[smem, vmem, vmem, vmem],
@@ -438,17 +477,20 @@
     )(where, all_attended, w_out, w_out_sib)
     parts = heads(projected)
 
-    shares, stream = pl.pallas_call(
+    shares, stream, w_down_own, w_down_sib = pl.pallas_call(
         gate_up_kernel,
-        in_specs=[smem] + [vmem] * 10,
-        out_specs=[vmem, vmem],
+        in_specs=[smem] + [vmem] * 6 + [hbm] * 6,
+        out_specs=[vmem] * 4,
         out_shape=[
             jax.ShapeDtypeStruct((chips, 4 * tokens + 16, HD), bf16),
             jax.ShapeDtypeStruct((tokens, 2 * width), f32),
+            jax.ShapeDtypeStruct(w_down.shape, bf16),
+            jax.ShapeDtypeStruct(w_down.shape, bf16),
         ],
+        scratch_shapes=[pltpu.VMEM(w_gate.shape, bf16)] * 4 + [dma((4, 4)), dma((2,))],
         compiler_params=params,
         name="gate_up",
-    )(where, *parts, res, gain, w_gate, w_gate_sib, w_up, w_up_sib)
+    )(where, *parts, res, gain, w_gate, w_up, w_gate_sib, w_up_sib, w_down, w_down_sib)
 
     got_shares = over_chips(shares)
     down = pl.pallas_call(
@@ -458,7 +500,7 @@
         out_shape=jax.ShapeDtypeStruct((chips, tokens, 2 * width), bf16),
         compiler_params=params,
         name="down",
-    )(where, got_shares, w_down, w_down_sib)
+    )(where, got_shares, w_down_own, w_down_sib)
 
     lowered = jnp.sum(over_chips(down).astype(f32), axis=0)
     l0, l1, l2, l3 = heads(lowered)

time: 123 us -> 118 us (0.959)
  waiting for transfers between devices: 43.9 us -> 28.3 us
  blocking collectives: 13.9 us -> 27 us
  starting transfers between devices: 34.9 us -> 32.6 us
  other arithmetic: 0.29 us -> 2.34 us
  local copies, waits for them, and re-layouts: 5.98 us -> 4.39 us
    all_to_all x4 -> x3, waiting for transfers between devices: 35.5 us -> 17.7 us  [over_chips(): lax.all_to_all(x, 'seq', split_axis=0, concat_axis=0, tiled=True, axis_in...]
    all_to_all x1 -> x2, blocking collectives: 13.9 us -> 27 us  [over_chips(): lax.all_to_all(x, 'seq', split_axis=0, concat_axis=0, tiled=True, axis_in...]
    all_to_all x4 -> x3, starting transfers between devices: 18.7 us -> 14.8 us  [over_chips(): lax.all_to_all(x, 'seq', split_axis=0, concat_axis=0, tiled=True, axis_in...]
    ppermute x7, waiting for transfers between devices: 0.25 us -> 2.26 us  [sibling(): return lax.ppermute(x, 'seq', swap)]
    unnamed x24 -> x18, local copies, waits for them, and re-layouts: 3.08 us -> 1.48 us
    ppermute x7, starting transfers between devices: 9.55 us -> 11 us  [sibling(): return lax.ppermute(x, 'seq', swap)]
    select_n x2, other arithmetic: 0.02 us -> 1.45 us  [in_order(): low = jnp.where(core == 0, own, sib)]
  transfers between devices with their start and end apart: 17 -> 16, of which waited for: 9 -> 9; matrix products, arithmetic and copies ran while one was open for 2% -> 3% of each run, Pallas kernels for 11% -> 8%
where the time goes in v3:
time: 118 us; the launch traced here: 117 us
  starting transfers between devices  32.6 us (28%)
  waiting for transfers between devices  28.3 us (24%)
  blocking collectives  27 us (23%)
  Pallas kernels  21.3 us (18%)
  local copies, waits for them, and re-layouts  4.39 us (4%)
  other arithmetic  2.34 us (2%)
    all_to_all x2, blocking collectives, over_chips(): lax.all_to_all(x, 'seq', split_axis=0, concat_axis=0, tiled=True, axis_in...  27 us
    all_to_all x3, waiting for transfers between devices, over_chips(): lax.all_to_all(x, 'seq', split_axis=0, concat_axis=0, tiled=True, axis_in...  17.7 us
    all_to_all x3, starting transfers between devices, over_chips(): lax.all_to_all(x, 'seq', split_axis=0, concat_axis=0, tiled=True, axis_in...  14.8 us
    ppermute x7, starting transfers between devices, sibling(): return lax.ppermute(x, 'seq', swap)  11 us
    ppermute x6, waiting for transfers between devices, heads(): lax.ppermute(x, 'head', [(i, i ^ s) for i in range(4)])  8.31 us
    ppermute x6, starting transfers between devices, heads(): lax.ppermute(x, 'head', [(i, i ^ s) for i in range(4)])  6.75 us
    pallas_call x1, Pallas kernels, on_device(): pl.pallas_call(attend_kernel, in_specs=[smem, smem, vmem, hbm, hbm, pl.Bl...  6.6 us
    pallas_call x1, Pallas kernels, on_device(): pl.pallas_call(gather_kernel, in_specs=[smem, smem, vmem, vmem, hbm, hbm]...  5.77 us
  transfers between devices with their start and end apart: 16, of which 9 were waited for; matrix products, arithmetic and copies ran while one was open for 3% of the time, Pallas kernels for 8%

profile of v3, /device:TPU:1, one launch (start us, length us, event | category | flops | bytes accessed | tf_op | source)
XLA Modules:
  0.0 116.9 jit_solution(18068071941761657408)
XLA Ops:
  0.6 0.7 reshape.37.q_ref
  1.5 0.8 copy-done.2
  2.2 0.7 copy-done.3
  2.9 5.8 %gather.1 = (bf16[16,512,256]{2,1,0:T(8,128)(2,1)}, bf16[16,48,128]{2,1,0:T(8,128)(2,1)}, s32[32]{0:T(128)S(1)}) custom-call(s32[2]{0:T(128)S(1)} %pad_add_fusion.where_ref, s32[2,32]{1,0:T(2,128)S(1)} %bitcast.13, s32[32,2,128]{2,1,0:T(2,128)S(1)} %copy-done.2, bf16[48,128]{1,0:T(8,128)(2,1)S(1)} %reshape.37.q_ref, bf16[32,512,256]{2,1,0:T(8,128)(2,1)} %k_ref.3, ...), custom_call_target="tpu_custom_call" | custom-call | tf_op jit(solution)/shard_map/gather/pallas_call | solution.py:409
  8.7 1.3 %collective-permute-start = (bf16[16,512,256]{2,1,0:T(8,128)(2,1)}, bf16[16,512,256]{2,1,0:T(8,128)(2,1)}, u32[]{:S(2)}, u32[]{:S(2)}) collective-permute-start(bf16[16,512,256]{2,1,0:T(8,128)(2,1)} %get-tuple-element.11), channel_id=1, source_target_pairs={{0,4},{4,0},{8,12},{12,8},{16,20},{20,16},{24,28},{28,24},{32,36},... | collective-permute-start | bytes 12582920 | tf_op jit(solution)/shard_map/ppermute | solution.py:389
  11.0 7.7 %all-to-all-start = ((bf16[16,48,128]{2,1,0:T(8,128)(2,1)}), bf16[16,48,128]{2,1,0:T(8,128)(2,1)S(1)}, u32[]{:S(2)}, u32[]{:S(2)}) async-start(bf16[16,48,128]{2,1,0:T(8,128)(2,1)} %get-tuple-element.10), calls=%async_computation | async-start | bytes 393216 | tf_op jit(solution)/shard_map/all_to_all | solution.py:384
  19.6 2.0 %collective-permute-done.sib_hbm = bf16[16,512,256]{2,1,0:T(8,128)(2,1)} collective-permute-done((bf16[16,512,256]{2,1,0:T(8,128)(2,1)}, bf16[16,512,256]{2,1,0:T(8,128)(2,1)}, u32[]{:S(2)}, u32[]{:S(2)}) %collective-permute-start) | collective-permute-done | bytes 4194336 | tf_op jit(solution)/shard_map/ppermute | solution.py:389
  22.0 4.5 %all-to-all-done.q_ref = bf16[16,48,128]{2,1,0:T(8,128)(2,1)S(1)} async-done(((bf16[16,48,128]{2,1,0:T(8,128)(2,1)}), bf16[16,48,128]{2,1,0:T(8,128)(2,1)S(1)}, u32[]{:S(2)}, u32[]{:S(2)}) %all-to-all-start) | async-done | bytes 196640 | tf_op jit(solution)/shard_map/all_to_all | solution.py:384
  26.5 6.6 %attend.1 = bf16[16,64,128]{2,1,0:T(8,128)(2,1)} custom-call(s32[2]{0:T(128)S(1)} %pad_add_fusion.where_ref, s32[32]{0:T(128)S(1)} %get-tuple-element.9.codes_ref, bf16[16,48,128]{2,1,0:T(8,128)(2,1)S(1)} %all-to-all-done.q_ref, bf16[32,512,256]{2,1,0:T(8,128)(2,1)} %k_ref.3, bf16[32,512,256]{2,1,0:T(8,128)(2,1)} %v_ref.3, ...), custom_call_target="tpu_custom_call" | custom-call | tf_op jit(solution)/shard_map/attend/pallas_call | solution.py:432
  33.1 3.5 %all-to-all-start.1 = ((bf16[16,64,128]{2,1,0:T(8,128)(2,1)}), bf16[16,64,128]{2,1,0:T(8,128)(2,1)S(1)}, u32[]{:S(2)}, u32[]{:S(2)}) async-start(bf16[16,64,128]{2,1,0:T(8,128)(2,1)} %attend.1), calls=%async_computation.1 | async-start | bytes 524288 | tf_op jit(solution)/shard_map/all_to_all | solution.py:384
  36.7 0.7 bitcast_select_fusion.1
  37.4 6.8 %all-to-all-done.1.got_ref = bf16[16,64,128]{2,1,0:T(8,128)(2,1)S(1)} async-done(((bf16[16,64,128]{2,1,0:T(8,128)(2,1)}), bf16[16,64,128]{2,1,0:T(8,128)(2,1)S(1)}, u32[]{:S(2)}, u32[]{:S(2)}) %all-to-all-start.1) | async-done | bytes 262176 | tf_op jit(solution)/shard_map/all_to_all | solution.py:384
  44.2 0.6 combine.1
  44.9 0.7 broadcast_in_dim.4
  45.6 3.5 %all-to-all-start.2 = ((bf16[16,48,128]{2,1,0:T(8,128)(2,1)}), bf16[16,48,128]{2,1,0:T(8,128)(2,1)S(1)}, u32[]{:S(2)}, u32[]{:S(2)}) async-start(bf16[16,48,128]{2,1,0:T(8,128)(2,1)} %broadcast_in_dim.4), calls=%async_computation.2 | async-start | bytes 393216 | tf_op jit(solution)/shard_map/all_to_all | solution.py:384
  49.1 0.7 broadcast_select_fusion.5
  49.8 6.4 %all-to-all-done.2.got_ref = bf16[16,48,128]{2,1,0:T(8,128)(2,1)S(1)} async-done(((bf16[16,48,128]{2,1,0:T(8,128)(2,1)}), bf16[16,48,128]{2,1,0:T(8,128)(2,1)S(1)}, u32[]{:S(2)}, u32[]{:S(2)}) %all-to-all-start.2) | async-done | bytes 196640 | tf_op jit(solution)/shard_map/all_to_all | solution.py:384
  56.3 1.6 %project.1.p0 = f32[48,512]{1,0:T(8,128)S(1)} custom-call(s32[2]{0:T(128)S(1)} %pad_add_fusion.where_ref, bf16[16,48,128]{2,1,0:T(8,128)(2,1)S(1)} %all-to-all-done.2.got_ref, bf16[2048,256]{1,0:T(8,128)(2,1)S(1)} %copy-done.1, bf16[2048,256]{1,0:T(8,128)(2,1)} %collective-permute-done.1.sib_ref), custom_call_target="tpu_custom_call" | custom-call | tf_op jit(solution)/shard_map/project/pallas_call | solution.py:469
  57.9 1.3 %collective-permute-start.2 = (f32[48,512]{1,0:T(8,128)S(1)}, f32[48,512]{1,0:T(8,128)S(1)}, u32[]{:S(2)}, u32[]{:S(2)}) collective-permute-start(f32[48,512]{1,0:T(8,128)S(1)} %project.1.p0), channel_id=1, source_target_pairs={{0,1},{1,0},{2,3},{3,2},{4,5},{5,4},{6,7},{7,6},{8,9},{9,8},{10,11... | collective-permute-start | bytes 294920 | tf_op jit(solution)/shard_map/ppermute | solution.py:392
  59.2 2.7 %collective-permute-start.3 = (f32[48,512]{1,0:T(8,128)S(1)}, f32[48,512]{1,0:T(8,128)S(1)}, u32[]{:S(2)}, u32[]{:S(2)}) collective-permute-start(f32[48,512]{1,0:T(8,128)S(1)} %project.1.p0), channel_id=1, source_target_pairs={{0,2},{1,3},{2,0},{3,1},{4,6},{5,7},{6,4},{7,5},{8,10},{9,11},{10,... | collective-permute-start | bytes 294920 | tf_op jit(solution)/shard_map/ppermute | solution.py:392
  62.0 3.0 %collective-permute-done.3.p2 = f32[48,512]{1,0:T(8,128)S(1)} collective-permute-done((f32[48,512]{1,0:T(8,128)S(1)}, f32[48,512]{1,0:T(8,128)S(1)}, u32[]{:S(2)}, u32[]{:S(2)}) %collective-permute-start.3) | collective-permute-done | bytes 98336 | tf_op jit(solution)/shard_map/ppermute | solution.py:392
  65.0 1.6 %collective-permute-done.4.p3 = f32[48,512]{1,0:T(8,128)S(1)} collective-permute-done((f32[48,512]{1,0:T(8,128)S(1)}, f32[48,512]{1,0:T(8,128)S(1)}, u32[]{:S(2)}, u32[]{:S(2)}) %collective-permute-start.4) | collective-permute-done | bytes 98336 | tf_op jit(solution)/shard_map/ppermute | solution.py:392
  66.6 5.2 %gate_up.1 = (bf16[16,208,128]{2,1,0:T(8,128)(2,1)S(1)}, f32[48,512]{1,0:T(8,128)S(1)}, bf16[128,8192]{1,0:T(8,128)(2,1)S(1)}, bf16[128,8192]{1,0:T(8,128)(2,1)S(1)}) custom-call(s32[2]{0:T(128)S(1)} %pad_add_fusion.where_ref, f32[48,512]{1,0:T(8,128)S(1)} %project.1.p0, f32[48,512]{1,0:T(8,128)S(1)} %collective-permute-done.2.p1, ...), custom_call_target="tpu_custom_call" | custom-call | tf_op jit(solution)/shard_map/gate_up/pallas_call | solution.py:480
  71.9 13.9 %all_to_all.25.got_ref = bf16[16,208,128]{2,1,0:T(8,128)(2,1)S(1)} all-to-all(bf16[16,208,128]{2,1,0:T(8,128)(2,1)S(1)} %get-tuple-element.13), channel_id=1, replica_groups={{0,8,16,24,32,40,48,56,64,72,80,88,96,104,112,120},{4,12,20,28,36,44,52..., dimensions={0} | all-to-all | bytes 1703936 | tf_op jit(solution)/shard_map/all_to_all | solution.py:384
  85.7 1.5 %down.1 = bf16[16,48,512]{2,1,0:T(8,128)(2,1)S(1)} custom-call(s32[2]{0:T(128)S(1)} %pad_add_fusion.where_ref, bf16[16,208,128]{2,1,0:T(8,128)(2,1)S(1)} %all_to_all.25.got_ref, bf16[128,8192]{1,0:T(8,128)(2,1)S(1)} %get-tuple-element.14.own_ref, bf16[128,8192]{1,0:T(8,128)(2,1)S(1)} %get-tuple-element.15.sib_ref), custom_call_target="tpu_custom_call" | custom-call | tf_op jit(solution)/shard_map/down/pallas_call | solution.py:496
  87.2 13.2 %all_to_all.26 = bf16[16,48,512]{2,1,0:T(8,128)(2,1)S(1)} all-to-all(bf16[16,48,512]{2,1,0:T(8,128)(2,1)S(1)} %down.1), channel_id=1, replica_groups={{0,8,16,24,32,40,48,56,64,72,80,88,96,104,112,120},{4,12,20,28,36,44,52..., dimensions={0} | all-to-all | bytes 1572864 | tf_op jit(solution)/shard_map/all_to_all | solution.py:384
  100.5 0.6 collective-permute-start.10
  101.1 1.7 %collective-permute-start.11 = (f32[48,512]{1,0:T(8,128)S(1)}, f32[48,512]{1,0:T(8,128)S(1)}, u32[]{:S(2)}, u32[]{:S(2)}) collective-permute-start(f32[48,512]{1,0:T(8,128)S(1)} %convert_reduce_fusion), channel_id=1, source_target_pairs={{0,3},{1,2},{2,1},{3,0},{4,7},{5,6},{6,5},{7,4},{8,11},{9,10},{10,... | collective-permute-start | bytes 294920 | tf_op jit(solution)/shard_map/ppermute | solution.py:392
  103.2 2.6 %collective-permute-done.10 = f32[48,512]{1,0:T(8,128)S(1)} collective-permute-done((f32[48,512]{1,0:T(8,128)S(1)}, f32[48,512]{1,0:T(8,128)S(1)}, u32[]{:S(2)}, u32[]{:S(2)}) %collective-permute-start.10) | collective-permute-done | bytes 98336 | tf_op jit(solution)/shard_map/ppermute | solution.py:392
  105.8 1.1 collective-permute-done.11
  106.9 8.3 %collective-permute-start.12 = (bf16[48,256]{1,0:T(8,128)(2,1)S(1)}, bf16[48,256]{1,0:T(8,128)(2,1)S(1)}, u32[]{:S(2)}, u32[]{:S(2)}) collective-permute-start(bf16[48,256]{1,0:T(8,128)(2,1)S(1)} %broadcast_select_fusion.2), channel_id=1, source_target_pairs={{0,4},{4,0},{8,12},{12,8},{16,20},{20,16},{24,28},{28,24},{32,36},... | collective-permute-start | bytes 73736 | tf_op jit(solution)/shard_map/ppermute | solution.py:389
  116.2 0.6 reshape.46
  (47 shorter events, 3.8 us)
Async XLA Ops:
  1.5 0.8 copy-start.2
  2.2 0.7 copy-start.3
  2.9 7.1 %copy-start = (bf16[256,4096]{1,0:T(8,128)(2,1)S(1)}, bf16[256,4096]{1,0:T(8,128)(2,1)}, u32[]{:S(2)}) copy-start(bf16[256,4096]{1,0:T(8,128)(2,1)} %g_own_hbm.1) | copy-start | bytes 6291460
  2.9 7.7 %copy-start.1 = (bf16[2048,256]{1,0:T(8,128)(2,1)S(1)}, bf16[2048,256]{1,0:T(8,128)(2,1)}, u32[]{:S(2)}) copy-start(bf16[2048,256]{1,0:T(8,128)(2,1)} %own_ref.1) | copy-start | bytes 3145732
  2.9 15.9 %copy-start.4 = (bf16[3,32,256]{2,1,0:T(8,128)(2,1)S(1)}, bf16[3,32,256]{2,1,0:T(8,128)(2,1)}, u32[]{:S(2)}) copy-start(bf16[3,32,256]{2,1,0:T(8,128)(2,1)} %param.20) | copy-start | bytes 147460
  2.9 16.1 %copy-start.5 = (bf16[256]{0:T(256)(128)(2,1)S(1)}, bf16[256]{0:T(256)(128)(2,1)}, u32[]{:S(2)}) copy-start(bf16[256]{0:T(256)(128)(2,1)} %param.21) | copy-start | bytes 1540
  2.9 19.1 %copy-start.6 = (bf16[3,1,256]{2,0,1:T(4,128)(2,1)S(1)}, bf16[3,1,256]{2,0,1:T(4,128)(2,1)}, u32[]{:S(2)}) copy-start(bf16[3,1,256]{2,0,1:T(4,128)(2,1)} %param.18) | copy-start | bytes 4612
  2.9 19.1 %copy-start.7 = (bf16[3,1,256]{2,0,1:T(4,128)(2,1)S(1)}, bf16[3,1,256]{2,0,1:T(4,128)(2,1)}, u32[]{:S(2)}) copy-start(bf16[3,1,256]{2,0,1:T(4,128)(2,1)} %param.19) | copy-start | bytes 4612
  8.7 12.9 %collective-permute-start = (bf16[16,512,256]{2,1,0:T(8,128)(2,1)}, bf16[16,512,256]{2,1,0:T(8,128)(2,1)}, u32[]{:S(2)}, u32[]{:S(2)}) collective-permute-start(bf16[16,512,256]{2,1,0:T(8,128)(2,1)} %get-tuple-element.11), channel_id=1, source_target_pairs={{0,4},{4,0},{8,12},{12,8},{16,20},{20,16},{24,28},{28,24},{32,36},... | collective-permute-start | bytes 12582920 | tf_op jit(solution)/shard_map/ppermute | solution.py:389
  10.0 51.9 %collective-permute-start.6 = (bf16[256,4096]{1,0:T(8,128)(2,1)S(1)}, bf16[256,4096]{1,0:T(8,128)(2,1)}, u32[]{:S(2)}, u32[]{:S(2)}) collective-permute-start(bf16[256,4096]{1,0:T(8,128)(2,1)S(1)} %copy-done), channel_id=1, source_target_pairs={{0,4},{4,0},{8,12},{12,8},{16,20},{20,16},{24,28},{28,24},{32,36},... | collective-permute-start | bytes 6291464 | tf_op jit(solution)/shard_map/ppermute | solution.py:389
  10.1 51.9 %collective-permute-start.7 = (bf16[256,4096]{1,0:T(8,128)(2,1)}, bf16[256,4096]{1,0:T(8,128)(2,1)}, u32[]{:S(2)}, u32[]{:S(2)}) collective-permute-start(bf16[256,4096]{1,0:T(8,128)(2,1)} %u_own_hbm.1), channel_id=1, source_target_pairs={{0,4},{4,0},{8,12},{12,8},{16,20},{20,16},{24,28},{28,24},{32,36},... | collective-permute-start | bytes 6291464 | tf_op jit(solution)/shard_map/ppermute | solution.py:389
  10.5 51.5 %collective-permute-start.8 = (bf16[128,8192]{1,0:T(8,128)(2,1)}, bf16[128,8192]{1,0:T(8,128)(2,1)}, u32[]{:S(2)}, u32[]{:S(2)}) collective-permute-start(bf16[128,8192]{1,0:T(8,128)(2,1)} %d_own_hbm.1), channel_id=1, source_target_pairs={{0,4},{4,0},{8,12},{12,8},{16,20},{20,16},{24,28},{28,24},{32,36},... | collective-permute-start | bytes 6291464 | tf_op jit(solution)/shard_map/ppermute | solution.py:389
  10.6 39.2 %collective-permute-start.1 = (bf16[2048,256]{1,0:T(8,128)(2,1)S(1)}, bf16[2048,256]{1,0:T(8,128)(2,1)}, u32[]{:S(2)}, u32[]{:S(2)}) collective-permute-start(bf16[2048,256]{1,0:T(8,128)(2,1)S(1)} %copy-done.1), channel_id=1, source_target_pairs={{0,4},{4,0},{8,12},{12,8},{16,20},{20,16},{24,28},{28,24},{32,36},... | collective-permute-start | bytes 3145736 | tf_op jit(solution)/shard_map/ppermute | solution.py:389
  11.0 15.5 %all-to-all-start = ((bf16[16,48,128]{2,1,0:T(8,128)(2,1)}), bf16[16,48,128]{2,1,0:T(8,128)(2,1)S(1)}, u32[]{:S(2)}, u32[]{:S(2)}) async-start(bf16[16,48,128]{2,1,0:T(8,128)(2,1)} %get-tuple-element.10), calls=%async_computation | async-start | bytes 393216 | tf_op jit(solution)/shard_map/all_to_all | solution.py:384
  21.6 15.1 %collective-permute-start.5 = (bf16[64,256]{1,0:T(8,128)(2,1)}, bf16[64,256]{1,0:T(8,128)(2,1)}, u32[]{:S(2)}, u32[]{:S(2)}) collective-permute-start(bf16[64,256]{1,0:T(8,128)(2,1)} %pad_maximum_fusion.2), channel_id=1, source_target_pairs={{0,4},{4,0},{8,12},{12,8},{16,20},{20,16},{24,28},{28,24},{32,36},... | collective-permute-start | bytes 98312 | tf_op jit(solution)/shard_map/ppermute | solution.py:389
  33.1 11.1 %all-to-all-start.1 = ((bf16[16,64,128]{2,1,0:T(8,128)(2,1)}), bf16[16,64,128]{2,1,0:T(8,128)(2,1)S(1)}, u32[]{:S(2)}, u32[]{:S(2)}) async-start(bf16[16,64,128]{2,1,0:T(8,128)(2,1)} %attend.1), calls=%async_computation.1 | async-start | bytes 524288 | tf_op jit(solution)/shard_map/all_to_all | solution.py:384
  45.6 10.7 %all-to-all-start.2 = ((bf16[16,48,128]{2,1,0:T(8,128)(2,1)}), bf16[16,48,128]{2,1,0:T(8,128)(2,1)S(1)}, u32[]{:S(2)}, u32[]{:S(2)}) async-start(bf16[16,48,128]{2,1,0:T(8,128)(2,1)} %broadcast_in_dim.4), calls=%async_computation.2 | async-start | bytes 393216 | tf_op jit(solution)/shard_map/all_to_all | solution.py:384
  57.9 4.1 %collective-permute-start.2 = (f32[48,512]{1,0:T(8,128)S(1)}, f32[48,512]{1,0:T(8,128)S(1)}, u32[]{:S(2)}, u32[]{:S(2)}) collective-permute-start(f32[48,512]{1,0:T(8,128)S(1)} %project.1.p0), channel_id=1, source_target_pairs={{0,1},{1,0},{2,3},{3,2},{4,5},{5,4},{6,7},{7,6},{8,9},{9,8},{10,11... | collective-permute-start | bytes 294920 | tf_op jit(solution)/shard_map/ppermute | solution.py:392
  59.2 5.8 %collective-permute-start.3 = (f32[48,512]{1,0:T(8,128)S(1)}, f32[48,512]{1,0:T(8,128)S(1)}, u32[]{:S(2)}, u32[]{:S(2)}) collective-permute-start(f32[48,512]{1,0:T(8,128)S(1)} %project.1.p0), channel_id=1, source_target_pairs={{0,2},{1,3},{2,0},{3,1},{4,6},{5,7},{6,4},{7,5},{8,10},{9,11},{10,... | collective-permute-start | bytes 294920 | tf_op jit(solution)/shard_map/ppermute | solution.py:392
  61.9 4.7 %collective-permute-start.4 = (f32[48,512]{1,0:T(8,128)S(1)}, f32[48,512]{1,0:T(8,128)S(1)}, u32[]{:S(2)}, u32[]{:S(2)}) collective-permute-start(f32[48,512]{1,0:T(8,128)S(1)} %project.1.p0), channel_id=1, source_target_pairs={{0,3},{1,2},{2,1},{3,0},{4,7},{5,6},{6,5},{7,4},{8,11},{9,10},{10,... | collective-permute-start | bytes 294920 | tf_op jit(solution)/shard_map/ppermute | solution.py:392
  100.5 5.3 %collective-permute-start.10 = (f32[48,512]{1,0:T(8,128)S(1)}, f32[48,512]{1,0:T(8,128)S(1)}, u32[]{:S(2)}, u32[]{:S(2)}) collective-permute-start(f32[48,512]{1,0:T(8,128)S(1)} %convert_reduce_fusion), channel_id=1, source_target_pairs={{0,2},{1,3},{2,0},{3,1},{4,6},{5,7},{6,4},{7,5},{8,10},{9,11},{10,... | collective-permute-start | bytes 294920 | tf_op jit(solution)/shard_map/ppermute | solution.py:392
  101.1 5.8 %collective-permute-start.11 = (f32[48,512]{1,0:T(8,128)S(1)}, f32[48,512]{1,0:T(8,128)S(1)}, u32[]{:S(2)}, u32[]{:S(2)}) collective-permute-start(f32[48,512]{1,0:T(8,128)S(1)} %convert_reduce_fusion), channel_id=1, source_target_pairs={{0,3},{1,2},{2,1},{3,0},{4,7},{5,6},{6,5},{7,4},{8,11},{9,10},{10,... | collective-permute-start | bytes 294920 | tf_op jit(solution)/shard_map/ppermute | solution.py:392
  102.8 4.1 %collective-permute-start.9 = (f32[48,512]{1,0:T(8,128)S(1)}, f32[48,512]{1,0:T(8,128)S(1)}, u32[]{:S(2)}, u32[]{:S(2)}) collective-permute-start(f32[48,512]{1,0:T(8,128)S(1)} %convert_reduce_fusion), channel_id=1, source_target_pairs={{0,1},{1,0},{2,3},{3,2},{4,5},{5,4},{6,7},{7,6},{8,9},{9,8},{10,11... | collective-permute-start | bytes 294920 | tf_op jit(solution)/shard_map/ppermute | solution.py:392
  106.9 9.2 %collective-permute-start.12 = (bf16[48,256]{1,0:T(8,128)(2,1)S(1)}, bf16[48,256]{1,0:T(8,128)(2,1)S(1)}, u32[]{:S(2)}, u32[]{:S(2)}) collective-permute-start(bf16[48,256]{1,0:T(8,128)(2,1)S(1)} %broadcast_select_fusion.2), channel_id=1, source_target_pairs={{0,4},{4,0},{8,12},{12,8},{16,20},{20,16},{24,28},{28,24},{32,36},... | collective-permute-start | bytes 73736 | tf_op jit(solution)/shard_map/ppermute | solution.py:389

commit v4 on v3

--- a/solution.py
+++ b/solution.py
@@ -181,10 +181,9 @@
         out_ref[chip, :ROWS, :] = summed.astype(bf16)
         out_ref[chip, ROWS:, :] = dot(unit, notes, 1, 1).astype(bf16)
 
-    fetch(0)
     for g in range(groups):
-        if g + 1 < groups:
-            fetch(g + 1)
+        fetch(g)
+    for g in range(groups):
         at = pl.ds(g * size, size)
         pltpu.make_async_copy(own_ref.at[at], own_ref.at[at], own_sems.at[g]).wait()
         from_sib(g).wait()
@@ -487,7 +486,7 @@
             jax.ShapeDtypeStruct(w_down.shape, bf16),
             jax.ShapeDtypeStruct(w_down.shape, bf16),
         ],
-        scratch_shapes=[pltpu.VMEM(w_gate.shape, bf16)] * 4 + [dma((4, 4)), dma((2,))],
+        scratch_shapes=[pltpu.VMEM(w_gate.shape, bf16)] * 4 + [dma((4, 8)), dma((2,))],
         compiler_params=params,
         name="gate_up",
     )(where, *parts, res, gain, w_gate, w_up, w_gate_sib, w_up_sib, w_down, w_down_sib)

time: 118 us -> 117 us (level)
  transfers between devices with their start and end apart: 16 -> 16, of which waited for: 9 -> 9; matrix products, arithmetic and copies ran while one was open for 3% -> 3% of each run, Pallas kernels for 8% -> 7%
where the time goes in v4:
time: 117 us; the launch traced here: 116 us
  starting transfers between devices  32.6 us (28%)
  waiting for transfers between devices  28.3 us (24%)
  blocking collectives  27 us (23%)
  Pallas kernels  20.7 us (18%)
  local copies, waits for them, and re-layouts  4.39 us (4%)
  other arithmetic  2.34 us (2%)
    all_to_all x2, blocking collectives, over_chips(): lax.all_to_all(x, 'seq', split_axis=0, concat_axis=0, tiled=True, axis_in...  27 us
    all_to_all x3, waiting for transfers between devices, over_chips(): lax.all_to_all(x, 'seq', split_axis=0, concat_axis=0, tiled=True, axis_in...  17.6 us
    all_to_all x3, starting transfers between devices, over_chips(): lax.all_to_all(x, 'seq', split_axis=0, concat_axis=0, tiled=True, axis_in...  14.7 us
    ppermute x7, starting transfers between devices, sibling(): return lax.ppermute(x, 'seq', swap)  11.1 us
    ppermute x6, waiting for transfers between devices, heads(): lax.ppermute(x, 'head', [(i, i ^ s) for i in range(4)])  8.31 us
    ppermute x6, starting transfers between devices, heads(): lax.ppermute(x, 'head', [(i, i ^ s) for i in range(4)])  6.86 us
    pallas_call x1, Pallas kernels, on_device(): pl.pallas_call(attend_kernel, in_specs=[smem, smem, vmem, hbm, hbm, pl.Bl...  5.98 us
    pallas_call x1, Pallas kernels, on_device(): pl.pallas_call(gather_kernel, in_specs=[smem, smem, vmem, vmem, hbm, hbm]...  5.77 us
  transfers between devices with their start and end apart: 16, of which 9 were waited for; matrix products, arithmetic and copies ran while one was open for 3% of the time, Pallas kernels for 7%

profile of v4, /device:TPU:1, one launch (start us, length us, event | category | flops | bytes accessed | tf_op | source)
XLA Modules:
  0.0 116.2 jit_solution(15518284748932152096)
XLA Ops:
  0.6 0.7 reshape.37.q_ref
  1.5 0.8 copy-done.2
  2.2 0.7 copy-done.3
  2.9 5.8 %gather.1 = (bf16[16,512,256]{2,1,0:T(8,128)(2,1)}, bf16[16,48,128]{2,1,0:T(8,128)(2,1)}, s32[32]{0:T(128)S(1)}) custom-call(s32[2]{0:T(128)S(1)} %pad_add_fusion.where_ref, s32[2,32]{1,0:T(2,128)S(1)} %bitcast.13, s32[32,2,128]{2,1,0:T(2,128)S(1)} %copy-done.2, bf16[48,128]{1,0:T(8,128)(2,1)S(1)} %reshape.37.q_ref, bf16[32,512,256]{2,1,0:T(8,128)(2,1)} %k_ref.3, ...), custom_call_target="tpu_custom_call" | custom-call | tf_op jit(solution)/shard_map/gather/pallas_call | solution.py:408
  8.7 1.3 %collective-permute-start = (bf16[16,512,256]{2,1,0:T(8,128)(2,1)}, bf16[16,512,256]{2,1,0:T(8,128)(2,1)}, u32[]{:S(2)}, u32[]{:S(2)}) collective-permute-start(bf16[16,512,256]{2,1,0:T(8,128)(2,1)} %get-tuple-element.11), channel_id=1, source_target_pairs={{0,4},{4,0},{8,12},{12,8},{16,20},{20,16},{24,28},{28,24},{32,36},... | collective-permute-start | bytes 12582920 | tf_op jit(solution)/shard_map/ppermute | solution.py:388
  11.1 7.6 %all-to-all-start = ((bf16[16,48,128]{2,1,0:T(8,128)(2,1)}), bf16[16,48,128]{2,1,0:T(8,128)(2,1)S(1)}, u32[]{:S(2)}, u32[]{:S(2)}) async-start(bf16[16,48,128]{2,1,0:T(8,128)(2,1)} %get-tuple-element.10), calls=%async_computation | async-start | bytes 393216 | tf_op jit(solution)/shard_map/all_to_all | solution.py:383
  18.9 0.6 pad_maximum_fusion.2
  19.6 2.1 %collective-permute-done.sib_hbm = bf16[16,512,256]{2,1,0:T(8,128)(2,1)} collective-permute-done((bf16[16,512,256]{2,1,0:T(8,128)(2,1)}, bf16[16,512,256]{2,1,0:T(8,128)(2,1)}, u32[]{:S(2)}, u32[]{:S(2)}) %collective-permute-start) | collective-permute-done | bytes 4194336 | tf_op jit(solution)/shard_map/ppermute | solution.py:388
  22.1 4.4 %all-to-all-done.q_ref = bf16[16,48,128]{2,1,0:T(8,128)(2,1)S(1)} async-done(((bf16[16,48,128]{2,1,0:T(8,128)(2,1)}), bf16[16,48,128]{2,1,0:T(8,128)(2,1)S(1)}, u32[]{:S(2)}, u32[]{:S(2)}) %all-to-all-start) | async-done | bytes 196640 | tf_op jit(solution)/shard_map/all_to_all | solution.py:383
  26.5 6.0 %attend.1 = bf16[16,64,128]{2,1,0:T(8,128)(2,1)} custom-call(s32[2]{0:T(128)S(1)} %pad_add_fusion.where_ref, s32[32]{0:T(128)S(1)} %get-tuple-element.9.codes_ref, bf16[16,48,128]{2,1,0:T(8,128)(2,1)S(1)} %all-to-all-done.q_ref, bf16[32,512,256]{2,1,0:T(8,128)(2,1)} %k_ref.3, bf16[32,512,256]{2,1,0:T(8,128)(2,1)} %v_ref.3, ...), custom_call_target="tpu_custom_call" | custom-call | tf_op jit(solution)/shard_map/attend/pallas_call | solution.py:431
  32.5 3.5 %all-to-all-start.1 = ((bf16[16,64,128]{2,1,0:T(8,128)(2,1)}), bf16[16,64,128]{2,1,0:T(8,128)(2,1)S(1)}, u32[]{:S(2)}, u32[]{:S(2)}) async-start(bf16[16,64,128]{2,1,0:T(8,128)(2,1)} %attend.1), calls=%async_computation.1 | async-start | bytes 524288 | tf_op jit(solution)/shard_map/all_to_all | solution.py:383
  36.0 0.7 bitcast_select_fusion.1
  36.8 6.8 %all-to-all-done.1.got_ref = bf16[16,64,128]{2,1,0:T(8,128)(2,1)S(1)} async-done(((bf16[16,64,128]{2,1,0:T(8,128)(2,1)}), bf16[16,64,128]{2,1,0:T(8,128)(2,1)S(1)}, u32[]{:S(2)}, u32[]{:S(2)}) %all-to-all-start.1) | async-done | bytes 262176 | tf_op jit(solution)/shard_map/all_to_all | solution.py:383
  43.6 0.6 combine.1
  44.2 0.7 broadcast_in_dim.4
  44.9 3.5 %all-to-all-start.2 = ((bf16[16,48,128]{2,1,0:T(8,128)(2,1)}), bf16[16,48,128]{2,1,0:T(8,128)(2,1)S(1)}, u32[]{:S(2)}, u32[]{:S(2)}) async-start(bf16[16,48,128]{2,1,0:T(8,128)(2,1)} %broadcast_in_dim.4), calls=%async_computation.2 | async-start | bytes 393216 | tf_op jit(solution)/shard_map/all_to_all | solution.py:383
  48.4 0.7 broadcast_select_fusion.5
  49.1 6.4 %all-to-all-done.2.got_ref = bf16[16,48,128]{2,1,0:T(8,128)(2,1)S(1)} async-done(((bf16[16,48,128]{2,1,0:T(8,128)(2,1)}), bf16[16,48,128]{2,1,0:T(8,128)(2,1)S(1)}, u32[]{:S(2)}, u32[]{:S(2)}) %all-to-all-start.2) | async-done | bytes 196640 | tf_op jit(solution)/shard_map/all_to_all | solution.py:383
  55.6 1.6 %project.1.p0 = f32[48,512]{1,0:T(8,128)S(1)} custom-call(s32[2]{0:T(128)S(1)} %pad_add_fusion.where_ref, bf16[16,48,128]{2,1,0:T(8,128)(2,1)S(1)} %all-to-all-done.2.got_ref, bf16[2048,256]{1,0:T(8,128)(2,1)S(1)} %copy-done.1, bf16[2048,256]{1,0:T(8,128)(2,1)} %collective-permute-done.1.sib_ref), custom_call_target="tpu_custom_call" | custom-call | tf_op jit(solution)/shard_map/project/pallas_call | solution.py:468
  57.2 1.6 %collective-permute-start.2 = (f32[48,512]{1,0:T(8,128)S(1)}, f32[48,512]{1,0:T(8,128)S(1)}, u32[]{:S(2)}, u32[]{:S(2)}) collective-permute-start(f32[48,512]{1,0:T(8,128)S(1)} %project.1.p0), channel_id=1, source_target_pairs={{0,1},{1,0},{2,3},{3,2},{4,5},{5,4},{6,7},{7,6},{8,9},{9,8},{10,11... | collective-permute-start | bytes 294920 | tf_op jit(solution)/shard_map/ppermute | solution.py:391
  58.9 2.5 %collective-permute-start.3 = (f32[48,512]{1,0:T(8,128)S(1)}, f32[48,512]{1,0:T(8,128)S(1)}, u32[]{:S(2)}, u32[]{:S(2)}) collective-permute-start(f32[48,512]{1,0:T(8,128)S(1)} %project.1.p0), channel_id=1, source_target_pairs={{0,2},{1,3},{2,0},{3,1},{4,6},{5,7},{6,4},{7,5},{8,10},{9,11},{10,... | collective-permute-start | bytes 294920 | tf_op jit(solution)/shard_map/ppermute | solution.py:391
  61.4 3.0 %collective-permute-done.3.p2 = f32[48,512]{1,0:T(8,128)S(1)} collective-permute-done((f32[48,512]{1,0:T(8,128)S(1)}, f32[48,512]{1,0:T(8,128)S(1)}, u32[]{:S(2)}, u32[]{:S(2)}) %collective-permute-start.3) | collective-permute-done | bytes 98336 | tf_op jit(solution)/shard_map/ppermute | solution.py:391
  64.4 1.6 %collective-permute-done.4.p3 = f32[48,512]{1,0:T(8,128)S(1)} collective-permute-done((f32[48,512]{1,0:T(8,128)S(1)}, f32[48,512]{1,0:T(8,128)S(1)}, u32[]{:S(2)}, u32[]{:S(2)}) %collective-permute-start.4) | collective-permute-done | bytes 98336 | tf_op jit(solution)/shard_map/ppermute | solution.py:391
  66.1 5.2 %gate_up.1 = (bf16[16,208,128]{2,1,0:T(8,128)(2,1)S(1)}, f32[48,512]{1,0:T(8,128)S(1)}, bf16[128,8192]{1,0:T(8,128)(2,1)S(1)}, bf16[128,8192]{1,0:T(8,128)(2,1)S(1)}) custom-call(s32[2]{0:T(128)S(1)} %pad_add_fusion.where_ref, f32[48,512]{1,0:T(8,128)S(1)} %project.1.p0, f32[48,512]{1,0:T(8,128)S(1)} %collective-permute-done.2.p1, ...), custom_call_target="tpu_custom_call" | custom-call | tf_op jit(solution)/shard_map/gate_up/pallas_call | solution.py:479
  71.3 13.9 %all_to_all.25.got_ref = bf16[16,208,128]{2,1,0:T(8,128)(2,1)S(1)} all-to-all(bf16[16,208,128]{2,1,0:T(8,128)(2,1)S(1)} %get-tuple-element.13), channel_id=1, replica_groups={{0,8,16,24,32,40,48,56,64,72,80,88,96,104,112,120},{4,12,20,28,36,44,52..., dimensions={0} | all-to-all | bytes 1703936 | tf_op jit(solution)/shard_map/all_to_all | solution.py:383
  85.1 1.5 %down.1 = bf16[16,48,512]{2,1,0:T(8,128)(2,1)S(1)} custom-call(s32[2]{0:T(128)S(1)} %pad_add_fusion.where_ref, bf16[16,208,128]{2,1,0:T(8,128)(2,1)S(1)} %all_to_all.25.got_ref, bf16[128,8192]{1,0:T(8,128)(2,1)S(1)} %get-tuple-element.14.own_ref, bf16[128,8192]{1,0:T(8,128)(2,1)S(1)} %get-tuple-element.15.sib_ref), custom_call_target="tpu_custom_call" | custom-call | tf_op jit(solution)/shard_map/down/pallas_call | solution.py:495
  86.6 13.2 %all_to_all.26 = bf16[16,48,512]{2,1,0:T(8,128)(2,1)S(1)} all-to-all(bf16[16,48,512]{2,1,0:T(8,128)(2,1)S(1)} %down.1), channel_id=1, replica_groups={{0,8,16,24,32,40,48,56,64,72,80,88,96,104,112,120},{4,12,20,28,36,44,52..., dimensions={0} | all-to-all | bytes 1572864 | tf_op jit(solution)/shard_map/all_to_all | solution.py:383
  100.3 1.9 %collective-permute-start.11 = (f32[48,512]{1,0:T(8,128)S(1)}, f32[48,512]{1,0:T(8,128)S(1)}, u32[]{:S(2)}, u32[]{:S(2)}) collective-permute-start(f32[48,512]{1,0:T(8,128)S(1)} %convert_reduce_fusion), channel_id=1, source_target_pairs={{0,3},{1,2},{2,1},{3,0},{4,7},{5,6},{6,5},{7,4},{8,11},{9,10},{10,... | collective-permute-start | bytes 294920 | tf_op jit(solution)/shard_map/ppermute | solution.py:391
  102.6 2.6 %collective-permute-done.10 = f32[48,512]{1,0:T(8,128)S(1)} collective-permute-done((f32[48,512]{1,0:T(8,128)S(1)}, f32[48,512]{1,0:T(8,128)S(1)}, u32[]{:S(2)}, u32[]{:S(2)}) %collective-permute-start.10) | collective-permute-done | bytes 98336 | tf_op jit(solution)/shard_map/ppermute | solution.py:391
  105.2 1.1 collective-permute-done.11
  106.3 8.3 %collective-permute-start.12 = (bf16[48,256]{1,0:T(8,128)(2,1)S(1)}, bf16[48,256]{1,0:T(8,128)(2,1)S(1)}, u32[]{:S(2)}, u32[]{:S(2)}) collective-permute-start(bf16[48,256]{1,0:T(8,128)(2,1)S(1)} %broadcast_select_fusion.2), channel_id=1, source_target_pairs={{0,4},{4,0},{8,12},{12,8},{16,20},{20,16},{24,28},{28,24},{32,36},... | collective-permute-start | bytes 73736 | tf_op jit(solution)/shard_map/ppermute | solution.py:388
  115.6 0.6 reshape.46
  (47 shorter events, 3.6 us)
Async XLA Ops:
  1.5 0.8 copy-start.2
  2.2 0.7 copy-start.3
  2.9 7.2 %copy-start = (bf16[256,4096]{1,0:T(8,128)(2,1)S(1)}, bf16[256,4096]{1,0:T(8,128)(2,1)}, u32[]{:S(2)}) copy-start(bf16[256,4096]{1,0:T(8,128)(2,1)} %g_own_hbm.1) | copy-start | bytes 6291460
  2.9 7.8 %copy-start.1 = (bf16[2048,256]{1,0:T(8,128)(2,1)S(1)}, bf16[2048,256]{1,0:T(8,128)(2,1)}, u32[]{:S(2)}) copy-start(bf16[2048,256]{1,0:T(8,128)(2,1)} %own_ref.1) | copy-start | bytes 3145732
  2.9 15.8 %copy-start.4 = (bf16[3,32,256]{2,1,0:T(8,128)(2,1)S(1)}, bf16[3,32,256]{2,1,0:T(8,128)(2,1)}, u32[]{:S(2)}) copy-start(bf16[3,32,256]{2,1,0:T(8,128)(2,1)} %param.20) | copy-start | bytes 147460
  2.9 16.0 %copy-start.5 = (bf16[256]{0:T(256)(128)(2,1)S(1)}, bf16[256]{0:T(256)(128)(2,1)}, u32[]{:S(2)}) copy-start(bf16[256]{0:T(256)(128)(2,1)} %param.21) | copy-start | bytes 1540
  2.9 19.1 %copy-start.6 = (bf16[3,1,256]{2,0,1:T(4,128)(2,1)S(1)}, bf16[3,1,256]{2,0,1:T(4,128)(2,1)}, u32[]{:S(2)}) copy-start(bf16[3,1,256]{2,0,1:T(4,128)(2,1)} %param.18) | copy-start | bytes 4612
  2.9 19.1 %copy-start.7 = (bf16[3,1,256]{2,0,1:T(4,128)(2,1)S(1)}, bf16[3,1,256]{2,0,1:T(4,128)(2,1)}, u32[]{:S(2)}) copy-start(bf16[3,1,256]{2,0,1:T(4,128)(2,1)} %param.19) | copy-start | bytes 4612
  8.7 13.0 %collective-permute-start = (bf16[16,512,256]{2,1,0:T(8,128)(2,1)}, bf16[16,512,256]{2,1,0:T(8,128)(2,1)}, u32[]{:S(2)}, u32[]{:S(2)}) collective-permute-start(bf16[16,512,256]{2,1,0:T(8,128)(2,1)} %get-tuple-element.11), channel_id=1, source_target_pairs={{0,4},{4,0},{8,12},{12,8},{16,20},{20,16},{24,28},{28,24},{32,36},... | collective-permute-start | bytes 12582920 | tf_op jit(solution)/shard_map/ppermute | solution.py:388
  10.1 51.3 %collective-permute-start.6 = (bf16[256,4096]{1,0:T(8,128)(2,1)S(1)}, bf16[256,4096]{1,0:T(8,128)(2,1)}, u32[]{:S(2)}, u32[]{:S(2)}) collective-permute-start(bf16[256,4096]{1,0:T(8,128)(2,1)S(1)} %copy-done), channel_id=1, source_target_pairs={{0,4},{4,0},{8,12},{12,8},{16,20},{20,16},{24,28},{28,24},{32,36},... | collective-permute-start | bytes 6291464 | tf_op jit(solution)/shard_map/ppermute | solution.py:388
  10.2 51.2 %collective-permute-start.7 = (bf16[256,4096]{1,0:T(8,128)(2,1)}, bf16[256,4096]{1,0:T(8,128)(2,1)}, u32[]{:S(2)}, u32[]{:S(2)}) collective-permute-start(bf16[256,4096]{1,0:T(8,128)(2,1)} %u_own_hbm.1), channel_id=1, source_target_pairs={{0,4},{4,0},{8,12},{12,8},{16,20},{20,16},{24,28},{28,24},{32,36},... | collective-permute-start | bytes 6291464 | tf_op jit(solution)/shard_map/ppermute | solution.py:388
  10.6 50.8 %collective-permute-start.8 = (bf16[128,8192]{1,0:T(8,128)(2,1)}, bf16[128,8192]{1,0:T(8,128)(2,1)}, u32[]{:S(2)}, u32[]{:S(2)}) collective-permute-start(bf16[128,8192]{1,0:T(8,128)(2,1)} %d_own_hbm.1), channel_id=1, source_target_pairs={{0,4},{4,0},{8,12},{12,8},{16,20},{20,16},{24,28},{28,24},{32,36},... | collective-permute-start | bytes 6291464 | tf_op jit(solution)/shard_map/ppermute | solution.py:388
  10.7 38.5 %collective-permute-start.1 = (bf16[2048,256]{1,0:T(8,128)(2,1)S(1)}, bf16[2048,256]{1,0:T(8,128)(2,1)}, u32[]{:S(2)}, u32[]{:S(2)}) collective-permute-start(bf16[2048,256]{1,0:T(8,128)(2,1)S(1)} %copy-done.1), channel_id=1, source_target_pairs={{0,4},{4,0},{8,12},{12,8},{16,20},{20,16},{24,28},{28,24},{32,36},... | collective-permute-start | bytes 3145736 | tf_op jit(solution)/shard_map/ppermute | solution.py:388
  11.1 15.4 %all-to-all-start = ((bf16[16,48,128]{2,1,0:T(8,128)(2,1)}), bf16[16,48,128]{2,1,0:T(8,128)(2,1)S(1)}, u32[]{:S(2)}, u32[]{:S(2)}) async-start(bf16[16,48,128]{2,1,0:T(8,128)(2,1)} %get-tuple-element.10), calls=%async_computation | async-start | bytes 393216 | tf_op jit(solution)/shard_map/all_to_all | solution.py:383
  21.7 14.3 %collective-permute-start.5 = (bf16[64,256]{1,0:T(8,128)(2,1)}, bf16[64,256]{1,0:T(8,128)(2,1)}, u32[]{:S(2)}, u32[]{:S(2)}) collective-permute-start(bf16[64,256]{1,0:T(8,128)(2,1)} %pad_maximum_fusion.2), channel_id=1, source_target_pairs={{0,4},{4,0},{8,12},{12,8},{16,20},{20,16},{24,28},{28,24},{32,36},... | collective-permute-start | bytes 98312 | tf_op jit(solution)/shard_map/ppermute | solution.py:388
  32.5 11.1 %all-to-all-start.1 = ((bf16[16,64,128]{2,1,0:T(8,128)(2,1)}), bf16[16,64,128]{2,1,0:T(8,128)(2,1)S(1)}, u32[]{:S(2)}, u32[]{:S(2)}) async-start(bf16[16,64,128]{2,1,0:T(8,128)(2,1)} %attend.1), calls=%async_computation.1 | async-start | bytes 524288 | tf_op jit(solution)/shard_map/all_to_all | solution.py:383
  44.9 10.7 %all-to-all-start.2 = ((bf16[16,48,128]{2,1,0:T(8,128)(2,1)}), bf16[16,48,128]{2,1,0:T(8,128)(2,1)S(1)}, u32[]{:S(2)}, u32[]{:S(2)}) async-start(bf16[16,48,128]{2,1,0:T(8,128)(2,1)} %broadcast_in_dim.4), calls=%async_computation.2 | async-start | bytes 393216 | tf_op jit(solution)/shard_map/all_to_all | solution.py:383
  57.2 4.2 %collective-permute-start.2 = (f32[48,512]{1,0:T(8,128)S(1)}, f32[48,512]{1,0:T(8,128)S(1)}, u32[]{:S(2)}, u32[]{:S(2)}) collective-permute-start(f32[48,512]{1,0:T(8,128)S(1)} %project.1.p0), channel_id=1, source_target_pairs={{0,1},{1,0},{2,3},{3,2},{4,5},{5,4},{6,7},{7,6},{8,9},{9,8},{10,11... | collective-permute-start | bytes 294920 | tf_op jit(solution)/shard_map/ppermute | solution.py:391
  58.9 5.6 %collective-permute-start.3 = (f32[48,512]{1,0:T(8,128)S(1)}, f32[48,512]{1,0:T(8,128)S(1)}, u32[]{:S(2)}, u32[]{:S(2)}) collective-permute-start(f32[48,512]{1,0:T(8,128)S(1)} %project.1.p0), channel_id=1, source_target_pairs={{0,2},{1,3},{2,0},{3,1},{4,6},{5,7},{6,4},{7,5},{8,10},{9,11},{10,... | collective-permute-start | bytes 294920 | tf_op jit(solution)/shard_map/ppermute | solution.py:391
  61.4 4.7 %collective-permute-start.4 = (f32[48,512]{1,0:T(8,128)S(1)}, f32[48,512]{1,0:T(8,128)S(1)}, u32[]{:S(2)}, u32[]{:S(2)}) collective-permute-start(f32[48,512]{1,0:T(8,128)S(1)} %project.1.p0), channel_id=1, source_target_pairs={{0,3},{1,2},{2,1},{3,0},{4,7},{5,6},{6,5},{7,4},{8,11},{9,10},{10,... | collective-permute-start | bytes 294920 | tf_op jit(solution)/shard_map/ppermute | solution.py:391
  99.9 5.3 %collective-permute-start.10 = (f32[48,512]{1,0:T(8,128)S(1)}, f32[48,512]{1,0:T(8,128)S(1)}, u32[]{:S(2)}, u32[]{:S(2)}) collective-permute-start(f32[48,512]{1,0:T(8,128)S(1)} %convert_reduce_fusion), channel_id=1, source_target_pairs={{0,2},{1,3},{2,0},{3,1},{4,6},{5,7},{6,4},{7,5},{8,10},{9,11},{10,... | collective-permute-start | bytes 294920 | tf_op jit(solution)/shard_map/ppermute | solution.py:391
  100.3 6.0 %collective-permute-start.11 = (f32[48,512]{1,0:T(8,128)S(1)}, f32[48,512]{1,0:T(8,128)S(1)}, u32[]{:S(2)}, u32[]{:S(2)}) collective-permute-start(f32[48,512]{1,0:T(8,128)S(1)} %convert_reduce_fusion), channel_id=1, source_target_pairs={{0,3},{1,2},{2,1},{3,0},{4,7},{5,6},{6,5},{7,4},{8,11},{9,10},{10,... | collective-permute-start | bytes 294920 | tf_op jit(solution)/shard_map/ppermute | solution.py:391
  102.2 4.1 %collective-permute-start.9 = (f32[48,512]{1,0:T(8,128)S(1)}, f32[48,512]{1,0:T(8,128)S(1)}, u32[]{:S(2)}, u32[]{:S(2)}) collective-permute-start(f32[48,512]{1,0:T(8,128)S(1)} %convert_reduce_fusion), channel_id=1, source_target_pairs={{0,1},{1,0},{2,3},{3,2},{4,5},{5,4},{6,7},{7,6},{8,9},{9,8},{10,11... | collective-permute-start | bytes 294920 | tf_op jit(solution)/shard_map/ppermute | solution.py:391
  106.3 9.2 %collective-permute-start.12 = (bf16[48,256]{1,0:T(8,128)(2,1)S(1)}, bf16[48,256]{1,0:T(8,128)(2,1)S(1)}, u32[]{:S(2)}, u32[]{:S(2)}) collective-permute-start(bf16[48,256]{1,0:T(8,128)(2,1)S(1)} %broadcast_select_fusion.2), channel_id=1, source_target_pairs={{0,4},{4,0},{8,12},{12,8},{16,20},{20,16},{24,28},{28,24},{32,36},... | collective-permute-start | bytes 73736 | tf_op jit(solution)/shard_map/ppermute | solution.py:388

commit v5 on v4

--- a/solution.py
+++ b/solution.py
@@ -242,8 +242,8 @@
         own = own + dot(rows, own_ref[at, :])
         sib = sib + dot(rows, sib_ref[at, :])
     half = own_ref.shape[1]
-    out_ref[:, :half] = jnp.where(core == 0, own, sib)
-    out_ref[:, half:] = jnp.where(core == 0, sib, own)
+    out_ref[:, :half] = jnp.where(core == 0, own, sib).astype(bf16)
+    out_ref[:, half:] = jnp.where(core == 0, sib, own).astype(bf16)
 
 
 def gate_up_kernel(
@@ -280,7 +280,9 @@
         copy.start()
     half = g_own.shape[0]
     chips = out_ref.shape[0]
-    stream = res_ref[...].astype(f32) + ((p0[...] + p1[...]) + (p2[...] + p3[...]))
+    stream = res_ref[...].astype(f32) + (
+        (p0[...].astype(f32) + p1[...].astype(f32)) + (p2[...].astype(f32) + p3[...].astype(f32))
+    )
     stream_ref[...] = stream
     scaled = stream * gain_ref[0:1, :].astype(f32)
     mine = jnp.where(core == 0, scaled[:, :half], scaled[:, half:]).astype(bf16)
@@ -469,7 +471,7 @@
         project_kernel,
         in_specs=[smem, vmem, vmem, vmem],
         out_specs=vmem,
-        out_shape=jax.ShapeDtypeStruct((tokens, 2 * width), f32),
+        out_shape=jax.ShapeDtypeStruct((tokens, 2 * width), bf16),
         scratch_shapes=[pltpu.VMEM((chips * ROWS, HD), f32)],
         compiler_params=params,
         name="project",
@@ -502,7 +504,8 @@
     )(where, got_shares, w_down_own, w_down_sib)
 
     lowered = jnp.sum(over_chips(down).astype(f32), axis=0)
-    l0, l1, l2, l3 = heads(lowered)
+    rounded = lax.reduce_precision(lowered, 8, 7).astype(bf16)
+    l0, l1, l2, l3 = (each.astype(f32) for each in heads(rounded))
     final = (stream + ((l0 + l1) + (l2 + l3))).astype(bf16)
     low, high = final[:, :width], final[:, width:]
     keep = jnp.where(core == 0, low, high)

time: 117 us -> 115 us (0.983)
  other arithmetic: 2.34 us -> 0.91 us
    ppermute x6, waiting for transfers between devices: 8.31 us -> 6.73 us  [heads(): lax.ppermute(x, 'head', [(i, i ^ s) for i in range(4)])]
    select_n x2, other arithmetic: 1.45 us -> 0.02 us  [in_order(): low = jnp.where(core == 0, own, sib)]
    all_to_all x3, waiting for transfers between devices: 17.6 us -> 19 us  [over_chips(): lax.all_to_all(x, 'seq', split_axis=0, concat_axis=0, tiled=True, axis_in...]
  transfers between devices with their start and end apart: 16 -> 16, of which waited for: 9 -> 9; matrix products, arithmetic and copies ran while one was open for 3% -> 2% of each run, Pallas kernels for 7% -> 7%
where the time goes in v5:
time: 115 us
  starting transfers between devices  32.8 us (29%)
  waiting for transfers between devices  28.1 us (24%)
  blocking collectives  27 us (23%)
  Pallas kernels  20.6 us (18%)
  local copies, waits for them, and re-layouts  4.39 us (4%)
    all_to_all x2, blocking collectives, over_chips(): lax.all_to_all(x, 'seq', split_axis=0, concat_axis=0, tiled=True, axis_in...  27 us
    all_to_all x3, waiting for transfers between devices, over_chips(): lax.all_to_all(x, 'seq', split_axis=0, concat_axis=0, tiled=True, axis_in...  19 us
    all_to_all x3, starting transfers between devices, over_chips(): lax.all_to_all(x, 'seq', split_axis=0, concat_axis=0, tiled=True, axis_in...  14.7 us
    ppermute x7, starting transfers between devices, sibling(): return lax.ppermute(x, 'seq', swap)  11.4 us
    ppermute x6, waiting for transfers between devices, heads(): lax.ppermute(x, 'head', [(i, i ^ s) for i in range(4)])  6.73 us
    ppermute x6, starting transfers between devices, heads(): lax.ppermute(x, 'head', [(i, i ^ s) for i in range(4)])  6.71 us
    pallas_call x1, Pallas kernels, on_device(): pl.pallas_call(attend_kernel, in_specs=[smem, smem, vmem, hbm, hbm, pl.Bl...  6.13 us
    pallas_call x1, Pallas kernels, on_device(): pl.pallas_call(gather_kernel, in_specs=[smem, smem, vmem, vmem, hbm, hbm]...  5.51 us
  transfers between devices with their start and end apart: 16, of which 9 were waited for; matrix products, arithmetic and copies ran while one was open for 2% of the time, Pallas kernels for 7%

profile of v5, /device:TPU:1, one launch (start us, length us, event | category | flops | bytes accessed | tf_op | source)
XLA Modules:
  0.0 114.7 jit_solution(9680531475199603651)
XLA Ops:
  0.6 0.7 reshape.37.q_ref
  1.5 0.8 copy-done.2
  2.2 0.7 copy-done.3
  2.9 5.5 %gather.1 = (bf16[16,512,256]{2,1,0:T(8,128)(2,1)}, bf16[16,48,128]{2,1,0:T(8,128)(2,1)}, s32[32]{0:T(128)S(1)}) custom-call(s32[2]{0:T(128)S(1)} %pad_add_fusion.where_ref, s32[2,32]{1,0:T(2,128)S(1)} %bitcast.13, s32[32,2,128]{2,1,0:T(2,128)S(1)} %copy-done.2, bf16[48,128]{1,0:T(8,128)(2,1)S(1)} %reshape.37.q_ref, bf16[32,512,256]{2,1,0:T(8,128)(2,1)} %k_ref.3, ...), custom_call_target="tpu_custom_call" | custom-call | tf_op jit(solution)/shard_map/gather/pallas_call | solution.py:410
  8.5 1.6 %collective-permute-start = (bf16[16,512,256]{2,1,0:T(8,128)(2,1)}, bf16[16,512,256]{2,1,0:T(8,128)(2,1)}, u32[]{:S(2)}, u32[]{:S(2)}) collective-permute-start(bf16[16,512,256]{2,1,0:T(8,128)(2,1)} %get-tuple-element.11), channel_id=1, source_target_pairs={{0,4},{4,0},{8,12},{12,8},{16,20},{20,16},{24,28},{28,24},{32,36},... | collective-permute-start | bytes 12582920 | tf_op jit(solution)/shard_map/ppermute | solution.py:390
  11.1 7.7 %all-to-all-start = ((bf16[16,48,128]{2,1,0:T(8,128)(2,1)}), bf16[16,48,128]{2,1,0:T(8,128)(2,1)S(1)}, u32[]{:S(2)}, u32[]{:S(2)}) async-start(bf16[16,48,128]{2,1,0:T(8,128)(2,1)} %get-tuple-element.10), calls=%async_computation | async-start | bytes 393216 | tf_op jit(solution)/shard_map/all_to_all | solution.py:385
  19.0 0.6 pad_maximum_fusion.2
  19.7 2.1 %collective-permute-done.sib_hbm = bf16[16,512,256]{2,1,0:T(8,128)(2,1)} collective-permute-done((bf16[16,512,256]{2,1,0:T(8,128)(2,1)}, bf16[16,512,256]{2,1,0:T(8,128)(2,1)}, u32[]{:S(2)}, u32[]{:S(2)}) %collective-permute-start) | collective-permute-done | bytes 4194336 | tf_op jit(solution)/shard_map/ppermute | solution.py:390
  22.1 4.4 %all-to-all-done.q_ref = bf16[16,48,128]{2,1,0:T(8,128)(2,1)S(1)} async-done(((bf16[16,48,128]{2,1,0:T(8,128)(2,1)}), bf16[16,48,128]{2,1,0:T(8,128)(2,1)S(1)}, u32[]{:S(2)}, u32[]{:S(2)}) %all-to-all-start) | async-done | bytes 196640 | tf_op jit(solution)/shard_map/all_to_all | solution.py:385
  26.6 6.1 %attend.1 = bf16[16,64,128]{2,1,0:T(8,128)(2,1)} custom-call(s32[2]{0:T(128)S(1)} %pad_add_fusion.where_ref, s32[32]{0:T(128)S(1)} %get-tuple-element.9.codes_ref, bf16[16,48,128]{2,1,0:T(8,128)(2,1)S(1)} %all-to-all-done.q_ref, bf16[32,512,256]{2,1,0:T(8,128)(2,1)} %k_ref.3, bf16[32,512,256]{2,1,0:T(8,128)(2,1)} %v_ref.3, ...), custom_call_target="tpu_custom_call" | custom-call | tf_op jit(solution)/shard_map/attend/pallas_call | solution.py:433
  32.7 3.5 %all-to-all-start.1 = ((bf16[16,64,128]{2,1,0:T(8,128)(2,1)}), bf16[16,64,128]{2,1,0:T(8,128)(2,1)S(1)}, u32[]{:S(2)}, u32[]{:S(2)}) async-start(bf16[16,64,128]{2,1,0:T(8,128)(2,1)} %attend.1), calls=%async_computation.1 | async-start | bytes 524288 | tf_op jit(solution)/shard_map/all_to_all | solution.py:385
  36.3 7.5 %all-to-all-done.1.got_ref = bf16[16,64,128]{2,1,0:T(8,128)(2,1)S(1)} async-done(((bf16[16,64,128]{2,1,0:T(8,128)(2,1)}), bf16[16,64,128]{2,1,0:T(8,128)(2,1)S(1)}, u32[]{:S(2)}, u32[]{:S(2)}) %all-to-all-start.1) | async-done | bytes 262176 | tf_op jit(solution)/shard_map/all_to_all | solution.py:385
  43.8 0.6 combine.1
  44.4 0.7 broadcast_in_dim.4
  45.1 3.5 %all-to-all-start.2 = ((bf16[16,48,128]{2,1,0:T(8,128)(2,1)}), bf16[16,48,128]{2,1,0:T(8,128)(2,1)S(1)}, u32[]{:S(2)}, u32[]{:S(2)}) async-start(bf16[16,48,128]{2,1,0:T(8,128)(2,1)} %broadcast_in_dim.4), calls=%async_computation.2 | async-start | bytes 393216 | tf_op jit(solution)/shard_map/all_to_all | solution.py:385
  48.7 7.1 %all-to-all-done.2.got_ref = bf16[16,48,128]{2,1,0:T(8,128)(2,1)S(1)} async-done(((bf16[16,48,128]{2,1,0:T(8,128)(2,1)}), bf16[16,48,128]{2,1,0:T(8,128)(2,1)S(1)}, u32[]{:S(2)}, u32[]{:S(2)}) %all-to-all-start.2) | async-done | bytes 196640 | tf_op jit(solution)/shard_map/all_to_all | solution.py:385
  55.8 1.6 %project.1.p0 = bf16[48,512]{1,0:T(8,128)(2,1)S(1)} custom-call(s32[2]{0:T(128)S(1)} %pad_add_fusion.where_ref, bf16[16,48,128]{2,1,0:T(8,128)(2,1)S(1)} %all-to-all-done.2.got_ref, bf16[2048,256]{1,0:T(8,128)(2,1)S(1)} %copy-done.1, bf16[2048,256]{1,0:T(8,128)(2,1)} %collective-permute-done.1.sib_ref), custom_call_target="tpu_custom_call" | custom-call | tf_op jit(solution)/shard_map/project/pallas_call | solution.py:470
  57.4 1.2 %collective-permute-start.2 = (bf16[48,512]{1,0:T(8,128)(2,1)S(1)}, bf16[48,512]{1,0:T(8,128)(2,1)S(1)}, u32[]{:S(2)}, u32[]{:S(2)}) collective-permute-start(bf16[48,512]{1,0:T(8,128)(2,1)S(1)} %project.1.p0), channel_id=1, source_target_pairs={{0,1},{1,0},{2,3},{3,2},{4,5},{5,4},{6,7},{7,6},{8,9},{9,8},{10,11... | collective-permute-start | bytes 147464 | tf_op jit(solution)/shard_map/ppermute | solution.py:393
  58.6 2.8 %collective-permute-start.3 = (bf16[48,512]{1,0:T(8,128)(2,1)S(1)}, bf16[48,512]{1,0:T(8,128)(2,1)S(1)}, u32[]{:S(2)}, u32[]{:S(2)}) collective-permute-start(bf16[48,512]{1,0:T(8,128)(2,1)S(1)} %project.1.p0), channel_id=1, source_target_pairs={{0,2},{1,3},{2,0},{3,1},{4,6},{5,7},{6,4},{7,5},{8,10},{9,11},{10,... | collective-permute-start | bytes 147464 | tf_op jit(solution)/shard_map/ppermute | solution.py:393
  61.5 2.0 %collective-permute-done.3.p2 = bf16[48,512]{1,0:T(8,128)(2,1)S(1)} collective-permute-done((bf16[48,512]{1,0:T(8,128)(2,1)S(1)}, bf16[48,512]{1,0:T(8,128)(2,1)S(1)}, u32[]{:S(2)}, u32[]{:S(2)}) %collective-permute-start.3) | collective-permute-done | bytes 49184 | tf_op jit(solution)/shard_map/ppermute | solution.py:393
  63.4 2.2 %collective-permute-done.4.p3 = bf16[48,512]{1,0:T(8,128)(2,1)S(1)} collective-permute-done((bf16[48,512]{1,0:T(8,128)(2,1)S(1)}, bf16[48,512]{1,0:T(8,128)(2,1)S(1)}, u32[]{:S(2)}, u32[]{:S(2)}) %collective-permute-start.4) | collective-permute-done | bytes 49184 | tf_op jit(solution)/shard_map/ppermute | solution.py:393
  65.6 5.2 %gate_up.1 = (bf16[16,208,128]{2,1,0:T(8,128)(2,1)S(1)}, f32[48,512]{1,0:T(8,128)S(1)}, bf16[128,8192]{1,0:T(8,128)(2,1)S(1)}, bf16[128,8192]{1,0:T(8,128)(2,1)S(1)}) custom-call(s32[2]{0:T(128)S(1)} %pad_add_fusion.where_ref, bf16[48,512]{1,0:T(8,128)(2,1)S(1)} %project.1.p0, bf16[48,512]{1,0:T(8,128)(2,1)S(1)} %collective-permute-done.2.p1, ...), custom_call_target="tpu_custom_call" | custom-call | tf_op jit(solution)/shard_map/gate_up/pallas_call | solution.py:481
  70.8 13.9 %all_to_all.25.got_ref = bf16[16,208,128]{2,1,0:T(8,128)(2,1)S(1)} all-to-all(bf16[16,208,128]{2,1,0:T(8,128)(2,1)S(1)} %get-tuple-element.13), channel_id=1, replica_groups={{0,8,16,24,32,40,48,56,64,72,80,88,96,104,112,120},{4,12,20,28,36,44,52..., dimensions={0} | all-to-all | bytes 1703936 | tf_op jit(solution)/shard_map/all_to_all | solution.py:385
  84.6 1.5 %down.1 = bf16[16,48,512]{2,1,0:T(8,128)(2,1)S(1)} custom-call(s32[2]{0:T(128)S(1)} %pad_add_fusion.where_ref, bf16[16,208,128]{2,1,0:T(8,128)(2,1)S(1)} %all_to_all.25.got_ref, bf16[128,8192]{1,0:T(8,128)(2,1)S(1)} %get-tuple-element.14.own_ref, bf16[128,8192]{1,0:T(8,128)(2,1)S(1)} %get-tuple-element.15.sib_ref), custom_call_target="tpu_custom_call" | custom-call | tf_op jit(solution)/shard_map/down/pallas_call | solution.py:497
  86.1 13.2 %all_to_all.26 = bf16[16,48,512]{2,1,0:T(8,128)(2,1)S(1)} all-to-all(bf16[16,48,512]{2,1,0:T(8,128)(2,1)S(1)} %down.1), channel_id=1, replica_groups={{0,8,16,24,32,40,48,56,64,72,80,88,96,104,112,120},{4,12,20,28,36,44,52..., dimensions={0} | all-to-all | bytes 1572864 | tf_op jit(solution)/shard_map/all_to_all | solution.py:385
  99.9 0.6 collective-permute-start.11
  100.5 1.6 %collective-permute-start.9 = (bf16[48,512]{1,0:T(8,128)(2,1)S(1)}, bf16[48,512]{1,0:T(8,128)(2,1)S(1)}, u32[]{:S(2)}, u32[]{:S(2)}) collective-permute-start(bf16[48,512]{1,0:T(8,128)(2,1)S(1)} %reduce-precision_convert_fusion), channel_id=1, source_target_pairs={{0,1},{1,0},{2,3},{3,2},{4,5},{5,4},{6,7},{7,6},{8,9},{9,8},{10,11... | collective-permute-start | bytes 147464 | tf_op jit(solution)/shard_map/ppermute | solution.py:393
  102.1 2.1 %collective-permute-done.10 = bf16[48,512]{1,0:T(8,128)(2,1)S(1)} collective-permute-done((bf16[48,512]{1,0:T(8,128)(2,1)S(1)}, bf16[48,512]{1,0:T(8,128)(2,1)S(1)}, u32[]{:S(2)}, u32[]{:S(2)}) %collective-permute-start.10) | collective-permute-done | bytes 49184 | tf_op jit(solution)/shard_map/ppermute | solution.py:393
  104.2 0.5 collective-permute-done.11
  104.8 8.3 %collective-permute-start.12 = (bf16[48,256]{1,0:T(8,128)(2,1)S(1)}, bf16[48,256]{1,0:T(8,128)(2,1)S(1)}, u32[]{:S(2)}, u32[]{:S(2)}) collective-permute-start(bf16[48,256]{1,0:T(8,128)(2,1)S(1)} %broadcast_select_fusion.2), channel_id=1, source_target_pairs={{0,4},{4,0},{8,12},{12,8},{16,20},{20,16},{24,28},{28,24},{32,36},... | collective-permute-start | bytes 73736 | tf_op jit(solution)/shard_map/ppermute | solution.py:390
  113.2 0.6 reshape.40
  114.1 0.6 reshape.46
  (48 shorter events, 2.7 us)
Async XLA Ops:
  1.5 0.8 copy-start.2
  2.2 0.7 copy-start.3
  2.9 7.2 %copy-start = (bf16[256,4096]{1,0:T(8,128)(2,1)S(1)}, bf16[256,4096]{1,0:T(8,128)(2,1)}, u32[]{:S(2)}) copy-start(bf16[256,4096]{1,0:T(8,128)(2,1)} %g_own_hbm.1) | copy-start | bytes 6291460
  2.9 7.8 %copy-start.1 = (bf16[2048,256]{1,0:T(8,128)(2,1)S(1)}, bf16[2048,256]{1,0:T(8,128)(2,1)}, u32[]{:S(2)}) copy-start(bf16[2048,256]{1,0:T(8,128)(2,1)} %own_ref.1) | copy-start | bytes 3145732
  2.9 15.9 %copy-start.4 = (bf16[3,32,256]{2,1,0:T(8,128)(2,1)S(1)}, bf16[3,32,256]{2,1,0:T(8,128)(2,1)}, u32[]{:S(2)}) copy-start(bf16[3,32,256]{2,1,0:T(8,128)(2,1)} %param.20) | copy-start | bytes 147460
  2.9 16.1 %copy-start.5 = (bf16[256]{0:T(256)(128)(2,1)S(1)}, bf16[256]{0:T(256)(128)(2,1)}, u32[]{:S(2)}) copy-start(bf16[256]{0:T(256)(128)(2,1)} %param.21) | copy-start | bytes 1540
  2.9 19.2 %copy-start.6 = (bf16[3,1,256]{2,0,1:T(4,128)(2,1)S(1)}, bf16[3,1,256]{2,0,1:T(4,128)(2,1)}, u32[]{:S(2)}) copy-start(bf16[3,1,256]{2,0,1:T(4,128)(2,1)} %param.18) | copy-start | bytes 4612
  2.9 19.2 %copy-start.7 = (bf16[3,1,256]{2,0,1:T(4,128)(2,1)S(1)}, bf16[3,1,256]{2,0,1:T(4,128)(2,1)}, u32[]{:S(2)}) copy-start(bf16[3,1,256]{2,0,1:T(4,128)(2,1)} %param.19) | copy-start | bytes 4612
  8.5 13.3 %collective-permute-start = (bf16[16,512,256]{2,1,0:T(8,128)(2,1)}, bf16[16,512,256]{2,1,0:T(8,128)(2,1)}, u32[]{:S(2)}, u32[]{:S(2)}) collective-permute-start(bf16[16,512,256]{2,1,0:T(8,128)(2,1)} %get-tuple-element.11), channel_id=1, source_target_pairs={{0,4},{4,0},{8,12},{12,8},{16,20},{20,16},{24,28},{28,24},{32,36},... | collective-permute-start | bytes 12582920 | tf_op jit(solution)/shard_map/ppermute | solution.py:390
  10.1 51.3 %collective-permute-start.6 = (bf16[256,4096]{1,0:T(8,128)(2,1)S(1)}, bf16[256,4096]{1,0:T(8,128)(2,1)}, u32[]{:S(2)}, u32[]{:S(2)}) collective-permute-start(bf16[256,4096]{1,0:T(8,128)(2,1)S(1)} %copy-done), channel_id=1, source_target_pairs={{0,4},{4,0},{8,12},{12,8},{16,20},{20,16},{24,28},{28,24},{32,36},... | collective-permute-start | bytes 6291464 | tf_op jit(solution)/shard_map/ppermute | solution.py:390
  10.2 51.2 %collective-permute-start.7 = (bf16[256,4096]{1,0:T(8,128)(2,1)}, bf16[256,4096]{1,0:T(8,128)(2,1)}, u32[]{:S(2)}, u32[]{:S(2)}) collective-permute-start(bf16[256,4096]{1,0:T(8,128)(2,1)} %u_own_hbm.1), channel_id=1, source_target_pairs={{0,4},{4,0},{8,12},{12,8},{16,20},{20,16},{24,28},{28,24},{32,36},... | collective-permute-start | bytes 6291464 | tf_op jit(solution)/shard_map/ppermute | solution.py:390
  10.6 50.8 %collective-permute-start.8 = (bf16[128,8192]{1,0:T(8,128)(2,1)}, bf16[128,8192]{1,0:T(8,128)(2,1)}, u32[]{:S(2)}, u32[]{:S(2)}) collective-permute-start(bf16[128,8192]{1,0:T(8,128)(2,1)} %d_own_hbm.1), channel_id=1, source_target_pairs={{0,4},{4,0},{8,12},{12,8},{16,20},{20,16},{24,28},{28,24},{32,36},... | collective-permute-start | bytes 6291464 | tf_op jit(solution)/shard_map/ppermute | solution.py:390
  10.7 37.9 %collective-permute-start.1 = (bf16[2048,256]{1,0:T(8,128)(2,1)S(1)}, bf16[2048,256]{1,0:T(8,128)(2,1)}, u32[]{:S(2)}, u32[]{:S(2)}) collective-permute-start(bf16[2048,256]{1,0:T(8,128)(2,1)S(1)} %copy-done.1), channel_id=1, source_target_pairs={{0,4},{4,0},{8,12},{12,8},{16,20},{20,16},{24,28},{28,24},{32,36},... | collective-permute-start | bytes 3145736 | tf_op jit(solution)/shard_map/ppermute | solution.py:390
  11.1 15.4 %all-to-all-start = ((bf16[16,48,128]{2,1,0:T(8,128)(2,1)}), bf16[16,48,128]{2,1,0:T(8,128)(2,1)S(1)}, u32[]{:S(2)}, u32[]{:S(2)}) async-start(bf16[16,48,128]{2,1,0:T(8,128)(2,1)} %get-tuple-element.10), calls=%async_computation | async-start | bytes 393216 | tf_op jit(solution)/shard_map/all_to_all | solution.py:385
  21.7 14.5 %collective-permute-start.5 = (bf16[64,256]{1,0:T(8,128)(2,1)}, bf16[64,256]{1,0:T(8,128)(2,1)S(1)}, u32[]{:S(2)}, u32[]{:S(2)}) collective-permute-start(bf16[64,256]{1,0:T(8,128)(2,1)} %pad_maximum_fusion.2), channel_id=1, source_target_pairs={{0,4},{4,0},{8,12},{12,8},{16,20},{20,16},{24,28},{28,24},{32,36},... | collective-permute-start | bytes 98312 | tf_op jit(solution)/shard_map/ppermute | solution.py:390
  32.7 11.1 %all-to-all-start.1 = ((bf16[16,64,128]{2,1,0:T(8,128)(2,1)}), bf16[16,64,128]{2,1,0:T(8,128)(2,1)S(1)}, u32[]{:S(2)}, u32[]{:S(2)}) async-start(bf16[16,64,128]{2,1,0:T(8,128)(2,1)} %attend.1), calls=%async_computation.1 | async-start | bytes 524288 | tf_op jit(solution)/shard_map/all_to_all | solution.py:385
  45.1 10.7 %all-to-all-start.2 = ((bf16[16,48,128]{2,1,0:T(8,128)(2,1)}), bf16[16,48,128]{2,1,0:T(8,128)(2,1)S(1)}, u32[]{:S(2)}, u32[]{:S(2)}) async-start(bf16[16,48,128]{2,1,0:T(8,128)(2,1)} %broadcast_in_dim.4), calls=%async_computation.2 | async-start | bytes 393216 | tf_op jit(solution)/shard_map/all_to_all | solution.py:385
  57.4 4.0 %collective-permute-start.2 = (bf16[48,512]{1,0:T(8,128)(2,1)S(1)}, bf16[48,512]{1,0:T(8,128)(2,1)S(1)}, u32[]{:S(2)}, u32[]{:S(2)}) collective-permute-start(bf16[48,512]{1,0:T(8,128)(2,1)S(1)} %project.1.p0), channel_id=1, source_target_pairs={{0,1},{1,0},{2,3},{3,2},{4,5},{5,4},{6,7},{7,6},{8,9},{9,8},{10,11... | collective-permute-start | bytes 147464 | tf_op jit(solution)/shard_map/ppermute | solution.py:393
  58.6 4.8 %collective-permute-start.3 = (bf16[48,512]{1,0:T(8,128)(2,1)S(1)}, bf16[48,512]{1,0:T(8,128)(2,1)S(1)}, u32[]{:S(2)}, u32[]{:S(2)}) collective-permute-start(bf16[48,512]{1,0:T(8,128)(2,1)S(1)} %project.1.p0), channel_id=1, source_target_pairs={{0,2},{1,3},{2,0},{3,1},{4,6},{5,7},{6,4},{7,5},{8,10},{9,11},{10,... | collective-permute-start | bytes 147464 | tf_op jit(solution)/shard_map/ppermute | solution.py:393
  61.4 4.2 %collective-permute-start.4 = (bf16[48,512]{1,0:T(8,128)(2,1)S(1)}, bf16[48,512]{1,0:T(8,128)(2,1)S(1)}, u32[]{:S(2)}, u32[]{:S(2)}) collective-permute-start(bf16[48,512]{1,0:T(8,128)(2,1)S(1)} %project.1.p0), channel_id=1, source_target_pairs={{0,3},{1,2},{2,1},{3,0},{4,7},{5,6},{6,5},{7,4},{8,11},{9,10},{10,... | collective-permute-start | bytes 147464 | tf_op jit(solution)/shard_map/ppermute | solution.py:393
  99.4 4.8 %collective-permute-start.10 = (bf16[48,512]{1,0:T(8,128)(2,1)S(1)}, bf16[48,512]{1,0:T(8,128)(2,1)S(1)}, u32[]{:S(2)}, u32[]{:S(2)}) collective-permute-start(bf16[48,512]{1,0:T(8,128)(2,1)S(1)} %reduce-precision_convert_fusion), channel_id=1, source_target_pairs={{0,2},{1,3},{2,0},{3,1},{4,6},{5,7},{6,4},{7,5},{8,10},{9,11},{10,... | collective-permute-start | bytes 147464 | tf_op jit(solution)/shard_map/ppermute | solution.py:393
  99.9 4.9 %collective-permute-start.11 = (bf16[48,512]{1,0:T(8,128)(2,1)S(1)}, bf16[48,512]{1,0:T(8,128)(2,1)S(1)}, u32[]{:S(2)}, u32[]{:S(2)}) collective-permute-start(bf16[48,512]{1,0:T(8,128)(2,1)S(1)} %reduce-precision_convert_fusion), channel_id=1, source_target_pairs={{0,3},{1,2},{2,1},{3,0},{4,7},{5,6},{6,5},{7,4},{8,11},{9,10},{10,... | collective-permute-start | bytes 147464 | tf_op jit(solution)/shard_map/ppermute | solution.py:393
  100.5 4.3 %collective-permute-start.9 = (bf16[48,512]{1,0:T(8,128)(2,1)S(1)}, bf16[48,512]{1,0:T(8,128)(2,1)S(1)}, u32[]{:S(2)}, u32[]{:S(2)}) collective-permute-start(bf16[48,512]{1,0:T(8,128)(2,1)S(1)} %reduce-precision_convert_fusion), channel_id=1, source_target_pairs={{0,1},{1,0},{2,3},{3,2},{4,5},{5,4},{6,7},{7,6},{8,9},{9,8},{10,11... | collective-permute-start | bytes 147464 | tf_op jit(solution)/shard_map/ppermute | solution.py:393
  104.8 9.2 %collective-permute-start.12 = (bf16[48,256]{1,0:T(8,128)(2,1)S(1)}, bf16[48,256]{1,0:T(8,128)(2,1)S(1)}, u32[]{:S(2)}, u32[]{:S(2)}) collective-permute-start(bf16[48,256]{1,0:T(8,128)(2,1)S(1)} %broadcast_select_fusion.2), channel_id=1, source_target_pairs={{0,4},{4,0},{8,12},{12,8},{16,20},{20,16},{24,28},{28,24},{32,36},... | collective-permute-start | bytes 73736 | tf_op jit(solution)/shard_map/ppermute | solution.py:390

commit v6 on v5

--- a/solution.py
+++ b/solution.py
@@ -422,8 +422,8 @@
             pltpu.VMEM(tile, bf16),
             dma,
             dma((chips,)),
-            dma((groups,)),
-            dma((groups,)),
+            dma((2 * groups,)),
+            dma((2 * groups,)),
         ],
         compiler_params=pltpu.CompilerParams(vmem_limit_bytes=50 * MIB),
         name="gather",

time: 115 us -> 116 us (level)
  no operation moved by 1% of the time
where the time goes in v6:
time: 116 us; the launch traced here: 115 us
  starting transfers between devices  33.1 us (29%)
  waiting for transfers between devices  28.1 us (24%)
  blocking collectives  27 us (23%)
  Pallas kernels  20.6 us (18%)
  local copies, waits for them, and re-layouts  4.39 us (4%)
    all_to_all x2, blocking collectives, over_chips(): lax.all_to_all(x, 'seq', split_axis=0, concat_axis=0, tiled=True, axis_in...  27 us
    all_to_all x3, waiting for transfers between devices, over_chips(): lax.all_to_all(x, 'seq', split_axis=0, concat_axis=0, tiled=True, axis_in...  19 us
    all_to_all x3, starting transfers between devices, over_chips(): lax.all_to_all(x, 'seq', split_axis=0, concat_axis=0, tiled=True, axis_in...  14.7 us
    ppermute x7, starting transfers between devices, sibling(): return lax.ppermute(x, 'seq', swap)  11.5 us
    ppermute x6, starting transfers between devices, heads(): lax.ppermute(x, 'head', [(i, i ^ s) for i in range(4)])  6.91 us
    ppermute x6, waiting for transfers between devices, heads(): lax.ppermute(x, 'head', [(i, i ^ s) for i in range(4)])  6.73 us
    pallas_call x1, Pallas kernels, on_device(): pl.pallas_call(attend_kernel, in_specs=[smem, smem, vmem, hbm, hbm, pl.Bl...  6.01 us
    pallas_call x1, Pallas kernels, on_device(): pl.pallas_call(gather_kernel, in_specs=[smem, smem, vmem, vmem, hbm, hbm]...  5.65 us
  transfers between devices with their start and end apart: 16, of which 9 were waited for; matrix products, arithmetic and copies ran while one was open for 2% of the time, Pallas kernels for 7%

profile of v6, /device:TPU:1, one launch (start us, length us, event | category | flops | bytes accessed | tf_op | source)
XLA Modules:
  0.0 115.0 jit_solution(8025619967855013780)
XLA Ops:
  0.6 0.7 reshape.37.q_ref
  1.5 0.8 copy-done.2
  2.2 0.7 copy-done.3
  2.9 5.6 %gather.1 = (bf16[16,512,256]{2,1,0:T(8,128)(2,1)}, bf16[16,48,128]{2,1,0:T(8,128)(2,1)}, s32[32]{0:T(128)S(1)}) custom-call(s32[2]{0:T(128)S(1)} %pad_add_fusion.where_ref, s32[2,32]{1,0:T(2,128)S(1)} %bitcast.13, s32[32,2,128]{2,1,0:T(2,128)S(1)} %copy-done.2, bf16[48,128]{1,0:T(8,128)(2,1)S(1)} %reshape.37.q_ref, bf16[32,512,256]{2,1,0:T(8,128)(2,1)} %k_ref.3, ...), custom_call_target="tpu_custom_call" | custom-call | tf_op jit(solution)/shard_map/gather/pallas_call | solution.py:410
  8.6 1.7 %collective-permute-start = (bf16[16,512,256]{2,1,0:T(8,128)(2,1)}, bf16[16,512,256]{2,1,0:T(8,128)(2,1)}, u32[]{:S(2)}, u32[]{:S(2)}) collective-permute-start(bf16[16,512,256]{2,1,0:T(8,128)(2,1)} %get-tuple-element.11), channel_id=1, source_target_pairs={{0,4},{4,0},{8,12},{12,8},{16,20},{20,16},{24,28},{28,24},{32,36},... | collective-permute-start | bytes 12582920 | tf_op jit(solution)/shard_map/ppermute | solution.py:390
  11.3 7.7 %all-to-all-start = ((bf16[16,48,128]{2,1,0:T(8,128)(2,1)}), bf16[16,48,128]{2,1,0:T(8,128)(2,1)S(1)}, u32[]{:S(2)}, u32[]{:S(2)}) async-start(bf16[16,48,128]{2,1,0:T(8,128)(2,1)} %get-tuple-element.10), calls=%async_computation | async-start | bytes 393216 | tf_op jit(solution)/shard_map/all_to_all | solution.py:385
  19.2 0.6 pad_maximum_fusion.2
  19.9 2.1 %collective-permute-done.sib_hbm = bf16[16,512,256]{2,1,0:T(8,128)(2,1)} collective-permute-done((bf16[16,512,256]{2,1,0:T(8,128)(2,1)}, bf16[16,512,256]{2,1,0:T(8,128)(2,1)}, u32[]{:S(2)}, u32[]{:S(2)}) %collective-permute-start) | collective-permute-done | bytes 4194336 | tf_op jit(solution)/shard_map/ppermute | solution.py:390
  22.4 4.4 %all-to-all-done.q_ref = bf16[16,48,128]{2,1,0:T(8,128)(2,1)S(1)} async-done(((bf16[16,48,128]{2,1,0:T(8,128)(2,1)}), bf16[16,48,128]{2,1,0:T(8,128)(2,1)S(1)}, u32[]{:S(2)}, u32[]{:S(2)}) %all-to-all-start) | async-done | bytes 196640 | tf_op jit(solution)/shard_map/all_to_all | solution.py:385
  26.8 6.0 %attend.1 = bf16[16,64,128]{2,1,0:T(8,128)(2,1)} custom-call(s32[2]{0:T(128)S(1)} %pad_add_fusion.where_ref, s32[32]{0:T(128)S(1)} %get-tuple-element.9.codes_ref, bf16[16,48,128]{2,1,0:T(8,128)(2,1)S(1)} %all-to-all-done.q_ref, bf16[32,512,256]{2,1,0:T(8,128)(2,1)} %k_ref.3, bf16[32,512,256]{2,1,0:T(8,128)(2,1)} %v_ref.3, ...), custom_call_target="tpu_custom_call" | custom-call | tf_op jit(solution)/shard_map/attend/pallas_call | solution.py:433
  32.8 3.5 %all-to-all-start.1 = ((bf16[16,64,128]{2,1,0:T(8,128)(2,1)}), bf16[16,64,128]{2,1,0:T(8,128)(2,1)S(1)}, u32[]{:S(2)}, u32[]{:S(2)}) async-start(bf16[16,64,128]{2,1,0:T(8,128)(2,1)} %attend.1), calls=%async_computation.1 | async-start | bytes 524288 | tf_op jit(solution)/shard_map/all_to_all | solution.py:385
  36.4 7.5 %all-to-all-done.1.got_ref = bf16[16,64,128]{2,1,0:T(8,128)(2,1)S(1)} async-done(((bf16[16,64,128]{2,1,0:T(8,128)(2,1)}), bf16[16,64,128]{2,1,0:T(8,128)(2,1)S(1)}, u32[]{:S(2)}, u32[]{:S(2)}) %all-to-all-start.1) | async-done | bytes 262176 | tf_op jit(solution)/shard_map/all_to_all | solution.py:385
  43.8 0.6 combine.1
  44.5 0.7 broadcast_in_dim.4
  45.2 3.5 %all-to-all-start.2 = ((bf16[16,48,128]{2,1,0:T(8,128)(2,1)}), bf16[16,48,128]{2,1,0:T(8,128)(2,1)S(1)}, u32[]{:S(2)}, u32[]{:S(2)}) async-start(bf16[16,48,128]{2,1,0:T(8,128)(2,1)} %broadcast_in_dim.4), calls=%async_computation.2 | async-start | bytes 393216 | tf_op jit(solution)/shard_map/all_to_all | solution.py:385
  48.8 7.1 %all-to-all-done.2.got_ref = bf16[16,48,128]{2,1,0:T(8,128)(2,1)S(1)} async-done(((bf16[16,48,128]{2,1,0:T(8,128)(2,1)}), bf16[16,48,128]{2,1,0:T(8,128)(2,1)S(1)}, u32[]{:S(2)}, u32[]{:S(2)}) %all-to-all-start.2) | async-done | bytes 196640 | tf_op jit(solution)/shard_map/all_to_all | solution.py:385
  55.9 1.6 %project.1.p0 = bf16[48,512]{1,0:T(8,128)(2,1)S(1)} custom-call(s32[2]{0:T(128)S(1)} %pad_add_fusion.where_ref, bf16[16,48,128]{2,1,0:T(8,128)(2,1)S(1)} %all-to-all-done.2.got_ref, bf16[2048,256]{1,0:T(8,128)(2,1)S(1)} %copy-done.1, bf16[2048,256]{1,0:T(8,128)(2,1)} %collective-permute-done.1.sib_ref), custom_call_target="tpu_custom_call" | custom-call | tf_op jit(solution)/shard_map/project/pallas_call | solution.py:470
  57.5 1.6 %collective-permute-start.2 = (bf16[48,512]{1,0:T(8,128)(2,1)S(1)}, bf16[48,512]{1,0:T(8,128)(2,1)S(1)}, u32[]{:S(2)}, u32[]{:S(2)}) collective-permute-start(bf16[48,512]{1,0:T(8,128)(2,1)S(1)} %project.1.p0), channel_id=1, source_target_pairs={{0,1},{1,0},{2,3},{3,2},{4,5},{5,4},{6,7},{7,6},{8,9},{9,8},{10,11... | collective-permute-start | bytes 147464 | tf_op jit(solution)/shard_map/ppermute | solution.py:393
  59.1 2.6 %collective-permute-start.3 = (bf16[48,512]{1,0:T(8,128)(2,1)S(1)}, bf16[48,512]{1,0:T(8,128)(2,1)S(1)}, u32[]{:S(2)}, u32[]{:S(2)}) collective-permute-start(bf16[48,512]{1,0:T(8,128)(2,1)S(1)} %project.1.p0), channel_id=1, source_target_pairs={{0,2},{1,3},{2,0},{3,1},{4,6},{5,7},{6,4},{7,5},{8,10},{9,11},{10,... | collective-permute-start | bytes 147464 | tf_op jit(solution)/shard_map/ppermute | solution.py:393
  61.7 2.0 %collective-permute-done.3.p2 = bf16[48,512]{1,0:T(8,128)(2,1)S(1)} collective-permute-done((bf16[48,512]{1,0:T(8,128)(2,1)S(1)}, bf16[48,512]{1,0:T(8,128)(2,1)S(1)}, u32[]{:S(2)}, u32[]{:S(2)}) %collective-permute-start.3) | collective-permute-done | bytes 49184 | tf_op jit(solution)/shard_map/ppermute | solution.py:393
  63.7 2.2 %collective-permute-done.4.p3 = bf16[48,512]{1,0:T(8,128)(2,1)S(1)} collective-permute-done((bf16[48,512]{1,0:T(8,128)(2,1)S(1)}, bf16[48,512]{1,0:T(8,128)(2,1)S(1)}, u32[]{:S(2)}, u32[]{:S(2)}) %collective-permute-start.4) | collective-permute-done | bytes 49184 | tf_op jit(solution)/shard_map/ppermute | solution.py:393
  65.9 5.2 %gate_up.1 = (bf16[16,208,128]{2,1,0:T(8,128)(2,1)S(1)}, f32[48,512]{1,0:T(8,128)S(1)}, bf16[128,8192]{1,0:T(8,128)(2,1)S(1)}, bf16[128,8192]{1,0:T(8,128)(2,1)S(1)}) custom-call(s32[2]{0:T(128)S(1)} %pad_add_fusion.where_ref, bf16[48,512]{1,0:T(8,128)(2,1)S(1)} %project.1.p0, bf16[48,512]{1,0:T(8,128)(2,1)S(1)} %collective-permute-done.2.p1, ...), custom_call_target="tpu_custom_call" | custom-call | tf_op jit(solution)/shard_map/gate_up/pallas_call | solution.py:481
  71.1 13.9 %all_to_all.25.got_ref = bf16[16,208,128]{2,1,0:T(8,128)(2,1)S(1)} all-to-all(bf16[16,208,128]{2,1,0:T(8,128)(2,1)S(1)} %get-tuple-element.13), channel_id=1, replica_groups={{0,8,16,24,32,40,48,56,64,72,80,88,96,104,112,120},{4,12,20,28,36,44,52..., dimensions={0} | all-to-all | bytes 1703936 | tf_op jit(solution)/shard_map/all_to_all | solution.py:385
  84.9 1.5 %down.1 = bf16[16,48,512]{2,1,0:T(8,128)(2,1)S(1)} custom-call(s32[2]{0:T(128)S(1)} %pad_add_fusion.where_ref, bf16[16,208,128]{2,1,0:T(8,128)(2,1)S(1)} %all_to_all.25.got_ref, bf16[128,8192]{1,0:T(8,128)(2,1)S(1)} %get-tuple-element.14.own_ref, bf16[128,8192]{1,0:T(8,128)(2,1)S(1)} %get-tuple-element.15.sib_ref), custom_call_target="tpu_custom_call" | custom-call | tf_op jit(solution)/shard_map/down/pallas_call | solution.py:497
  86.4 13.2 %all_to_all.26 = bf16[16,48,512]{2,1,0:T(8,128)(2,1)S(1)} all-to-all(bf16[16,48,512]{2,1,0:T(8,128)(2,1)S(1)} %down.1), channel_id=1, replica_groups={{0,8,16,24,32,40,48,56,64,72,80,88,96,104,112,120},{4,12,20,28,36,44,52..., dimensions={0} | all-to-all | bytes 1572864 | tf_op jit(solution)/shard_map/all_to_all | solution.py:385
  100.2 0.7 collective-permute-start.11
  100.9 1.6 %collective-permute-start.9 = (bf16[48,512]{1,0:T(8,128)(2,1)S(1)}, bf16[48,512]{1,0:T(8,128)(2,1)S(1)}, u32[]{:S(2)}, u32[]{:S(2)}) collective-permute-start(bf16[48,512]{1,0:T(8,128)(2,1)S(1)} %reduce-precision_convert_fusion), channel_id=1, source_target_pairs={{0,1},{1,0},{2,3},{3,2},{4,5},{5,4},{6,7},{7,6},{8,9},{9,8},{10,11... | collective-permute-start | bytes 147464 | tf_op jit(solution)/shard_map/ppermute | solution.py:393
  102.4 2.1 %collective-permute-done.10 = bf16[48,512]{1,0:T(8,128)(2,1)S(1)} collective-permute-done((bf16[48,512]{1,0:T(8,128)(2,1)S(1)}, bf16[48,512]{1,0:T(8,128)(2,1)S(1)}, u32[]{:S(2)}, u32[]{:S(2)}) %collective-permute-start.10) | collective-permute-done | bytes 49184 | tf_op jit(solution)/shard_map/ppermute | solution.py:393
  104.5 0.5 collective-permute-done.11
  105.1 8.3 %collective-permute-start.12 = (bf16[48,256]{1,0:T(8,128)(2,1)S(1)}, bf16[48,256]{1,0:T(8,128)(2,1)S(1)}, u32[]{:S(2)}, u32[]{:S(2)}) collective-permute-start(bf16[48,256]{1,0:T(8,128)(2,1)S(1)} %broadcast_select_fusion.2), channel_id=1, source_target_pairs={{0,4},{4,0},{8,12},{12,8},{16,20},{20,16},{24,28},{28,24},{32,36},... | collective-permute-start | bytes 73736 | tf_op jit(solution)/shard_map/ppermute | solution.py:390
  113.5 0.6 reshape.40
  114.4 0.6 reshape.46
  (48 shorter events, 2.7 us)
Async XLA Ops:
  1.5 0.8 copy-start.2
  2.2 0.7 copy-start.3
  2.9 7.4 %copy-start = (bf16[256,4096]{1,0:T(8,128)(2,1)S(1)}, bf16[256,4096]{1,0:T(8,128)(2,1)}, u32[]{:S(2)}) copy-start(bf16[256,4096]{1,0:T(8,128)(2,1)} %g_own_hbm.1) | copy-start | bytes 6291460
  2.9 8.0 %copy-start.1 = (bf16[2048,256]{1,0:T(8,128)(2,1)S(1)}, bf16[2048,256]{1,0:T(8,128)(2,1)}, u32[]{:S(2)}) copy-start(bf16[2048,256]{1,0:T(8,128)(2,1)} %own_ref.1) | copy-start | bytes 3145732
  2.9 16.1 %copy-start.4 = (bf16[3,32,256]{2,1,0:T(8,128)(2,1)S(1)}, bf16[3,32,256]{2,1,0:T(8,128)(2,1)}, u32[]{:S(2)}) copy-start(bf16[3,32,256]{2,1,0:T(8,128)(2,1)} %param.20) | copy-start | bytes 147460
  2.9 16.3 %copy-start.5 = (bf16[256]{0:T(256)(128)(2,1)S(1)}, bf16[256]{0:T(256)(128)(2,1)}, u32[]{:S(2)}) copy-start(bf16[256]{0:T(256)(128)(2,1)} %param.21) | copy-start | bytes 1540
  2.9 19.4 %copy-start.6 = (bf16[3,1,256]{2,0,1:T(4,128)(2,1)S(1)}, bf16[3,1,256]{2,0,1:T(4,128)(2,1)}, u32[]{:S(2)}) copy-start(bf16[3,1,256]{2,0,1:T(4,128)(2,1)} %param.18) | copy-start | bytes 4612
  2.9 19.4 %copy-start.7 = (bf16[3,1,256]{2,0,1:T(4,128)(2,1)S(1)}, bf16[3,1,256]{2,0,1:T(4,128)(2,1)}, u32[]{:S(2)}) copy-start(bf16[3,1,256]{2,0,1:T(4,128)(2,1)} %param.19) | copy-start | bytes 4612
  8.6 13.3 %collective-permute-start = (bf16[16,512,256]{2,1,0:T(8,128)(2,1)}, bf16[16,512,256]{2,1,0:T(8,128)(2,1)}, u32[]{:S(2)}, u32[]{:S(2)}) collective-permute-start(bf16[16,512,256]{2,1,0:T(8,128)(2,1)} %get-tuple-element.11), channel_id=1, source_target_pairs={{0,4},{4,0},{8,12},{12,8},{16,20},{20,16},{24,28},{28,24},{32,36},... | collective-permute-start | bytes 12582920 | tf_op jit(solution)/shard_map/ppermute | solution.py:390
  10.3 51.4 %collective-permute-start.6 = (bf16[256,4096]{1,0:T(8,128)(2,1)S(1)}, bf16[256,4096]{1,0:T(8,128)(2,1)}, u32[]{:S(2)}, u32[]{:S(2)}) collective-permute-start(bf16[256,4096]{1,0:T(8,128)(2,1)S(1)} %copy-done), channel_id=1, source_target_pairs={{0,4},{4,0},{8,12},{12,8},{16,20},{20,16},{24,28},{28,24},{32,36},... | collective-permute-start | bytes 6291464 | tf_op jit(solution)/shard_map/ppermute | solution.py:390
  10.4 51.3 %collective-permute-start.7 = (bf16[256,4096]{1,0:T(8,128)(2,1)}, bf16[256,4096]{1,0:T(8,128)(2,1)}, u32[]{:S(2)}, u32[]{:S(2)}) collective-permute-start(bf16[256,4096]{1,0:T(8,128)(2,1)} %u_own_hbm.1), channel_id=1, source_target_pairs={{0,4},{4,0},{8,12},{12,8},{16,20},{20,16},{24,28},{28,24},{32,36},... | collective-permute-start | bytes 6291464 | tf_op jit(solution)/shard_map/ppermute | solution.py:390
  10.8 50.9 %collective-permute-start.8 = (bf16[128,8192]{1,0:T(8,128)(2,1)}, bf16[128,8192]{1,0:T(8,128)(2,1)}, u32[]{:S(2)}, u32[]{:S(2)}) collective-permute-start(bf16[128,8192]{1,0:T(8,128)(2,1)} %d_own_hbm.1), channel_id=1, source_target_pairs={{0,4},{4,0},{8,12},{12,8},{16,20},{20,16},{24,28},{28,24},{32,36},... | collective-permute-start | bytes 6291464 | tf_op jit(solution)/shard_map/ppermute | solution.py:390
  10.9 37.8 %collective-permute-start.1 = (bf16[2048,256]{1,0:T(8,128)(2,1)S(1)}, bf16[2048,256]{1,0:T(8,128)(2,1)}, u32[]{:S(2)}, u32[]{:S(2)}) collective-permute-start(bf16[2048,256]{1,0:T(8,128)(2,1)S(1)} %copy-done.1), channel_id=1, source_target_pairs={{0,4},{4,0},{8,12},{12,8},{16,20},{20,16},{24,28},{28,24},{32,36},... | collective-permute-start | bytes 3145736 | tf_op jit(solution)/shard_map/ppermute | solution.py:390
  11.3 15.4 %all-to-all-start = ((bf16[16,48,128]{2,1,0:T(8,128)(2,1)}), bf16[16,48,128]{2,1,0:T(8,128)(2,1)S(1)}, u32[]{:S(2)}, u32[]{:S(2)}) async-start(bf16[16,48,128]{2,1,0:T(8,128)(2,1)} %get-tuple-element.10), calls=%async_computation | async-start | bytes 393216 | tf_op jit(solution)/shard_map/all_to_all | solution.py:385
  21.9 14.4 %collective-permute-start.5 = (bf16[64,256]{1,0:T(8,128)(2,1)}, bf16[64,256]{1,0:T(8,128)(2,1)S(1)}, u32[]{:S(2)}, u32[]{:S(2)}) collective-permute-start(bf16[64,256]{1,0:T(8,128)(2,1)} %pad_maximum_fusion.2), channel_id=1, source_target_pairs={{0,4},{4,0},{8,12},{12,8},{16,20},{20,16},{24,28},{28,24},{32,36},... | collective-permute-start | bytes 98312 | tf_op jit(solution)/shard_map/ppermute | solution.py:390
  32.8 11.1 %all-to-all-start.1 = ((bf16[16,64,128]{2,1,0:T(8,128)(2,1)}), bf16[16,64,128]{2,1,0:T(8,128)(2,1)S(1)}, u32[]{:S(2)}, u32[]{:S(2)}) async-start(bf16[16,64,128]{2,1,0:T(8,128)(2,1)} %attend.1), calls=%async_computation.1 | async-start | bytes 524288 | tf_op jit(solution)/shard_map/all_to_all | solution.py:385
  45.2 10.7 %all-to-all-start.2 = ((bf16[16,48,128]{2,1,0:T(8,128)(2,1)}), bf16[16,48,128]{2,1,0:T(8,128)(2,1)S(1)}, u32[]{:S(2)}, u32[]{:S(2)}) async-start(bf16[16,48,128]{2,1,0:T(8,128)(2,1)} %broadcast_in_dim.4), calls=%async_computation.2 | async-start | bytes 393216 | tf_op jit(solution)/shard_map/all_to_all | solution.py:385
  57.5 4.2 %collective-permute-start.2 = (bf16[48,512]{1,0:T(8,128)(2,1)S(1)}, bf16[48,512]{1,0:T(8,128)(2,1)S(1)}, u32[]{:S(2)}, u32[]{:S(2)}) collective-permute-start(bf16[48,512]{1,0:T(8,128)(2,1)S(1)} %project.1.p0), channel_id=1, source_target_pairs={{0,1},{1,0},{2,3},{3,2},{4,5},{5,4},{6,7},{7,6},{8,9},{9,8},{10,11... | collective-permute-start | bytes 147464 | tf_op jit(solution)/shard_map/ppermute | solution.py:393
  59.1 4.6 %collective-permute-start.3 = (bf16[48,512]{1,0:T(8,128)(2,1)S(1)}, bf16[48,512]{1,0:T(8,128)(2,1)S(1)}, u32[]{:S(2)}, u32[]{:S(2)}) collective-permute-start(bf16[48,512]{1,0:T(8,128)(2,1)S(1)} %project.1.p0), channel_id=1, source_target_pairs={{0,2},{1,3},{2,0},{3,1},{4,6},{5,7},{6,4},{7,5},{8,10},{9,11},{10,... | collective-permute-start | bytes 147464 | tf_op jit(solution)/shard_map/ppermute | solution.py:393
  61.7 4.2 %collective-permute-start.4 = (bf16[48,512]{1,0:T(8,128)(2,1)S(1)}, bf16[48,512]{1,0:T(8,128)(2,1)S(1)}, u32[]{:S(2)}, u32[]{:S(2)}) collective-permute-start(bf16[48,512]{1,0:T(8,128)(2,1)S(1)} %project.1.p0), channel_id=1, source_target_pairs={{0,3},{1,2},{2,1},{3,0},{4,7},{5,6},{6,5},{7,4},{8,11},{9,10},{10,... | collective-permute-start | bytes 147464 | tf_op jit(solution)/shard_map/ppermute | solution.py:393
  99.7 4.8 %collective-permute-start.10 = (bf16[48,512]{1,0:T(8,128)(2,1)S(1)}, bf16[48,512]{1,0:T(8,128)(2,1)S(1)}, u32[]{:S(2)}, u32[]{:S(2)}) collective-permute-start(bf16[48,512]{1,0:T(8,128)(2,1)S(1)} %reduce-precision_convert_fusion), channel_id=1, source_target_pairs={{0,2},{1,3},{2,0},{3,1},{4,6},{5,7},{6,4},{7,5},{8,10},{9,11},{10,... | collective-permute-start | bytes 147464 | tf_op jit(solution)/shard_map/ppermute | solution.py:393
  100.2 4.9 %collective-permute-start.11 = (bf16[48,512]{1,0:T(8,128)(2,1)S(1)}, bf16[48,512]{1,0:T(8,128)(2,1)S(1)}, u32[]{:S(2)}, u32[]{:S(2)}) collective-permute-start(bf16[48,512]{1,0:T(8,128)(2,1)S(1)} %reduce-precision_convert_fusion), channel_id=1, source_target_pairs={{0,3},{1,2},{2,1},{3,0},{4,7},{5,6},{6,5},{7,4},{8,11},{9,10},{10,... | collective-permute-start | bytes 147464 | tf_op jit(solution)/shard_map/ppermute | solution.py:393
  100.9 4.2 %collective-permute-start.9 = (bf16[48,512]{1,0:T(8,128)(2,1)S(1)}, bf16[48,512]{1,0:T(8,128)(2,1)S(1)}, u32[]{:S(2)}, u32[]{:S(2)}) collective-permute-start(bf16[48,512]{1,0:T(8,128)(2,1)S(1)} %reduce-precision_convert_fusion), channel_id=1, source_target_pairs={{0,1},{1,0},{2,3},{3,2},{4,5},{5,4},{6,7},{7,6},{8,9},{9,8},{10,11... | collective-permute-start | bytes 147464 | tf_op jit(solution)/shard_map/ppermute | solution.py:393
  105.1 9.2 %collective-permute-start.12 = (bf16[48,256]{1,0:T(8,128)(2,1)S(1)}, bf16[48,256]{1,0:T(8,128)(2,1)S(1)}, u32[]{:S(2)}, u32[]{:S(2)}) collective-permute-start(bf16[48,256]{1,0:T(8,128)(2,1)S(1)} %broadcast_select_fusion.2), channel_id=1, source_target_pairs={{0,4},{4,0},{8,12},{12,8},{16,20},{20,16},{24,28},{28,24},{32,36},... | collective-permute-start | bytes 73736 | tf_op jit(solution)/shard_map/ppermute | solution.py:390
